TPU v7x, 32 devices: a whole 2x2x4 slice. The times are simulated.
32 devices in a mesh: seq: 8 (over z, x), head: 4 (over y, core).
Axes of the slice: x: 2, y: 2, z: 4, core: 2. Of those that a mesh axis runs over, the one named last changes fastest.
Arguments:
- queries: float32 [2048, 4096], P('seq', 'head'), may hold values from -0.54 to 0.54
- key_input: float32 [2048, 4096], P('seq', 'head'), may hold values from -0.54 to 0.54
- value_input: float32 [2048, 4096], P('seq', 'head'), may hold values from -6 to 6
- grad_output: float32 [2048, 4096], P('seq', 'head'), may hold values from -0.54 to 0.54
- log_decay: float32 [2048, 32], P('seq', 'head'), may hold values from -2 to 0
- level_weight: float32 [2048, 7], P('seq'), may hold values from 0.3 to 1.5
- segment: int32 [2048], P('seq'), may hold values from 0 to 3, never falling along the last dimension, each value on 1 to 1024 neighbouring positions
Outputs:
- grad_query: float32 [2048, 4096], P('seq', 'head')
- grad_key: float32 [2048, 4096], P('seq', 'head')
- grad_value: float32 [2048, 4096], P('seq', 'head')
- grad_level: float32 [2048, 7], P('seq')
Inputs may be any that keep to these rules, and one draw needn't show every extreme that they name: `segment`: document numbers never fall along the tokens; each document has at most 1024 tokens, one exactly that many.
All inputs are finite; a program needn't handle non-finite values.
Results may differ from a plain program's by a relative error of at most 0.00012.
Values sent between devices are 32-bit elements; how exact they have to be, the bound alone decides.
No kernel may reach another device: no remote copies, remote signals or barrier semaphores. Data moves between devices by JAX's collectives and lax.ppermute only.
A program may use at most 128 MiB of HBM per device.

v0:
```python
import jax
import jax.numpy as jnp
from jax import lax
from jax.sharding import PartitionSpec as P

PRECISE = lax.Precision.HIGHEST


def from_partner(block, axis, distance):
    count = lax.axis_size(axis)
    route = []
    for low in range(count):
        high = low | 1 << distance
        if high != low and high < count:
            route += [(low, high), (high, low)]
    return lax.ppermute(block, axis, route)


def span_sum(totals, stretch_index, low_bound, high_bound):
    inside = (stretch_index > low_bound) & (stretch_index <= high_bound)
    return jnp.sum(jnp.where(inside[:, None], totals, 0.0), axis=0)


def on_device(queries, key_input, value_input, grad_output, log_decay, level_weight, segment):
    stretches = lax.axis_size("seq")
    tree_depth = stretches.bit_length() - 1
    device = lax.axis_index("seq")
    stretch_len, head_count = log_decay.shape
    head_width = queries.shape[1] // head_count
    levels = level_weight.shape[1]
    query_heads = queries.reshape(stretch_len, head_count, head_width)
    key_heads = key_input.reshape(stretch_len, head_count, head_width)
    value_heads = value_input.reshape(stretch_len, head_count, head_width)
    grad_heads = grad_output.reshape(stretch_len, head_count, head_width)
    cumulative = jnp.cumsum(log_decay, axis=0)
    totals = cumulative[-1]
    segment_float = segment.astype(jnp.float32)
    own_end = segment_float[-1]
    all_totals, all_ends = (
        lax.all_gather(totals[None, :], "seq", axis=0, tiled=True),
        lax.all_gather(own_end.reshape(1, 1), "seq", axis=0, tiled=True),
    )
    stretch_ends = all_ends[:, 0]
    stretch_index = jnp.arange(stretches, dtype=jnp.int32)
    source_weight = jnp.exp(totals[None, :] - cumulative) * (segment_float == own_end)[
        :, None
    ].astype(jnp.float32)
    own_state = jnp.einsum(
        "thi,thj->hij", source_weight[:, :, None] * key_heads, value_heads, precision=PRECISE
    )
    upper_flags = []
    query_factors = []
    level_scales = []
    block_factors = []
    source_factors = []
    level_grads = []
    for distance in range(tree_depth):
        half_size = 1 << distance
        upper_half = (device >> distance & 1).astype(jnp.float32)
        lower_end = (device >> distance + 1 << distance + 1) + half_size - 1
        upper_end = lower_end + half_size
        end_lower = stretch_ends[lower_end]
        query_span = span_sum(all_totals, stretch_index, lower_end, device - 1)
        factor = (
            jnp.exp(cumulative + query_span[None, :])
            * (segment_float == end_lower)[:, None].astype(jnp.float32)
            * upper_half
        )
        level_scale = level_weight[:, distance + 1][:, None] * factor
        block_factor = jnp.exp(span_sum(all_totals, stretch_index, lower_end, upper_end)) * (
            stretch_ends[upper_end] == end_lower
        ).astype(jnp.float32)
        own_last = device | half_size - 1
        source_factor = (
            jnp.exp(span_sum(all_totals, stretch_index, device, own_last))
            * (stretch_ends[own_last] == own_end).astype(jnp.float32)
            * (1.0 - upper_half)
        )
        upper_flags.append(upper_half)
        query_factors.append(factor)
        level_scales.append(level_scale)
        block_factors.append(block_factor[:, None, None])
        source_factors.append(source_factor[:, None, None])
        level_grads.append(
            jnp.einsum(
                "thi,thj->hij", level_scale[:, :, None] * query_heads, grad_heads, precision=PRECISE
            )
        )
    blocks = []
    running_state = own_state
    for distance in range(tree_depth):
        their_state = from_partner(running_state, "seq", distance)
        upper_half = upper_flags[distance]
        block_factor = block_factors[distance]
        blocks.append(upper_half * their_state)
        running_state = upper_half * (block_factor * their_state + running_state) + (
            1.0 - upper_half
        ) * (block_factor * running_state + their_state)
    pending = jnp.stack(level_grads)
    grad_source = jnp.zeros_like(own_state)
    for distance in range(tree_depth):
        their_levels = from_partner(pending, "seq", distance)
        grad_source = grad_source + source_factors[distance] * their_levels[0]
        pending = pending[1:] + their_levels[1:]
    position = jnp.arange(stretch_len, dtype=jnp.int32)
    visible = (position[:, None] >= position[None, :]) & (segment[:, None] == segment[None, :])
    decay_gap = cumulative.T[:, :, None] - cumulative.T[:, None, :]
    within = jnp.where(visible[None], jnp.exp(jnp.minimum(decay_gap, 0.0)), 0.0)
    scores = jnp.einsum("thd,shd->hts", query_heads, key_heads, precision=PRECISE)
    grad_scores = jnp.einsum("thd,shd->hts", grad_heads, value_heads, precision=PRECISE)
    weight = within * level_weight[:, 0][None, :, None]
    grad_value = jnp.einsum("hts,thd->shd", weight * scores, grad_heads, precision=PRECISE)
    grad_query = jnp.einsum("hts,shd->thd", weight * grad_scores, key_heads, precision=PRECISE)
    grad_key = jnp.einsum("hts,thd->shd", weight * grad_scores, query_heads, precision=PRECISE)
    level_zero = jnp.sum(within * scores * grad_scores, axis=(0, 2))
    state_stack = jnp.stack(blocks)
    scale_stack = jnp.stack(level_scales)
    factor_stack = jnp.stack(query_factors)
    reached = jnp.einsum("thi,lhij->lthj", query_heads, state_stack, precision=PRECISE)
    level_terms = jnp.sum(jnp.sum(reached * grad_heads[None], axis=3) * factor_stack, axis=2)
    returned = jnp.einsum("thj,lhij->lthi", grad_heads, state_stack, precision=PRECISE)
    grad_query = grad_query + jnp.sum(returned * scale_stack[:, :, :, None], axis=0)
    grad_key = grad_key + source_weight[:, :, None] * jnp.einsum(
        "thj,hij->thi", value_heads, grad_source, precision=PRECISE
    )
    grad_value = grad_value + source_weight[:, :, None] * jnp.einsum(
        "thi,hij->thj", key_heads, grad_source, precision=PRECISE
    )
    level_parts = [level_zero[:, None], level_terms.T]
    if levels - 1 - tree_depth > 0:
        level_parts.append(jnp.zeros((stretch_len, levels - 1 - tree_depth), jnp.float32))
    partial_levels = jnp.concatenate(level_parts, axis=1)
    grad_level = lax.psum(partial_levels, "head")
    width_all = head_count * head_width
    return (
        grad_query.reshape(stretch_len, width_all),
        grad_key.reshape(stretch_len, width_all),
        grad_value.reshape(stretch_len, width_all),
        grad_level,
    )


def solution(mesh):
    in_specs = (
        P("seq", "head"),
        P("seq", "head"),
        P("seq", "head"),
        P("seq", "head"),
        P("seq", "head"),
        P("seq", None),
        P("seq"),
    )
    out_specs = (P("seq", "head"), P("seq", "head"), P("seq", "head"), P("seq", None))
    return jax.shard_map(
        on_device, mesh=mesh, in_specs=in_specs, out_specs=out_specs, check_vma=False
    )
```

profile of v0, /device:TPU:2, one launch (start us, length us, event | category | flops | bytes accessed | tf_op | source)
XLA Modules:
  0.0 163.0 jit_solution(7349376848744152504)
XLA Ops:
  0.8 0.7 convert_element_type.44
  1.5 1.2 dynamic-slice.16
  2.7 1.3 fusion.66
  4.0 18.0 %all-reduce = f32[8]{0:T(128)S(1)} all-reduce(f32[8]{0:T(128)S(1)} %get-tuple-element.54), channel_id=2, replica_groups=mesh['seq'=8,'head'=4] {'seq'}, use_global_device_ids=true, to_apply=%add | all-reduce | flops 8 | bytes 64
  22.0 0.8 fusion.65
  22.8 1.2 reduce-window.6
  24.1 0.2 slice_reduce_fusion
  24.3 0.2 slice_reduce_fusion.1
  24.5 20.3 %all-gather.1 = f32[8,1,8]{2,1,0:T(1,128)S(1)} all-gather(f32[1,1,8]{2,1,0:T(1,128)S(1)} %bitcast.158), channel_id=1, replica_groups=mesh['seq'=8,'head'=4] {'seq'}, dimensions={0}, use_global_device_ids=true | all-gather | bytes 288 | tf_op jit(solution)/shard_map/all_gather | solution.py:40
  44.9 1.6 %copy.106 = f32[256,1024]{0,1:T(8,128)S(1)} copy(f32[256,1024]{1,0:T(8,128)} %param.8) | data formatting | bytes 2097152 | tf_op args[1]
  46.5 0.7 fusion.67
  47.2 2.5 %compare_convert_fusion.3 = (f32[256]{0:T(256)S(1)}, f32[256]{0:T(256)S(1)}, f32[256]{0:T(256)S(1)}, f32[256]{0:T(256)S(1)}) fusion(f32[]{:T(128)} %bitcast.7, s32[256]{0:T(256)S(1)} %copy-done.15, f32[]{:T(128)} %bitcast.12, f32[]{:T(128)} %bitcast.15, f32[]{:T(128)} %bitcast.25), kind=kLoop, calls=%fused_computation.110 | loop fusion | flops 2304 | bytes 5136 | tf_op jit(solution)/shard_map/convert_element_type | solution.py:47
  49.7 0.1 select_reduce_fusion.2
  49.9 2.0 %fusion.20 = f32[8,128,128]{2,1,0:T(8,128)} fusion(f32[256,8,128]{0,2,1:T(8,128)S(1)} %bitcast.136, f32[256,8]{0,1:T(8,128)S(1)} %get-tuple-element.44, f32[256,1024]{1,0:T(8,128)S(1)} %copy-done), kind=kOutput, calls=%fused_computation.28 | convolution fusion | flops 402915328 | bytes 2629632 | tf_op jit(solution)/shard_map/thi,thj->hij/dot_general | solution.py:48
  51.9 1.2 copy.151
  53.1 1.6 copy.113
  54.7 2.4 %copy.150 = f32[32,8,8,128]{3,2,1,0:T(8,128)} copy(f32[32,8,8,128]{3,1,2,0:T(8,128)} %bitcast.148) | data formatting | bytes 2097152
  57.1 2.6 %copy.124 = f32[256,8,128]{0,2,1:T(8,128)} copy(f32[256,8,128]{2,1,0:T(8,128)} %bitcast.143) | data formatting | bytes 2097152 | tf_op jit(solution)/shard_map/reshape | solution.py:34
  59.6 2.5 %convolution_bitcast_fusion.4 = f32[1,8,128,128]{3,2,1,0:T(8,128)S(1)} fusion(f32[256,8,128]{0,2,1:T(8,128)} %copy.124, f32[256,8,128]{0,2,1:T(8,128)S(1)} %copy.113, f32[256,8]{0,1:T(8,128)S(1)} %get-tuple-element.42), kind=kOutput, calls=%fused_computation.24 | convolution fusion | flops 402915328 | bytes 2629632 | tf_op jit(solution)/shard_map/thi,thj->hij/dot_general | solution.py:85
  62.1 1.1 convolution_bitcast_fusion.5
  63.3 1.1 convolution_bitcast_fusion.6
  64.4 1.3 pad_maximum_fusion.1
  65.7 2.0 %collective-permute-start.3 = (f32[3,8,128,128]{3,2,1,0:T(8,128)}, f32[3,8,128,128]{3,2,1,0:T(8,128)}, u32[]{:S(2)}, u32[]{:S(2)}) collective-permute-start(f32[3,8,128,128]{3,2,1,0:T(8,128)} %pad_maximum_fusion.1), channel_id=1, source_target_pairs={{0,4},{4,0},{8,12},{12,8},{16,20},{20,16},{24,28},{28,24},{1,5},{5... | collective-permute-start | bytes 4718600 | tf_op jit(solution)/shard_map/ppermute | solution.py:16
  67.8 0.1 fusion.56
  67.9 3.2 %fusion.68 = f32[8,256,256]{1,2,0:T(8,128)} fusion(f32[256,8,128]{0,2,1:T(8,128)S(1)} %copy.113, f32[256,8,128]{0,2,1:T(8,128)S(1)} %bitcast.137), kind=kOutput, calls=%fused_computation.127 | convolution fusion | flops 805306368 | bytes 4194304 | tf_op jit(solution)/shard_map/thd,shd->hts/dot_general | solution.py:109
  76.2 5.9 %fusion.9 = f32[256,8,128]{0,2,1:T(8,128)} fusion(f32[256,8,128]{0,2,1:T(8,128)} %copy.124, f32[8,256,256]{1,2,0:T(8,128)} %fusion.68, f32[256]{0:T(256)S(1)} %bitcast.154, f32[8,256]{1,0:T(8,128)S(1)} %get-tuple-element.38, pred[256,256]{0,1:T(8,128)(4,1)S(1)} %fusion.56), kind=kOutput, calls=%fused_computation.14 | convolution fusion | flops 807927808 | bytes 4269056 | tf_op jit(solution)/shard_map/hts,thd->shd/dot_general | solution.py:112
  82.1 2.3 %multiply_bitcast_fusion.2 = (f32[1,8,128,128]{3,2,1,0:T(8,128)}, f32[8,128,128]{2,1,0:T(8,128)S(1)}) fusion(f32[8,128,128]{2,1,0:T(8,128)} %collective-permute-done, f32[]{:T(128)S(6)} %convert_element_type.43, f32[8,128,128]{2,1,0:T(8,128)} %fusion.20, f32[]{:T(128)S(6)} %sub.52, f32[8]{0:T(128)S(1)} %exponential_multiply_fusion.2), kind=kLoop, calls=%fused_computation.72 | loop fusion | flops 1048576 | bytes 2097192 | tf_op jit(solution)/shard_map/stack | solution.py:116
  84.4 3.9 %multiply_reduce_fusion = (f32[256]{0:T(256)S(1)}, f32[8,256,256]{1,2,0:T(8,128)}) fusion(f32[8,256,256]{1,2,0:T(8,128)S(1)} %copy-done.5, f32[8,256]{1,0:T(8,128)S(1)} %get-tuple-element.38, pred[256,256]{0,1:T(8,128)(4,1)S(1)} %fusion.56, f32[256,8,128]{0,2,1:T(8,128)S(1)} %copy-done.2, f32[256,1024]{1,0:T(8,128)S(1)} %copy-done), kind=kOutput, calls=%fused_computation.4 | convolution fusion | flops 808451840 | bytes 6366208 | tf_op jit(solution)/shard_map/thd,shd->hts/dot_general | solution.py:110
  88.4 13.2 %collective-permute-done.1 = f32[8,128,128]{2,1,0:T(8,128)S(1)} collective-permute-done((f32[8,128,128]{2,1,0:T(8,128)S(1)}, f32[8,128,128]{2,1,0:T(8,128)S(1)}, u32[]{:S(2)}, u32[]{:S(2)}) %collective-permute-start.1) | collective-permute-done | bytes 524320 | tf_op jit(solution)/shard_map/ppermute | solution.py:16
  101.6 1.2 multiply_bitcast_fusion.1
  104.2 2.8 %slice_add_fusion = f32[2,8,128,128]{3,2,1,0:T(8,128)} fusion(f32[3,8,128,128]{3,2,1,0:T(8,128)} %collective-permute-done.3, f32[1,8,128,128]{3,2,1,0:T(8,128)} %copy-done.6, f32[1,8,128,128]{3,2,1,0:T(8,128)} %copy-done.7), kind=kLoop, calls=%fused_computation.32 | loop fusion | flops 524288 | bytes 3145728 | tf_op jit(solution)/shard_map/add | solution.py:104
  107.0 0.5 collective-permute-start.4
  107.5 10.9 %collective-permute-done.2 = f32[8,128,128]{2,1,0:T(8,128)} collective-permute-done((f32[8,128,128]{2,1,0:T(8,128)}, f32[8,128,128]{2,1,0:T(8,128)}, u32[]{:S(2)}, u32[]{:S(2)}) %collective-permute-start.2) | collective-permute-done | bytes 524320 | tf_op jit(solution)/shard_map/ppermute | solution.py:16
  118.4 1.1 multiply_bitcast_fusion
  119.6 2.8 %fusion.1 = f32[256,8,128]{0,2,1:T(8,128)S(1)} fusion(f32[3,256,8]{1,0,2:T(4,128)S(1)} %copy.111, f32[256,8,128,1]{2,1,0,3:T(8,128)S(1)} %bitcast.144, f32[1,8,128,128]{3,2,1,0:T(8,128)S(1)} %multiply_bitcast_fusion, f32[1,8,128,128]{3,2,1,0:T(8,128)S(1)} %copy-done.14, f32[1,8,128,128]{3,2,1,0:T(8,128)S(1)} %copy-done.13), kind=kOutput, calls=%fused_computation.3 | convolution fusion | flops 1210056704 | bytes 3694592 | tf_op jit(solution)/shard_map/thj,lhij->lthi/dot_general | solution.py:121
  122.4 3.0 %fusion.13 = f32[256,8,128]{0,2,1:T(8,128)} fusion(f32[256,8,128]{0,2,1:T(8,128)S(1)} %fusion.1, f32[256,8,128]{0,2,1:T(8,128)S(1)} %bitcast.138, f32[8,256,256]{1,2,0:T(8,128)S(1)} %copy-done.3, f32[256]{0:T(256)S(1)} %bitcast.155, f32[8,256]{1,0:T(8,128)S(1)} %get-tuple-element.38, pred[256,256]{0,1:T(8,128)(4,1)S(1)} %fusion.56), kind=kOutput, calls=%fused_computation.18 | convolution fusion | flops 808189952 | bytes 5317632 | tf_op jit(solution)/shard_map/hts,shd->thd/dot_general | solution.py:113
  125.4 2.5 %copy.132 = f32[256,1024]{1,0:T(8,128)} copy(f32[256,1024]{0,1:T(8,128)} %bitcast.146) | data formatting | bytes 2097152
  127.9 5.1 %collective-permute-done.4 = f32[2,8,128,128]{3,2,1,0:T(8,128)} collective-permute-done((f32[2,8,128,128]{3,2,1,0:T(8,128)}, f32[2,8,128,128]{3,2,1,0:T(8,128)}, u32[]{:S(2)}, u32[]{:S(2)}) %collective-permute-start.4) | collective-permute-done | bytes 1048608 | tf_op jit(solution)/shard_map/ppermute | solution.py:16
  133.0 2.0 %slice_add_fusion.1 = f32[1,8,128,128]{3,2,1,0:T(8,128)} fusion(f32[2,8,128,128]{3,2,1,0:T(8,128)} %collective-permute-done.4, f32[2,8,128,128]{3,2,1,0:T(8,128)} %slice_add_fusion), kind=kLoop, calls=%fused_computation.57 | loop fusion | flops 131072 | bytes 1572864 | tf_op jit(solution)/shard_map/add | solution.py:104
  135.1 4.8 %fusion = f32[3,256,8]{1,0,2:T(4,128)S(1)} fusion(f32[256,8,128]{0,2,1:T(8,128)} %copy.124, f32[256,8,128,1]{2,1,0,3:T(8,128)} %bitcast.142, f32[1,8,128,128]{3,2,1,0:T(8,128)} %copy-done.12, f32[1,8,128,128]{3,2,1,0:T(8,128)} %get-tuple-element.32, f32[1,8,128,128]{3,2,1,0:T(8,128)} %get-tuple-element.30), kind=kOutput, calls=%fused_computation.1 | convolution fusion | flops 1210312704 | bytes 3694592 | tf_op jit(solution)/shard_map/thi,lhij->lthj/dot_general | solution.py:119
  140.0 6.9 %psum.7 = f32[256,7]{0,1:T(8,128)} all-reduce(f32[256,7]{0,1:T(8,128)S(1)} %maximum_maximum_fusion), channel_id=1, replica_groups=mesh['seq'=8,'head'=4] {'head'}, use_global_device_ids=true, to_apply=%region_14.15 | all-reduce | flops 1792 | bytes 14336 | tf_op jit(solution)/shard_map/psum | solution.py:133
  147.0 3.6 %collective-permute-done.5 = f32[1,8,128,128]{3,2,1,0:T(8,128)} collective-permute-done((f32[1,8,128,128]{3,2,1,0:T(8,128)}, f32[1,8,128,128]{3,2,1,0:T(8,128)}, u32[]{:S(2)}, u32[]{:S(2)}) %collective-permute-start.5) | collective-permute-done | bytes 524320 | tf_op jit(solution)/shard_map/ppermute | solution.py:16
  150.5 1.5 fusion.50
  152.1 1.0 fusion.16
  153.1 2.0 %fusion.15 = f32[256,8,128]{0,2,1:T(8,128)} fusion(f32[256,8,128]{0,2,1:T(8,128)S(1)} %copy-done.10, f32[8,128,128]{2,1,0:T(8,128)S(1)} %fusion.50, f32[256,8,128]{0,2,1:T(8,128)S(1)} %bitcast.139, f32[256,8]{0,1:T(8,128)S(1)} %get-tuple-element.44), kind=kOutput, calls=%fused_computation.21 | convolution fusion | flops 403177472 | bytes 3678208 | tf_op jit(solution)/shard_map/thi,hij->thj/dot_general | solution.py:126
  155.2 3.9 %fusion.12 = f32[256,8,128]{0,2,1:T(8,128)} fusion(f32[256,8,128]{0,2,1:T(8,128)S(1)} %fusion.16, f32[256,8,128]{0,2,1:T(8,128)S(1)} %copy.113, f32[8,256,256]{1,2,0:T(8,128)S(1)} %copy-done.4, f32[256]{0:T(256)S(1)} %bitcast.156, f32[8,256]{1,0:T(8,128)S(1)} %get-tuple-element.38, pred[256,256]{0,1:T(8,128)(4,1)S(1)} %fusion.56), kind=kOutput, calls=%fused_computation.16 | convolution fusion | flops 808189952 | bytes 5317632 | tf_op jit(solution)/shard_map/hts,thd->shd/dot_general | solution.py:114
  159.1 2.6 %copy.133 = f32[256,1024]{1,0:T(8,128)} copy(f32[256,1024]{0,1:T(8,128)} %bitcast.145) | data formatting | bytes 2097152
  161.7 1.3 copy.134
  (61 shorter events, 0.6 us)
Async XLA Ops:
  0.6 49.3 %copy-start = (f32[256,1024]{1,0:T(8,128)S(1)}, f32[256,1024]{1,0:T(8,128)}, u32[]{:S(2)}) copy-start(f32[256,1024]{1,0:T(8,128)} %param.9) | copy-start | bytes 3145732
  0.6 46.6 %copy-start.15 = (s32[256]{0:T(256)S(1)}, s32[256]{0:T(256)}, u32[]{:S(2)}) copy-start(s32[256]{0:T(256)} %param.13) | copy-start | bytes 3076
  44.9 7.1 %copy-start.11 = (f32[256,1024]{1,0:T(8,128)S(1)}, f32[256,1024]{1,0:T(8,128)}, u32[]{:S(2)}) copy-start(f32[256,1024]{1,0:T(8,128)} %param.7) | copy-start | bytes 3145732
  51.9 30.2 %collective-permute-start = (f32[8,128,128]{2,1,0:T(8,128)}, f32[8,128,128]{2,1,0:T(8,128)}, u32[]{:S(2)}, u32[]{:S(2)}) collective-permute-start(f32[8,128,128]{2,1,0:T(8,128)} %fusion.20), channel_id=1, source_target_pairs={{0,4},{4,0},{8,12},{12,8},{16,20},{20,16},{24,28},{28,24},{1,5},{5... | collective-permute-start | bytes 1572872 | tf_op jit(solution)/shard_map/ppermute | solution.py:16
  59.6 2.5 %copy-start.1 = (f32[256,8,128]{0,2,1:T(8,128)S(1)}, f32[256,8,128]{0,2,1:T(8,128)}, u32[]{:S(2)}) copy-start(f32[256,8,128]{0,2,1:T(8,128)} %copy.124) | copy-start | bytes 3145732
  62.1 2.3 %copy-start.6 = (f32[1,8,128,128]{3,2,1,0:T(8,128)}, f32[1,8,128,128]{3,2,1,0:T(8,128)S(1)}, u32[]{:S(2)}) copy-start(f32[1,8,128,128]{3,2,1,0:T(8,128)S(1)} %convolution_bitcast_fusion.4) | copy-start | bytes 1572868
  63.3 2.5 %copy-start.7 = (f32[1,8,128,128]{3,2,1,0:T(8,128)}, f32[1,8,128,128]{3,2,1,0:T(8,128)S(1)}, u32[]{:S(2)}) copy-start(f32[1,8,128,128]{3,2,1,0:T(8,128)S(1)} %convolution_bitcast_fusion.5) | copy-start | bytes 1572868
  65.7 38.5 %collective-permute-start.3 = (f32[3,8,128,128]{3,2,1,0:T(8,128)}, f32[3,8,128,128]{3,2,1,0:T(8,128)}, u32[]{:S(2)}, u32[]{:S(2)}) collective-permute-start(f32[3,8,128,128]{3,2,1,0:T(8,128)} %pad_maximum_fusion.1), channel_id=1, source_target_pairs={{0,4},{4,0},{8,12},{12,8},{16,20},{20,16},{24,28},{28,24},{1,5},{5... | collective-permute-start | bytes 4718600 | tf_op jit(solution)/shard_map/ppermute | solution.py:16
  76.2 8.2 %copy-start.5 = (f32[8,256,256]{1,2,0:T(8,128)S(1)}, f32[8,256,256]{1,2,0:T(8,128)}, u32[]{:S(2)}) copy-start(f32[8,256,256]{1,2,0:T(8,128)} %fusion.68) | copy-start | bytes 6291460
  82.1 2.3 %copy-start.2 = (f32[256,8,128]{0,2,1:T(8,128)S(1)}, f32[256,8,128]{0,2,1:T(8,128)}, u32[]{:S(2)}) copy-start(f32[256,8,128]{0,2,1:T(8,128)} %copy.124) | copy-start | bytes 3145732
  84.4 17.2 %collective-permute-start.1 = (f32[8,128,128]{2,1,0:T(8,128)S(1)}, f32[8,128,128]{2,1,0:T(8,128)S(1)}, u32[]{:S(2)}, u32[]{:S(2)}) collective-permute-start(f32[8,128,128]{2,1,0:T(8,128)S(1)} %get-tuple-element.31), channel_id=1, source_target_pairs={{0,8},{8,0},{4,12},{12,4},{16,24},{24,16},{20,28},{28,20},{1,9},{9... | collective-permute-start | bytes 1572872 | tf_op jit(solution)/shard_map/ppermute | solution.py:16
  102.8 15.6 %collective-permute-start.2 = (f32[8,128,128]{2,1,0:T(8,128)}, f32[8,128,128]{2,1,0:T(8,128)}, u32[]{:S(2)}, u32[]{:S(2)}) collective-permute-start(f32[8,128,128]{2,1,0:T(8,128)} %get-tuple-element.33), channel_id=1, source_target_pairs={{0,16},{16,0},{4,20},{20,4},{8,24},{24,8},{12,28},{28,12},{1,17},{... | collective-permute-start | bytes 1572872 | tf_op jit(solution)/shard_map/ppermute | solution.py:16
  104.2 15.3 %copy-start.9 = (f32[32,8,8,128]{3,2,1,0:T(8,128)S(1)}, f32[32,8,8,128]{3,2,1,0:T(8,128)}, u32[]{:S(2)}) copy-start(f32[32,8,8,128]{3,2,1,0:T(8,128)} %copy.150) | copy-start | bytes 3145732
  104.2 15.3 %copy-start.13 = (f32[1,8,128,128]{3,2,1,0:T(8,128)S(1)}, f32[1,8,128,128]{3,2,1,0:T(8,128)}, u32[]{:S(2)}) copy-start(f32[1,8,128,128]{3,2,1,0:T(8,128)} %get-tuple-element.30) | copy-start | bytes 1572868
  104.2 15.3 %copy-start.14 = (f32[1,8,128,128]{3,2,1,0:T(8,128)S(1)}, f32[1,8,128,128]{3,2,1,0:T(8,128)}, u32[]{:S(2)}) copy-start(f32[1,8,128,128]{3,2,1,0:T(8,128)} %get-tuple-element.32) | copy-start | bytes 1572868
  107.0 26.0 %collective-permute-start.4 = (f32[2,8,128,128]{3,2,1,0:T(8,128)}, f32[2,8,128,128]{3,2,1,0:T(8,128)}, u32[]{:S(2)}, u32[]{:S(2)}) collective-permute-start(f32[2,8,128,128]{3,2,1,0:T(8,128)} %slice_add_fusion), channel_id=1, source_target_pairs={{0,8},{8,0},{4,12},{12,4},{16,24},{24,16},{20,28},{28,20},{1,9},{9... | collective-permute-start | bytes 3145736 | tf_op jit(solution)/shard_map/ppermute | solution.py:16
  119.5 2.9 %copy-start.12 = (f32[1,8,128,128]{3,2,1,0:T(8,128)}, f32[1,8,128,128]{3,2,1,0:T(8,128)S(1)}, u32[]{:S(2)}) copy-start(f32[1,8,128,128]{3,2,1,0:T(8,128)S(1)} %multiply_bitcast_fusion) | copy-start | bytes 1572868
  119.5 2.8 %copy-start.3 = (f32[8,256,256]{1,2,0:T(8,128)S(1)}, f32[8,256,256]{1,2,0:T(8,128)}, u32[]{:S(2)}) copy-start(f32[8,256,256]{1,2,0:T(8,128)} %get-tuple-element.64) | copy-start | bytes 6291460
  135.1 15.5 %collective-permute-start.5 = (f32[1,8,128,128]{3,2,1,0:T(8,128)}, f32[1,8,128,128]{3,2,1,0:T(8,128)}, u32[]{:S(2)}, u32[]{:S(2)}) collective-permute-start(f32[1,8,128,128]{3,2,1,0:T(8,128)} %slice_add_fusion.1), channel_id=1, source_target_pairs={{0,16},{16,0},{4,20},{20,4},{8,24},{24,8},{12,28},{28,12},{1,17},{... | collective-permute-start | bytes 1572872 | tf_op jit(solution)/shard_map/ppermute | solution.py:16
  146.9 6.2 %copy-start.10 = (f32[256,8,128]{0,2,1:T(8,128)S(1)}, f32[256,8,128]{0,2,1:T(8,128)}, u32[]{:S(2)}) copy-start(f32[256,8,128]{0,2,1:T(8,128)} %fusion.9) | copy-start | bytes 3145732
  153.1 2.1 %copy-start.4 = (f32[8,256,256]{1,2,0:T(8,128)S(1)}, f32[8,256,256]{1,2,0:T(8,128)}, u32[]{:S(2)}) copy-start(f32[8,256,256]{1,2,0:T(8,128)} %get-tuple-element.64) | copy-start | bytes 6291460
  159.1 2.6 %copy-start.8 = (f32[256,8,128]{0,2,1:T(8,128)S(1)}, f32[256,8,128]{0,2,1:T(8,128)}, u32[]{:S(2)}) copy-start(f32[256,8,128]{0,2,1:T(8,128)} %fusion.15) | copy-start | bytes 3145732
where the time goes:
time: 164 us; the launch traced here: 163 us
  blocking collectives  45.2 us (28%)
  matrix products  37.3 us (23%)
  waiting for transfers between devices  32.8 us (20%)
  local copies, waits for them, and re-layouts  20.4 us (12%)
  other arithmetic  17.2 us (10%)
  between operations  7.45 us (5%)
  starting transfers between devices  2.57 us (2%)
    ppermute x6, waiting for transfers between devices, from_partner(): return lax.ppermute(block, axis, route)  32.8 us
    all_gather x1, blocking collectives, on_device(): lax.all_gather(totals[None, :], 'seq', axis=0, tiled=True)  20.3 us
    unnamed x1, blocking collectives  18 us
    unnamed x41, local copies, waits for them, and re-layouts  13.7 us
    psum x1, blocking collectives, on_device(): grad_level = lax.psum(partial_levels, 'head')  6.93 us
    dot_general x1, matrix products, on_device(): jnp.einsum('hts,thd->shd', weight * scores, grad_heads, precision=PRECISE)  5.89 us
    add x2, other arithmetic, on_device(): pending = pending[1:] + their_levels[1:]  4.82 us
    dot_general x1, matrix products, on_device(): jnp.einsum('thi,lhij->lthj', query_heads, state_stack, precision=PRECISE)  4.81 us
  transfers between devices with their start and end apart: 6, of which 4 were waited for; matrix products, arithmetic and copies ran while one was open for 29% of the time, Pallas kernels for 0%

commit v1 on v0

v1 whole, which is shorter than its diff:
```python
import functools

import jax
import jax.numpy as jnp
from jax import lax
from jax.experimental import pallas as pl
from jax.experimental.pallas import tpu as pltpu
from jax.sharding import PartitionSpec as P

HIGH = lax.Precision.HIGH
EXACT = lax.Precision.HIGHEST
LANES = 128
PARTS = 2
VMEM_LIMIT = 40 * 1024 * 1024


def dot(a, b, over, precision=HIGH):
    return lax.dot_general(
        a, b, (over, ((), ())), precision=precision, preferred_element_type=jnp.float32
    )


def params(steps):
    return pltpu.CompilerParams(
        dimension_semantics=("arbitrary",) * steps, vmem_limit_bytes=VMEM_LIMIT
    )


def cost(flops, moved):
    return pl.CostEstimate(flops=int(flops), bytes_accessed=int(moved), transcendentals=0)


def lane_of(shape):
    return lax.broadcasted_iota(jnp.int32, shape, len(shape) - 1)


def prepare_kernel(heads, decay_ref, segment_ref, cols_ref, rows_ref, table_ref):
    tokens = decay_ref.shape[0]
    head = lax.broadcasted_iota(jnp.int32, (heads, LANES), 0)
    lane = lane_of((heads, LANES))
    spread = ((lane < 3 * heads) & (lax.rem(lane, heads) == head)).astype(jnp.float32)
    wide = dot(decay_ref[...], spread, ((1,), (0,)), EXACT)
    earlier = lax.broadcasted_iota(jnp.int32, (tokens, tokens), 0) >= lane_of((tokens, tokens))
    running = dot(earlier.astype(jnp.float32), wide, ((1,), (0,)), EXACT)
    document = jnp.broadcast_to(segment_ref[...].astype(jnp.float32), (LANES, tokens)).T
    total, first, last = running[tokens - 1 :], document[:1], document[tokens - 1 :]
    source = jnp.exp(total - running) * (document == last).astype(jnp.float32)
    query = jnp.exp(running) * (document == first).astype(jnp.float32)
    lane = lane_of((tokens, LANES))
    cols = jnp.where(
        lane < heads,
        running,
        jnp.where(lane < 2 * heads, source, jnp.where(lane < 3 * heads, query, document)),
    )
    cols_ref[...] = cols
    rows_ref[...] = cols.T[: rows_ref.shape[0]]
    row = lax.broadcasted_iota(jnp.int32, (8, LANES), 0)
    table_ref[...] = jnp.where(row == 0, total, jnp.where(row == 1, last, first))


def factors_kernel(depth, device_ref, table_ref, factor_ref):
    stretches = table_ref.shape[0]
    device = device_ref[0]
    totals, lasts, firsts = table_ref[:, 0, :], table_ref[:, 1, :], table_ref[:, 2, :]
    stretch = lax.broadcasted_iota(jnp.int32, (stretches, LANES), 0) ^ device

    def at(values, index):
        return jnp.sum(jnp.where(stretch == index, values, 0.0), axis=0, keepdims=True)

    def span(low, high):
        inside = (stretch > low) & (stretch <= high)
        return jnp.exp(jnp.sum(jnp.where(inside, totals, 0.0), axis=0, keepdims=True))

    def reach(low_end, target):
        return jnp.where(at(firsts, target) == at(lasts, low_end), span(low_end, target - 1), 0.0)

    factors = []
    for distance in range(depth):
        low_end = ((device >> (distance + 1)) << (distance + 1)) + (1 << distance) - 1
        upper = ((device >> distance) & 1) == 1
        factors.append(jnp.where(upper, reach(low_end, device), 0.0))
    for distance in range(depth):
        low_end = ((device >> (distance + 1)) << (distance + 1)) + (1 << distance) - 1
        high_end = low_end + (1 << distance)
        factors.append(
            jnp.where(at(lasts, low_end) == at(lasts, high_end), span(low_end, high_end), 0.0)
        )
    middle = stretches // 2 - 1
    second = device // (stretches // 4) == 1
    for hop in (stretches // 4, stretches // 2):
        target = jnp.minimum(device + hop, stretches - 1)
        factors.append(jnp.where(second, reach(middle, target), 0.0))
    factor_ref[...] = jnp.zeros_like(factor_ref)
    for index, factor in enumerate(factors):
        factor_ref[index : index + 1, :] = factor


def states_kernel(heads, base, depth, q_ref, k_ref, v_ref, o_ref, cols_ref, level_ref, *outs):
    head = base + pl.program_id(0)
    cols = pltpu.roll(cols_ref[...], lax.rem(LANES - head, LANES), axis=1)
    source, query = cols[:, heads : heads + 1], cols[:, 2 * heads : 2 * heads + 1]
    outs[0][0] = dot(source * k_ref[...], v_ref[...], ((0,), (0,)))
    q, o = q_ref[...], o_ref[...]
    scaled = [(query * level_ref[:, d + 1 : d + 2]) * o for d in range(depth)]
    grads = dot(q, jnp.concatenate(scaled, axis=1), ((0,), (0,)))
    for d in range(depth):
        outs[d + 1][0] = grads[:, d * o.shape[1] : (d + 1) * o.shape[1]]


def local_kernel(
    heads, q_ref, k_ref, v_ref, o_ref, cols_ref, rows_ref, level_ref, gq_ref, gk_ref, gv_ref, out_ref
):
    head = pl.program_id(0)
    q, k, v, o = q_ref[...], k_ref[...], v_ref[...], o_ref[...]
    tokens = q.shape[0]
    cols = pltpu.roll(cols_ref[...], lax.rem(LANES - head, LANES), axis=1)
    document = cols_ref[:, 3 * heads : 3 * heads + 1]
    gap = cols[:, 0:1] - rows_ref[pl.ds(head, 1), :]
    visible = (
        lax.broadcasted_iota(jnp.int32, (tokens, tokens), 0) >= lane_of((tokens, tokens))
    ) & (document == rows_ref[3 * heads : 3 * heads + 1, :])
    within = jnp.where(visible, jnp.exp(jnp.minimum(gap, 0.0)), 0.0)
    scores = dot(q, k, ((1,), (1,)))
    grad_scores = dot(o, v, ((1,), (1,)))
    shared = within * grad_scores
    own = jnp.sum(shared * scores, axis=1, keepdims=True)
    level = level_ref[:, 0:1]
    shared = shared * level
    weighted = (within * level) * scores
    gv_ref[...] = dot(weighted, o, ((0,), (0,)))
    gq_ref[...] = dot(shared, k, ((1,), (0,)))
    gk_ref[...] = dot(shared, q, ((0,), (0,)))

    @pl.when(head == 0)
    def _():
        out_ref[...] = jnp.zeros_like(out_ref)

    out_ref[...] += jnp.where(lane_of(out_ref.shape) == 0, own, 0.0)


def levels_kernel(heads, base, levels, spare, last, *refs):
    q_ref, o_ref, cols_ref, level_ref, factor_ref, gq_in, lev_in = refs[:7]
    blocks = refs[7 : 7 + len(levels) + spare]
    gq_ref, lev_ref = refs[7 + len(levels) + spare :][:2]
    step = pl.program_id(0)
    head = base + step
    shift = lax.rem(LANES - head, LANES)
    query = pltpu.roll(cols_ref[...], shift, axis=1)[:, 2 * heads : 2 * heads + 1]
    factor = pltpu.roll(factor_ref[...], shift, axis=1)
    q, o = q_ref[...], o_ref[...]
    states = [block[0] for block in blocks[: len(levels)]]
    if spare:
        states[0] = states[0] + blocks[-1][0]
    width = o.shape[1]
    reached = dot(q, jnp.concatenate(states, axis=1), ((1,), (0,)))
    gq = gq_in[...]
    terms = jnp.zeros(lev_ref.shape, jnp.float32)
    for index, level in enumerate(levels):
        scale = query * factor[level - 1 : level, 0:1]
        gq = gq + (scale * level_ref[:, level : level + 1]) * dot(o, states[index], ((1,), (1,)))
        term = scale * jnp.sum(reached[:, index * width : (index + 1) * width] * o, axis=1, keepdims=True)
        terms = terms + jnp.where(lane_of(terms.shape) == level, term, 0.0)
    gq_ref[...] = gq

    @pl.when(step == 0)
    def _():
        lev_ref[...] = lev_in[...]

    lev_ref[...] += terms
    if last:
        turned_ref = refs[-1]

        @pl.when(step == pl.num_programs(0) - 1)
        def _():
            turned_ref[...] = lev_ref[...].T[: turned_ref.shape[0]]


def sources_kernel(heads, base, bit, block_row, refs_in, *refs):
    del refs_in
    device_ref, k_ref, v_ref, cols_ref, factor_ref, kept_ref, came_ref, gk_in, gv_in, gk_ref, gv_ref = refs
    head = base + pl.program_id(0)
    shift = lax.rem(LANES - head, LANES)
    source = pltpu.roll(cols_ref[...], shift, axis=1)[:, heads : heads + 1]
    factor = pltpu.roll(factor_ref[...], shift, axis=1)
    upper = ((device_ref[0] >> bit) & 1).astype(jnp.float32)
    own = upper + (1.0 - upper) * factor[block_row : block_row + 1, 0:1]
    state = own * kept_ref[0] + came_ref[0]
    gk_ref[...] = gk_in[...] + source * dot(v_ref[...], state, ((1,), (1,)))
    gv_ref[...] = gv_in[...] + source * dot(k_ref[...], state, ((1,), (0,)))


def blend_kernel(base, recipes, inputs, device_ref, factor_ref, *refs):
    arrays, outs = refs[:inputs], refs[inputs:]
    device = device_ref[0]
    factor = factor_ref[...]
    for head in range(arrays[0].shape[0]):
        column = factor[:, base + head : base + head + 1]
        values = [array[head] for array in arrays]
        for out, recipe in zip(outs, recipes):
            total = None
            for index, coefficient in recipe:
                term = values[index]
                weight = coefficient(device, lambda row: column[row : row + 1, :])
                term = term if weight is None else weight * term
                total = term if total is None else total + term
            out[head] = total


def blend(base, recipes, arrays, device, factor):
    shape = arrays[0].shape
    whole = pl.BlockSpec(memory_space=pltpu.VMEM)
    size = arrays[0].size * 4
    return pl.pallas_call(
        functools.partial(blend_kernel, base, recipes, len(arrays)),
        out_shape=[jax.ShapeDtypeStruct(shape, jnp.float32)] * len(recipes),
        in_specs=[pl.BlockSpec(memory_space=pltpu.SMEM), whole] + [whole] * len(arrays),
        out_specs=[whole] * len(recipes),
        compiler_params=pltpu.CompilerParams(vmem_limit_bytes=VMEM_LIMIT),
        cost_estimate=cost(size, size * (len(arrays) + len(recipes))),
    )(device, factor, *arrays)


def upper_or(bit, row):
    def weight(device, scalar):
        upper = ((device >> bit) & 1).astype(jnp.float32)
        return upper + (1.0 - upper) * scalar(row)

    return weight


def lower_or(bit, row):
    def weight(device, scalar):
        upper = ((device >> bit) & 1).astype(jnp.float32)
        return upper * scalar(row) + (1.0 - upper)

    return weight


def by(*rows):
    def weight(device, scalar):
        value = scalar(rows[0])
        for row in rows[1:]:
            value = value * scalar(row)
        return value

    return weight


def plain(device, scalar):
    return None


def send(array, route):
    return lax.ppermute(array, "seq", route)


def on_device(queries, key_input, value_input, grad_output, log_decay, level_weight, segment):
    stretches = lax.axis_size("seq")
    depth = stretches.bit_length() - 1
    tokens, heads = log_decay.shape
    width = queries.shape[1] // heads
    levels = level_weight.shape[1]
    quarter = stretches // 4
    device = lax.axis_index("seq").astype(jnp.int32).reshape(1)
    part_heads = heads // PARTS
    f32 = jnp.float32
    smem = pl.BlockSpec(memory_space=pltpu.SMEM)
    whole = pl.BlockSpec(memory_space=pltpu.VMEM)
    side_rows = -(-(3 * heads + 1) // 8) * 8
    factor_rows = -(-(2 * depth + 2) // 8) * 8
    token_bytes = tokens * width * 4
    state_bytes = width * width * 4
    pair_work = 2 * tokens * width * width * 3

    def shape(*dims):
        return jax.ShapeDtypeStruct(dims, f32)

    def head_block(base):
        return pl.BlockSpec((tokens, width), lambda i: (0, base + i))

    state_block = pl.BlockSpec((1, width, width), lambda i: (i, 0, 0))

    def fixed(*dims):
        return pl.BlockSpec(dims, lambda i: (0,) * len(dims))

    cols, rows, table = pl.pallas_call(
        functools.partial(prepare_kernel, heads),
        out_shape=[shape(tokens, LANES), shape(side_rows, tokens), shape(8, LANES)],
        in_specs=[whole, whole],
        out_specs=[whole] * 3,
        compiler_params=pltpu.CompilerParams(vmem_limit_bytes=VMEM_LIMIT),
    )(log_decay, segment.reshape(1, tokens))

    swaps = [[(i, i ^ (1 << d)) for i in range(stretches)] for d in range(depth)]
    table = table[None]
    for d in range(depth):
        table = jnp.concatenate([table, send(table, swaps[d])], axis=0)
    factor = pl.pallas_call(
        functools.partial(factors_kernel, depth),
        out_shape=shape(factor_rows, LANES),
        in_specs=[smem, whole],
        out_specs=whole,
        compiler_params=pltpu.CompilerParams(vmem_limit_bytes=VMEM_LIMIT),
    )(device, table)

    states, grads = [], []
    for part in range(PARTS):
        base = part * part_heads
        outs = pl.pallas_call(
            functools.partial(states_kernel, heads, base, depth),
            grid=(part_heads,),
            out_shape=[shape(part_heads, width, width)] * (depth + 1),
            in_specs=[head_block(base)] * 4 + [fixed(tokens, LANES), fixed(tokens, levels)],
            out_specs=[state_block] * (depth + 1),
            compiler_params=params(1),
            cost_estimate=cost(
                part_heads * pair_work * (depth + 1), part_heads * 4 * (token_bytes + state_bytes)
            ),
        )(queries, key_input, value_input, grad_output, cols, level_weight)
        states.append(outs[0])
        grads.append(outs[1:])

    def own_level(level):
        return level - 1

    def block_row(distance):
        return depth + distance

    third, fourth = 2 * depth, 2 * depth + 1
    up = [(i, i + quarter) for i in range(stretches) if not i // quarter & 1]
    down = [(i + quarter, i) for i in range(stretches) if not i // quarter & 1]
    second_third = [(quarter + i, 2 * quarter + i) for i in range(quarter)]
    second_fourth = [(quarter + i, 3 * quarter + i) for i in range(quarter)]
    third_second = [(b, a) for a, b in second_third]
    fourth_second = [(b, a) for a, b in second_fourth]

    came = [[None] * (depth + 1) for _ in range(PARTS)]
    spare = [None] * PARTS
    kept, sources = [None] * PARTS, [None] * PARTS
    running = list(states)
    parts = range(PARTS)
    from_third = [send(grads[p][depth - 1], third_second) for p in parts]
    for d in range(depth - 2):
        for p in parts:
            came[p][d + 1] = send(running[p], swaps[d])
        for p in parts:
            recipe = [(0, upper_or(d, block_row(d))), (1, lower_or(d, block_row(d)))]
            (running[p],) = blend(
                p * part_heads, [recipe], [running[p], came[p][d + 1]], device, factor
            )
    from_fourth = [send(grads[p][depth - 1], fourth_second) for p in parts]
    for p in parts:
        came[p][depth - 1] = send(running[p], up)
        spare[p] = send(running[p], second_fourth)
    from_upper = [None] * PARTS
    for p in parts:
        recipe = [
            (0, by(own_level(depth - 1))),
            (1, by(block_row(depth - 2), third)),
        ]
        (message,) = blend(
            p * part_heads, [recipe], [grads[p][depth - 2], from_third[p]], device, factor
        )
        from_upper[p] = send(message, down)
    for p in parts:
        recipe = [(0, plain), (1, by(block_row(depth - 2)))]
        (half,) = blend(
            p * part_heads, [recipe], [running[p], came[p][depth - 1]], device, factor
        )
        came[p][depth] = send(half, second_third)
    for p in parts:
        pending, source_arrays = None, [from_upper[p], from_third[p], from_fourth[p]]
        total = [(0, plain), (1, by(third)), (2, by(fourth))]
        if depth == 2:
            (kept[p],) = blend(p * part_heads, [total], source_arrays, device, factor)
            continue
        (pending,) = blend(p * part_heads, [total], source_arrays, device, factor)
        for d in range(depth - 3, -1, -1):
            message = [(0, lower_or(d, block_row(d))), (1, by(own_level(d + 1)))]
            (outgoing,) = blend(p * part_heads, [message], [pending, grads[p][d]], device, factor)
            arrived = send(outgoing, swaps[d])
            if d == 0:
                kept[p], sources[p] = pending, arrived
            else:
                recipe = [(0, upper_or(d, block_row(d))), (1, plain)]
                (pending,) = blend(p * part_heads, [recipe], [pending, arrived], device, factor)

    grad_query, grad_key, grad_value, terms = pl.pallas_call(
        functools.partial(local_kernel, heads),
        grid=(heads,),
        out_shape=[shape(*queries.shape)] * 3 + [shape(tokens, LANES)],
        in_specs=[head_block(0)] * 4
        + [fixed(tokens, LANES), fixed(side_rows, tokens), fixed(tokens, levels)],
        out_specs=[head_block(0)] * 3 + [fixed(tokens, LANES)],
        compiler_params=params(1),
        cost_estimate=cost(heads * 30 * tokens * tokens * width, heads * 7 * token_bytes),
    )(queries, key_input, value_input, grad_output, cols, rows, level_weight)

    turned_rows = -(-levels // 8) * 8

    def add_levels(chosen, part, grad_query, terms, last):
        blocks = [came[part][level] for level in chosen]
        extra = chosen == [depth]
        if extra:
            blocks.append(spare[part])
        base = part * part_heads
        outs = pl.pallas_call(
            functools.partial(levels_kernel, heads, base, chosen, int(extra), last),
            grid=(part_heads,),
            out_shape=[shape(*queries.shape), shape(tokens, LANES)]
            + [shape(turned_rows, tokens)] * last,
            in_specs=[head_block(base)] * 2
            + [fixed(tokens, LANES), fixed(tokens, levels), fixed(factor_rows, LANES)]
            + [head_block(base), fixed(tokens, LANES)]
            + [state_block] * len(blocks),
            out_specs=[head_block(base), fixed(tokens, LANES)]
            + [fixed(turned_rows, tokens)] * last,
            input_output_aliases={5: 0, 6: 1},
            compiler_params=params(1),
            cost_estimate=cost(
                part_heads * pair_work * 2 * len(chosen), part_heads * 4 * token_bytes
            ),
        )(queries, grad_output, cols, level_weight, factor, grad_query, terms, *blocks)
        return outs

    for p in parts:
        grad_query, terms = add_levels(list(range(1, depth)), p, grad_query, terms, False)
    for p in parts:
        last = p == PARTS - 1
        outs = add_levels([depth], p, grad_query, terms, last)
        grad_query, terms = outs[:2]
        if last:
            turned = outs[2]

    groups = lax.axis_size("head")
    others = [
        lax.ppermute(turned, "head", [(i, (i + k) % groups) for i in range(groups)])
        for k in range(1, groups)
    ]

    for p in parts:
        base = p * part_heads
        grad_key, grad_value = pl.pallas_call(
            functools.partial(sources_kernel, heads, base, 0, block_row(0), None),
            grid=(part_heads,),
            out_shape=[shape(*queries.shape)] * 2,
            in_specs=[smem, head_block(base), head_block(base), fixed(tokens, LANES)]
            + [fixed(factor_rows, LANES), state_block, state_block]
            + [head_block(base)] * 2,
            out_specs=[head_block(base)] * 2,
            input_output_aliases={7: 0, 8: 1},
            compiler_params=params(1),
            cost_estimate=cost(part_heads * pair_work * 2, part_heads * 6 * token_bytes),
        )(device, key_input, value_input, cols, factor, kept[p], sources[p], grad_key, grad_value)

    def level_sum_kernel(*refs):
        total = refs[0][...]
        for ref in refs[1:-1]:
            total = total + ref[...]
        wide = jnp.concatenate(
            [total, jnp.zeros((LANES - turned_rows, tokens), f32)], axis=0
        )
        refs[-1][...] = wide.T[:, :levels]

    grad_level = pl.pallas_call(
        level_sum_kernel,
        out_shape=shape(tokens, levels),
        in_specs=[whole] * groups,
        out_specs=whole,
    )(turned, *others)
    return grad_query, grad_key, grad_value, grad_level


def solution(mesh):
    in_specs = (
        P("seq", "head"),
        P("seq", "head"),
        P("seq", "head"),
        P("seq", "head"),
        P("seq", "head"),
        P("seq", None),
        P("seq"),
    )
    out_specs = (P("seq", "head"), P("seq", "head"), P("seq", "head"), P("seq", None))
    return jax.shard_map(
        on_device, mesh=mesh, in_specs=in_specs, out_specs=out_specs, check_vma=False
    )
```

time: 164 us -> 104 us (0.63)
  the two profiles are of different devices: /device:TPU:2 before, /device:TPU:10 now
where the time goes in v1:
time: 104 us; the launch traced here: 103 us
  Pallas kernels  43.7 us (42%)
  starting transfers between devices  43.3 us (42%)
  local copies, waits for them, and re-layouts  9.3 us (9%)
  waiting for transfers between devices  5.22 us (5%)
    ppermute x19, starting transfers between devices, send(): return lax.ppermute(array, 'seq', route)  40.3 us
    pallas_call x4, Pallas kernels, add_levels(): pl.pallas_call(functools.partial(levels_kernel, heads, base, chosen, int(...  16.6 us
    unnamed x31, local copies, waits for them, and re-layouts  9.3 us
    pallas_call x1, Pallas kernels, on_device(): pl.pallas_call(functools.partial(local_kernel, heads), grid=(heads,), out...  8.55 us
    pallas_call x2, Pallas kernels, on_device(): pl.pallas_call(functools.partial(sources_kernel, heads, base, 0, block_ro...  8.35 us
    pallas_call x2, Pallas kernels, on_device(): pl.pallas_call(functools.partial(states_kernel, heads, base, depth), grid...  6.4 us
    ppermute x19, waiting for transfers between devices, send(): return lax.ppermute(array, 'seq', route)  5.21 us
    ppermute x3, starting transfers between devices, on_device(): lax.ppermute(turned, 'head', [(i, (i + k) % groups) for i in range(groups)])  3 us
  transfers between devices with their start and end apart: 22, of which 3 were waited for; matrix products, arithmetic and copies ran while one was open for 0% of the time, Pallas kernels for 40%

profile of v1, /device:TPU:10, one launch (start us, length us, event | category | flops | bytes accessed | tf_op | source)
XLA Modules:
  0.0 102.6 jit_solution(5471266544627308043)
XLA Ops:
  0.6 0.8 copy.23.decay_ref
  1.5 0.7 copy-done.9
  2.1 0.8 shard_map.102
  3.0 0.6 collective-permute-start
  3.7 2.9 %collective-permute-done = f32[1,8,128]{2,1,0:T(8,128)S(1)} collective-permute-done((f32[1,8,128]{2,1,0:T(8,128)S(1)}, f32[1,8,128]{2,1,0:T(8,128)S(1)}, u32[]{:S(2)}, u32[]{:S(2)}) %collective-permute-start) | collective-permute-done | bytes 4128 | tf_op jit(solution)/shard_map/ppermute | solution.py:254
  6.6 0.4 collective-permute-start.1
  7.1 1.2 %copy-done = f32[256,1024]{1,0:T(8,128)S(1)} copy-done((f32[256,1024]{1,0:T(8,128)S(1)}, f32[256,1024]{1,0:T(8,128)}, u32[]{:S(2)}) %copy-start) | copy-done | bytes 1048600
  8.3 1.2 %copy-done.2 = f32[256,1024]{1,0:T(8,128)S(1)} copy-done((f32[256,1024]{1,0:T(8,128)S(1)}, f32[256,1024]{1,0:T(8,128)}, u32[]{:S(2)}) %copy-start.2) | copy-done | bytes 1048600
  9.5 1.2 %copy-done.4 = f32[256,1024]{1,0:T(8,128)S(1)} copy-done((f32[256,1024]{1,0:T(8,128)S(1)}, f32[256,1024]{1,0:T(8,128)}, u32[]{:S(2)}) %copy-start.4) | copy-done | bytes 1048600
  10.8 1.2 %copy-done.6 = f32[256,1024]{1,0:T(8,128)S(1)} copy-done((f32[256,1024]{1,0:T(8,128)S(1)}, f32[256,1024]{1,0:T(8,128)}, u32[]{:S(2)}) %copy-start.6) | copy-done | bytes 1048600
  12.0 3.2 %shard_map.105 = (f32[4,128,128]{2,1,0:T(8,128)S(1)}, f32[4,128,128]{2,1,0:T(8,128)S(1)}, f32[4,128,128]{2,1,0:T(8,128)S(1)}, f32[4,128,128]{2,1,0:T(8,128)S(1)}) custom-call(f32[256,1024]{1,0:T(8,128)S(1)} %copy-done, f32[256,1024]{1,0:T(8,128)S(1)} %copy-done.4, f32[256,1024]{1,0:T(8,128)S(1)} %copy-done.6, f32[256,1024]{1,0:T(8,128)S(1)} %copy-done.2, ...), custom_call_target="tpu_custom_call" | custom-call | flops 402653184 | bytes 3145728 | tf_op jit(solution)/shard_map/pallas_call | solution.py:309
  15.2 1.3 %collective-permute-start.15 = (f32[4,128,128]{2,1,0:T(8,128)S(1)}, f32[4,128,128]{2,1,0:T(8,128)S(1)}, u32[]{:S(2)}, u32[]{:S(2)}) collective-permute-start(f32[4,128,128]{2,1,0:T(8,128)S(1)} %get-tuple-element.49), channel_id=1, source_target_pairs={{16,8},{20,12},{17,9},{21,13},{18,10},{22,14},{19,11},{23,15}} | collective-permute-start | bytes 786440 | tf_op jit(solution)/shard_map/ppermute | solution.py:254
  16.5 1.3 %collective-permute-start.17 = (f32[4,128,128]{2,1,0:T(8,128)S(1)}, f32[4,128,128]{2,1,0:T(8,128)S(1)}, u32[]{:S(2)}, u32[]{:S(2)}) collective-permute-start(f32[4,128,128]{2,1,0:T(8,128)S(1)} %get-tuple-element.49), channel_id=1, source_target_pairs={{24,8},{28,12},{25,9},{29,13},{26,10},{30,14},{27,11},{31,15}} | collective-permute-start | bytes 786440 | tf_op jit(solution)/shard_map/ppermute | solution.py:254
  17.8 0.2 collective-permute-start.3
  17.9 3.6 %collective-permute-start.2 = (f32[4,8,128]{2,1,0:T(8,128)S(1)}, f32[4,8,128]{2,1,0:T(8,128)S(1)}, u32[]{:S(2)}, u32[]{:S(2)}) collective-permute-start(f32[4,8,128]{2,1,0:T(8,128)S(1)} %pad_maximum_fusion.1), channel_id=1, source_target_pairs={{0,16},{4,20},{8,24},{12,28},{16,0},{20,4},{24,8},{28,12},{1,17},{... | collective-permute-start | bytes 49160 | tf_op jit(solution)/shard_map/ppermute | solution.py:254
  21.5 3.2 %shard_map.108 = (f32[4,128,128]{2,1,0:T(8,128)S(1)}, f32[4,128,128]{2,1,0:T(8,128)S(1)}, f32[4,128,128]{2,1,0:T(8,128)S(1)}, f32[4,128,128]{2,1,0:T(8,128)S(1)}) custom-call(f32[256,1024]{1,0:T(8,128)S(1)} %copy-done, f32[256,1024]{1,0:T(8,128)S(1)} %copy-done.4, f32[256,1024]{1,0:T(8,128)S(1)} %copy-done.6, f32[256,1024]{1,0:T(8,128)S(1)} %copy-done.2, ...), custom_call_target="tpu_custom_call" | custom-call | flops 402653184 | bytes 3145728 | tf_op jit(solution)/shard_map/pallas_call | solution.py:309
  24.7 2.0 %collective-permute-start.5 = (f32[4,128,128]{2,1,0:T(8,128)S(1)}, f32[4,128,128]{2,1,0:T(8,128)S(1)}, u32[]{:S(2)}, u32[]{:S(2)}) collective-permute-start(f32[4,128,128]{2,1,0:T(8,128)S(1)} %get-tuple-element.39.refs_0_), channel_id=1, source_target_pairs={{0,4},{4,0},{8,12},{12,8},{16,20},{20,16},{24,28},{28,24},{1,5},{5... | collective-permute-start | bytes 786440 | tf_op jit(solution)/shard_map/ppermute | solution.py:254
  26.7 1.3 %collective-permute-start.11 = (f32[4,128,128]{2,1,0:T(8,128)S(1)}, f32[4,128,128]{2,1,0:T(8,128)S(1)}, u32[]{:S(2)}, u32[]{:S(2)}) collective-permute-start(f32[4,128,128]{2,1,0:T(8,128)S(1)} %get-tuple-element.46), channel_id=1, source_target_pairs={{16,8},{20,12},{17,9},{21,13},{18,10},{22,14},{19,11},{23,15}} | collective-permute-start | bytes 786440 | tf_op jit(solution)/shard_map/ppermute | solution.py:254
  28.1 2.1 %collective-permute-done.15.refs_1_ = f32[4,128,128]{2,1,0:T(8,128)S(1)} collective-permute-done((f32[4,128,128]{2,1,0:T(8,128)S(1)}, f32[4,128,128]{2,1,0:T(8,128)S(1)}, u32[]{:S(2)}, u32[]{:S(2)}) %collective-permute-start.15) | collective-permute-done | bytes 262176 | tf_op jit(solution)/shard_map/ppermute | solution.py:254
  30.3 4.5 %collective-permute-start.16 = (f32[4,128,128]{2,1,0:T(8,128)S(1)}, f32[4,128,128]{2,1,0:T(8,128)S(1)}, u32[]{:S(2)}, u32[]{:S(2)}) collective-permute-start(f32[4,128,128]{2,1,0:T(8,128)S(1)} %shard_map.118), channel_id=1, source_target_pairs={{8,0},{12,4},{24,16},{28,20},{9,1},{13,5},{25,17},{29,21},{10,2},{... | collective-permute-start | bytes 786440 | tf_op jit(solution)/shard_map/ppermute | solution.py:254
  35.0 1.3 %collective-permute-start.4 = (f32[4,128,128]{2,1,0:T(8,128)S(1)}, f32[4,128,128]{2,1,0:T(8,128)S(1)}, u32[]{:S(2)}, u32[]{:S(2)}) collective-permute-start(f32[4,128,128]{2,1,0:T(8,128)S(1)} %shard_map.106.refs_0_), channel_id=1, source_target_pairs={{0,8},{4,12},{16,24},{20,28},{1,9},{5,13},{17,25},{21,29},{2,10},{... | collective-permute-start | bytes 786440 | tf_op jit(solution)/shard_map/ppermute | solution.py:254
  36.3 0.1 shard_map.109.refs_0_
  36.4 1.3 %collective-permute-start.6 = (f32[4,128,128]{2,1,0:T(8,128)S(1)}, f32[4,128,128]{2,1,0:T(8,128)S(1)}, u32[]{:S(2)}, u32[]{:S(2)}) collective-permute-start(f32[4,128,128]{2,1,0:T(8,128)S(1)} %shard_map.109.refs_0_), channel_id=1, source_target_pairs={{0,8},{4,12},{16,24},{20,28},{1,9},{5,13},{17,25},{21,29},{2,10},{... | collective-permute-start | bytes 786440 | tf_op jit(solution)/shard_map/ppermute | solution.py:254
  37.7 1.3 %collective-permute-start.13 = (f32[4,128,128]{2,1,0:T(8,128)S(1)}, f32[4,128,128]{2,1,0:T(8,128)S(1)}, u32[]{:S(2)}, u32[]{:S(2)}) collective-permute-start(f32[4,128,128]{2,1,0:T(8,128)S(1)} %get-tuple-element.46), channel_id=1, source_target_pairs={{24,8},{28,12},{25,9},{29,13},{26,10},{30,14},{27,11},{31,15}} | collective-permute-start | bytes 786440 | tf_op jit(solution)/shard_map/ppermute | solution.py:254
  39.0 0.1 shard_map.115
  39.2 4.0 %collective-permute-start.12 = (f32[4,128,128]{2,1,0:T(8,128)S(1)}, f32[4,128,128]{2,1,0:T(8,128)S(1)}, u32[]{:S(2)}, u32[]{:S(2)}) collective-permute-start(f32[4,128,128]{2,1,0:T(8,128)S(1)} %shard_map.115), channel_id=1, source_target_pairs={{8,0},{12,4},{24,16},{28,20},{9,1},{13,5},{25,17},{29,21},{10,2},{... | collective-permute-start | bytes 786440 | tf_op jit(solution)/shard_map/ppermute | solution.py:254
  43.2 2.8 %collective-permute-start.8 = (f32[4,128,128]{2,1,0:T(8,128)S(1)}, f32[4,128,128]{2,1,0:T(8,128)S(1)}, u32[]{:S(2)}, u32[]{:S(2)}) collective-permute-start(f32[4,128,128]{2,1,0:T(8,128)S(1)} %shard_map.106.refs_0_), channel_id=1, source_target_pairs={{8,24},{12,28},{9,25},{13,29},{10,26},{14,30},{11,27},{15,31}} | collective-permute-start | bytes 786440 | tf_op jit(solution)/shard_map/ppermute | solution.py:254
  46.0 0.1 shard_map.119.refs_0_.refs_5_
  46.3 1.4 %collective-permute-start.10 = (f32[4,128,128]{2,1,0:T(8,128)S(1)}, f32[4,128,128]{2,1,0:T(8,128)S(1)}, u32[]{:S(2)}, u32[]{:S(2)}) collective-permute-start(f32[4,128,128]{2,1,0:T(8,128)S(1)} %shard_map.109.refs_0_), channel_id=1, source_target_pairs={{8,24},{12,28},{9,25},{13,29},{10,26},{14,30},{11,27},{15,31}} | collective-permute-start | bytes 786440 | tf_op jit(solution)/shard_map/ppermute | solution.py:254
  48.0 9.5 %collective-permute-start.7 = (f32[4,128,128]{2,1,0:T(8,128)S(1)}, f32[4,128,128]{2,1,0:T(8,128)S(1)}, u32[]{:S(2)}, u32[]{:S(2)}) collective-permute-start(f32[4,128,128]{2,1,0:T(8,128)S(1)} %shard_map.111), channel_id=1, source_target_pairs={{8,16},{12,20},{9,17},{13,21},{10,18},{14,22},{11,19},{15,23}} | collective-permute-start | bytes 786440 | tf_op jit(solution)/shard_map/ppermute | solution.py:254
  57.8 1.4 %collective-permute-start.9 = (f32[4,128,128]{2,1,0:T(8,128)S(1)}, f32[4,128,128]{2,1,0:T(8,128)S(1)}, u32[]{:S(2)}, u32[]{:S(2)}) collective-permute-start(f32[4,128,128]{2,1,0:T(8,128)S(1)} %shard_map.113), channel_id=1, source_target_pairs={{8,16},{12,20},{9,17},{13,21},{10,18},{14,22},{11,19},{15,23}} | collective-permute-start | bytes 786440 | tf_op jit(solution)/shard_map/ppermute | solution.py:254
  59.2 1.1 %collective-permute-start.18 = (f32[4,128,128]{2,1,0:T(8,128)S(1)}, f32[4,128,128]{2,1,0:T(8,128)S(1)}, u32[]{:S(2)}, u32[]{:S(2)}) collective-permute-start(f32[4,128,128]{2,1,0:T(8,128)S(1)} %shard_map.120), channel_id=1, source_target_pairs={{0,4},{4,0},{8,12},{12,8},{16,20},{20,16},{24,28},{28,24},{1,5},{5... | collective-permute-start | bytes 786440 | tf_op jit(solution)/shard_map/ppermute | solution.py:254
  60.3 0.1 shard_map.116.refs_0_.refs_5_
  60.5 0.1 shard_map.117
  60.6 1.0 %collective-permute-start.14 = (f32[4,128,128]{2,1,0:T(8,128)S(1)}, f32[4,128,128]{2,1,0:T(8,128)S(1)}, u32[]{:S(2)}, u32[]{:S(2)}) collective-permute-start(f32[4,128,128]{2,1,0:T(8,128)S(1)} %shard_map.117), channel_id=1, source_target_pairs={{0,4},{4,0},{8,12},{12,8},{16,20},{20,16},{24,28},{28,24},{1,5},{5... | collective-permute-start | bytes 786440 | tf_op jit(solution)/shard_map/ppermute | solution.py:254
  61.7 8.6 %shard_map.104 = (f32[256,1024]{1,0:T(8,128)}, f32[256,1024]{1,0:T(8,128)}, f32[256,1024]{1,0:T(8,128)}, f32[256,128]{1,0:T(8,128)S(1)}) custom-call(f32[256,1024]{1,0:T(8,128)S(1)} %copy-done.1, f32[256,1024]{1,0:T(8,128)S(1)} %copy-done.5, f32[256,1024]{1,0:T(8,128)S(1)} %copy-done.7, f32[256,1024]{1,0:T(8,128)S(1)} %copy-done.3, ...), custom_call_target="tpu_custom_call" | custom-call | flops 2013265920 | bytes 7340032 | tf_op jit(solution)/shard_map/pallas_call | solution.py:388
  70.2 4.2 %shard_map.107 = (f32[256,1024]{1,0:T(8,128)}, f32[256,128]{1,0:T(8,128)S(1)}) custom-call(f32[256,1024]{1,0:T(8,128)S(1)} %copy-done.1, f32[256,1024]{1,0:T(8,128)S(1)} %copy-done.3, f32[256,128]{1,0:T(8,128)S(1)} %get-tuple-element.31.cols_ref.refs_2_.refs_3_, f32[256,7]{1,0:T(8,128)S(1)} %copy.30.level_ref.refs_3_, ...), custom_call_target="tpu_custom_call", output_to_operand_aliasing={{0}: (5, {}), {1}: (6, {})} | custom-call | flops 402653184 | bytes 2097152 | tf_op jit(solution)/shard_map/pallas_call | solution.py:407
  74.5 4.2 %shard_map.110 = (f32[256,1024]{1,0:T(8,128)}, f32[256,128]{1,0:T(8,128)S(1)}) custom-call(f32[256,1024]{1,0:T(8,128)S(1)} %copy-done.1, f32[256,1024]{1,0:T(8,128)S(1)} %copy-done.3, f32[256,128]{1,0:T(8,128)S(1)} %get-tuple-element.31.cols_ref.refs_2_.refs_3_, f32[256,7]{1,0:T(8,128)S(1)} %copy.30.level_ref.refs_3_, ...), custom_call_target="tpu_custom_call", output_to_operand_aliasing={{0}: (5, {}), {1}: (6, {})} | custom-call | flops 402653184 | bytes 2097152 | tf_op jit(solution)/shard_map/pallas_call | solution.py:407
  78.7 4.0 %shard_map.112 = (f32[256,1024]{1,0:T(8,128)}, f32[256,128]{1,0:T(8,128)S(1)}) custom-call(f32[256,1024]{1,0:T(8,128)S(1)} %copy-done.1, f32[256,1024]{1,0:T(8,128)S(1)} %copy-done.3, f32[256,128]{1,0:T(8,128)S(1)} %get-tuple-element.31.cols_ref.refs_2_.refs_3_, f32[256,7]{1,0:T(8,128)S(1)} %copy.30.level_ref.refs_3_, ...), custom_call_target="tpu_custom_call", output_to_operand_aliasing={{0}: (5, {}), {1}: (6, {})} | custom-call | flops 201326592 | bytes 2097152 | tf_op jit(solution)/shard_map/pallas_call | solution.py:407
  82.7 4.1 %shard_map.114 = (f32[256,1024]{1,0:T(8,128)}, f32[256,128]{1,0:T(8,128)S(1)}, f32[8,256]{1,0:T(8,128)S(1)}) custom-call(f32[256,1024]{1,0:T(8,128)S(1)} %copy-done.1, f32[256,1024]{1,0:T(8,128)S(1)} %copy-done.3, f32[256,128]{1,0:T(8,128)S(1)} %get-tuple-element.31.cols_ref.refs_2_.refs_3_, ...), custom_call_target="tpu_custom_call", output_to_operand_aliasing={{0}: (5, {}), {1}: (6, {})} | custom-call | flops 201326592 | bytes 2097152 | tf_op jit(solution)/shard_map/pallas_call | solution.py:407
  86.9 1.6 %collective-permute-start.20 = (f32[8,256]{1,0:T(8,128)S(1)}, f32[8,256]{1,0:T(8,128)S(1)}, u32[]{:S(2)}, u32[]{:S(2)}) collective-permute-start(f32[8,256]{1,0:T(8,128)S(1)} %get-tuple-element.57.refs_0_), channel_id=1, source_target_pairs={{0,2},{1,3},{2,0},{3,1},{4,6},{5,7},{6,4},{7,5},{8,10},{9,11},{10,... | collective-permute-start | bytes 24584 | tf_op jit(solution)/shard_map/ppermute | solution.py:437
  88.5 1.4 %collective-permute-start.21 = (f32[8,256]{1,0:T(8,128)S(1)}, f32[8,256]{1,0:T(8,128)S(1)}, u32[]{:S(2)}, u32[]{:S(2)}) collective-permute-start(f32[8,256]{1,0:T(8,128)S(1)} %get-tuple-element.57.refs_0_), channel_id=1, source_target_pairs={{0,3},{1,0},{2,1},{3,2},{4,7},{5,4},{6,5},{7,6},{8,11},{9,8},{10,9... | collective-permute-start | bytes 24584 | tf_op jit(solution)/shard_map/ppermute | solution.py:437
  89.9 4.2 %shard_map.121 = (f32[256,1024]{1,0:T(8,128)}, f32[256,1024]{1,0:T(8,128)}) custom-call(s32[1]{0:T(128)} %bitcast.1.device_ref.refs_0_, f32[256,1024]{1,0:T(8,128)S(1)} %copy-done.5, f32[256,1024]{1,0:T(8,128)S(1)} %copy-done.7, f32[256,128]{1,0:T(8,128)S(1)} %get-tuple-element.31.cols_ref.refs_2_.refs_3_, ...), custom_call_target="tpu_custom_call", output_to_operand_aliasing={{0}: (7, {}), {1}: (8, {})} | custom-call | flops 201326592 | bytes 3145728 | tf_op jit(solution)/shard_map/pallas_call | solution.py:443
  94.1 4.2 %shard_map.122 = (f32[256,1024]{1,0:T(8,128)}, f32[256,1024]{1,0:T(8,128)}) custom-call(s32[1]{0:T(128)} %bitcast.1.device_ref.refs_0_, f32[256,1024]{1,0:T(8,128)S(1)} %copy-done.5, f32[256,1024]{1,0:T(8,128)S(1)} %copy-done.7, f32[256,128]{1,0:T(8,128)S(1)} %get-tuple-element.31.cols_ref.refs_2_.refs_3_, ...), custom_call_target="tpu_custom_call", output_to_operand_aliasing={{0}: (7, {}), {1}: (8, {})} | custom-call | flops 201326592 | bytes 3145728 | tf_op jit(solution)/shard_map/pallas_call | solution.py:443
  98.3 0.6 copy-done.11
  98.9 0.6 copy-done.13
  99.5 1.5 %shard_map.123 = f32[256,7]{1,0:T(8,128)} custom-call(f32[8,256]{1,0:T(8,128)} %copy-done.8, f32[8,256]{1,0:T(8,128)} %copy-done.11, f32[8,256]{1,0:T(8,128)} %copy-done.12, f32[8,256]{1,0:T(8,128)} %copy-done.13), custom_call_target="tpu_custom_call" | custom-call | tf_op jit(solution)/shard_map/pallas_call | solution.py:465
  101.0 1.6 %copy.31 = f32[256,7]{0,1:T(8,128)} copy(f32[256,7]{1,0:T(8,128)} %shard_map.123) | data formatting | bytes 14336
  (52 shorter events, 1.1 us)
Async XLA Ops:
  1.5 0.7 copy-start.9
  2.1 1.4 %copy-start.10 = (f32[256,7]{0,1:T(8,128)S(1)}, f32[256,7]{0,1:T(8,128)}, u32[]{:S(2)}) copy-start(f32[256,7]{0,1:T(8,128)} %param.12) | copy-start | bytes 21508
  3.0 3.7 %collective-permute-start = (f32[1,8,128]{2,1,0:T(8,128)S(1)}, f32[1,8,128]{2,1,0:T(8,128)S(1)}, u32[]{:S(2)}, u32[]{:S(2)}) collective-permute-start(f32[1,8,128]{2,1,0:T(8,128)S(1)} %bitcast.3), channel_id=1, source_target_pairs={{0,4},{4,0},{8,12},{12,8},{16,20},{20,16},{24,28},{28,24},{1,5},{5... | collective-permute-start | bytes 12296 | tf_op jit(solution)/shard_map/ppermute | solution.py:254
  6.6 11.3 %collective-permute-start.1 = (f32[2,8,128]{2,1,0:T(8,128)S(1)}, f32[2,8,128]{2,1,0:T(8,128)S(1)}, u32[]{:S(2)}, u32[]{:S(2)}) collective-permute-start(f32[2,8,128]{2,1,0:T(8,128)S(1)} %pad_maximum_fusion.2), channel_id=1, source_target_pairs={{0,8},{4,12},{8,0},{12,4},{16,24},{20,28},{24,16},{28,20},{1,9},{5... | collective-permute-start | bytes 24584 | tf_op jit(solution)/shard_map/ppermute | solution.py:254
  7.1 1.2 %copy-start = (f32[256,1024]{1,0:T(8,128)S(1)}, f32[256,1024]{1,0:T(8,128)}, u32[]{:S(2)}) copy-start(f32[256,1024]{1,0:T(8,128)} %refs_0_.7) | copy-start | bytes 3145732
  8.3 1.2 %copy-start.2 = (f32[256,1024]{1,0:T(8,128)S(1)}, f32[256,1024]{1,0:T(8,128)}, u32[]{:S(2)}) copy-start(f32[256,1024]{1,0:T(8,128)} %refs_1_.9) | copy-start | bytes 3145732
  9.5 1.2 %copy-start.4 = (f32[256,1024]{1,0:T(8,128)S(1)}, f32[256,1024]{1,0:T(8,128)}, u32[]{:S(2)}) copy-start(f32[256,1024]{1,0:T(8,128)} %refs_1_.11) | copy-start | bytes 3145732
  10.8 1.2 %copy-start.6 = (f32[256,1024]{1,0:T(8,128)S(1)}, f32[256,1024]{1,0:T(8,128)}, u32[]{:S(2)}) copy-start(f32[256,1024]{1,0:T(8,128)} %refs_2_.3) | copy-start | bytes 3145732
  15.2 15.0 %collective-permute-start.15 = (f32[4,128,128]{2,1,0:T(8,128)S(1)}, f32[4,128,128]{2,1,0:T(8,128)S(1)}, u32[]{:S(2)}, u32[]{:S(2)}) collective-permute-start(f32[4,128,128]{2,1,0:T(8,128)S(1)} %get-tuple-element.49), channel_id=1, source_target_pairs={{16,8},{20,12},{17,9},{21,13},{18,10},{22,14},{19,11},{23,15}} | collective-permute-start | bytes 786440 | tf_op jit(solution)/shard_map/ppermute | solution.py:254
  16.5 22.7 %collective-permute-start.17 = (f32[4,128,128]{2,1,0:T(8,128)S(1)}, f32[4,128,128]{2,1,0:T(8,128)S(1)}, u32[]{:S(2)}, u32[]{:S(2)}) collective-permute-start(f32[4,128,128]{2,1,0:T(8,128)S(1)} %get-tuple-element.49), channel_id=1, source_target_pairs={{24,8},{28,12},{25,9},{29,13},{26,10},{30,14},{27,11},{31,15}} | collective-permute-start | bytes 786440 | tf_op jit(solution)/shard_map/ppermute | solution.py:254
  17.8 17.0 %collective-permute-start.3 = (f32[4,128,128]{2,1,0:T(8,128)S(1)}, f32[4,128,128]{2,1,0:T(8,128)S(1)}, u32[]{:S(2)}, u32[]{:S(2)}) collective-permute-start(f32[4,128,128]{2,1,0:T(8,128)S(1)} %get-tuple-element.36.refs_0_), channel_id=1, source_target_pairs={{0,4},{4,0},{8,12},{12,8},{16,20},{20,16},{24,28},{28,24},{1,5},{5... | collective-permute-start | bytes 786440 | tf_op jit(solution)/shard_map/ppermute | solution.py:254
  17.9 8.8 %collective-permute-start.2 = (f32[4,8,128]{2,1,0:T(8,128)S(1)}, f32[4,8,128]{2,1,0:T(8,128)S(1)}, u32[]{:S(2)}, u32[]{:S(2)}) collective-permute-start(f32[4,8,128]{2,1,0:T(8,128)S(1)} %pad_maximum_fusion.1), channel_id=1, source_target_pairs={{0,16},{4,20},{8,24},{12,28},{16,0},{20,4},{24,8},{28,12},{1,17},{... | collective-permute-start | bytes 49160 | tf_op jit(solution)/shard_map/ppermute | solution.py:254
  24.7 11.6 %collective-permute-start.5 = (f32[4,128,128]{2,1,0:T(8,128)S(1)}, f32[4,128,128]{2,1,0:T(8,128)S(1)}, u32[]{:S(2)}, u32[]{:S(2)}) collective-permute-start(f32[4,128,128]{2,1,0:T(8,128)S(1)} %get-tuple-element.39.refs_0_), channel_id=1, source_target_pairs={{0,4},{4,0},{8,12},{12,8},{16,20},{20,16},{24,28},{28,24},{1,5},{5... | collective-permute-start | bytes 786440 | tf_op jit(solution)/shard_map/ppermute | solution.py:254
  26.7 11.0 %collective-permute-start.11 = (f32[4,128,128]{2,1,0:T(8,128)S(1)}, f32[4,128,128]{2,1,0:T(8,128)S(1)}, u32[]{:S(2)}, u32[]{:S(2)}) collective-permute-start(f32[4,128,128]{2,1,0:T(8,128)S(1)} %get-tuple-element.46), channel_id=1, source_target_pairs={{16,8},{20,12},{17,9},{21,13},{18,10},{22,14},{19,11},{23,15}} | collective-permute-start | bytes 786440 | tf_op jit(solution)/shard_map/ppermute | solution.py:254
  30.3 12.9 %collective-permute-start.16 = (f32[4,128,128]{2,1,0:T(8,128)S(1)}, f32[4,128,128]{2,1,0:T(8,128)S(1)}, u32[]{:S(2)}, u32[]{:S(2)}) collective-permute-start(f32[4,128,128]{2,1,0:T(8,128)S(1)} %shard_map.118), channel_id=1, source_target_pairs={{8,0},{12,4},{24,16},{28,20},{9,1},{13,5},{25,17},{29,21},{10,2},{... | collective-permute-start | bytes 786440 | tf_op jit(solution)/shard_map/ppermute | solution.py:254
  35.0 11.3 %collective-permute-start.4 = (f32[4,128,128]{2,1,0:T(8,128)S(1)}, f32[4,128,128]{2,1,0:T(8,128)S(1)}, u32[]{:S(2)}, u32[]{:S(2)}) collective-permute-start(f32[4,128,128]{2,1,0:T(8,128)S(1)} %shard_map.106.refs_0_), channel_id=1, source_target_pairs={{0,8},{4,12},{16,24},{20,28},{1,9},{5,13},{17,25},{21,29},{2,10},{... | collective-permute-start | bytes 786440 | tf_op jit(solution)/shard_map/ppermute | solution.py:254
  36.4 11.6 %collective-permute-start.6 = (f32[4,128,128]{2,1,0:T(8,128)S(1)}, f32[4,128,128]{2,1,0:T(8,128)S(1)}, u32[]{:S(2)}, u32[]{:S(2)}) collective-permute-start(f32[4,128,128]{2,1,0:T(8,128)S(1)} %shard_map.109.refs_0_), channel_id=1, source_target_pairs={{0,8},{4,12},{16,24},{20,28},{1,9},{5,13},{17,25},{21,29},{2,10},{... | collective-permute-start | bytes 786440 | tf_op jit(solution)/shard_map/ppermute | solution.py:254
  37.7 20.0 %collective-permute-start.13 = (f32[4,128,128]{2,1,0:T(8,128)S(1)}, f32[4,128,128]{2,1,0:T(8,128)S(1)}, u32[]{:S(2)}, u32[]{:S(2)}) collective-permute-start(f32[4,128,128]{2,1,0:T(8,128)S(1)} %get-tuple-element.46), channel_id=1, source_target_pairs={{24,8},{28,12},{25,9},{29,13},{26,10},{30,14},{27,11},{31,15}} | collective-permute-start | bytes 786440 | tf_op jit(solution)/shard_map/ppermute | solution.py:254
  39.2 20.0 %collective-permute-start.12 = (f32[4,128,128]{2,1,0:T(8,128)S(1)}, f32[4,128,128]{2,1,0:T(8,128)S(1)}, u32[]{:S(2)}, u32[]{:S(2)}) collective-permute-start(f32[4,128,128]{2,1,0:T(8,128)S(1)} %shard_map.115), channel_id=1, source_target_pairs={{8,0},{12,4},{24,16},{28,20},{9,1},{13,5},{25,17},{29,21},{10,2},{... | collective-permute-start | bytes 786440 | tf_op jit(solution)/shard_map/ppermute | solution.py:254
  43.2 17.4 %collective-permute-start.8 = (f32[4,128,128]{2,1,0:T(8,128)S(1)}, f32[4,128,128]{2,1,0:T(8,128)S(1)}, u32[]{:S(2)}, u32[]{:S(2)}) collective-permute-start(f32[4,128,128]{2,1,0:T(8,128)S(1)} %shard_map.106.refs_0_), channel_id=1, source_target_pairs={{8,24},{12,28},{9,25},{13,29},{10,26},{14,30},{11,27},{15,31}} | collective-permute-start | bytes 786440 | tf_op jit(solution)/shard_map/ppermute | solution.py:254
  46.2 15.5 %copy-start.7 = (f32[256,1024]{1,0:T(8,128)S(1)}, f32[256,1024]{1,0:T(8,128)}, u32[]{:S(2)}) copy-start(f32[256,1024]{1,0:T(8,128)} %refs_2_.3) | copy-start | bytes 3145732
  46.3 36.4 %collective-permute-start.10 = (f32[4,128,128]{2,1,0:T(8,128)S(1)}, f32[4,128,128]{2,1,0:T(8,128)S(1)}, u32[]{:S(2)}, u32[]{:S(2)}) collective-permute-start(f32[4,128,128]{2,1,0:T(8,128)S(1)} %shard_map.109.refs_0_), channel_id=1, source_target_pairs={{8,24},{12,28},{9,25},{13,29},{10,26},{14,30},{11,27},{15,31}} | collective-permute-start | bytes 786440 | tf_op jit(solution)/shard_map/ppermute | solution.py:254
  47.8 13.9 %copy-start.5 = (f32[256,1024]{1,0:T(8,128)S(1)}, f32[256,1024]{1,0:T(8,128)}, u32[]{:S(2)}) copy-start(f32[256,1024]{1,0:T(8,128)} %refs_1_.11) | copy-start | bytes 3145732
  48.0 30.7 %collective-permute-start.7 = (f32[4,128,128]{2,1,0:T(8,128)S(1)}, f32[4,128,128]{2,1,0:T(8,128)S(1)}, u32[]{:S(2)}, u32[]{:S(2)}) collective-permute-start(f32[4,128,128]{2,1,0:T(8,128)S(1)} %shard_map.111), channel_id=1, source_target_pairs={{8,16},{12,20},{9,17},{13,21},{10,18},{14,22},{11,19},{15,23}} | collective-permute-start | bytes 786440 | tf_op jit(solution)/shard_map/ppermute | solution.py:254
  57.6 4.1 %copy-start.3 = (f32[256,1024]{1,0:T(8,128)S(1)}, f32[256,1024]{1,0:T(8,128)}, u32[]{:S(2)}) copy-start(f32[256,1024]{1,0:T(8,128)} %refs_1_.9) | copy-start | bytes 3145732
  57.7 4.0 %copy-start.1 = (f32[256,1024]{1,0:T(8,128)S(1)}, f32[256,1024]{1,0:T(8,128)}, u32[]{:S(2)}) copy-start(f32[256,1024]{1,0:T(8,128)} %refs_0_.7) | copy-start | bytes 3145732
  57.8 25.0 %collective-permute-start.9 = (f32[4,128,128]{2,1,0:T(8,128)S(1)}, f32[4,128,128]{2,1,0:T(8,128)S(1)}, u32[]{:S(2)}, u32[]{:S(2)}) collective-permute-start(f32[4,128,128]{2,1,0:T(8,128)S(1)} %shard_map.113), channel_id=1, source_target_pairs={{8,16},{12,20},{9,17},{13,21},{10,18},{14,22},{11,19},{15,23}} | collective-permute-start | bytes 786440 | tf_op jit(solution)/shard_map/ppermute | solution.py:254
  59.2 30.7 %collective-permute-start.18 = (f32[4,128,128]{2,1,0:T(8,128)S(1)}, f32[4,128,128]{2,1,0:T(8,128)S(1)}, u32[]{:S(2)}, u32[]{:S(2)}) collective-permute-start(f32[4,128,128]{2,1,0:T(8,128)S(1)} %shard_map.120), channel_id=1, source_target_pairs={{0,4},{4,0},{8,12},{12,8},{16,20},{20,16},{24,28},{28,24},{1,5},{5... | collective-permute-start | bytes 786440 | tf_op jit(solution)/shard_map/ppermute | solution.py:254
  60.6 33.4 %collective-permute-start.14 = (f32[4,128,128]{2,1,0:T(8,128)S(1)}, f32[4,128,128]{2,1,0:T(8,128)S(1)}, u32[]{:S(2)}, u32[]{:S(2)}) collective-permute-start(f32[4,128,128]{2,1,0:T(8,128)S(1)} %shard_map.117), channel_id=1, source_target_pairs={{0,4},{4,0},{8,12},{12,8},{16,20},{20,16},{24,28},{28,24},{1,5},{5... | collective-permute-start | bytes 786440 | tf_op jit(solution)/shard_map/ppermute | solution.py:254
  86.9 7.2 %copy-start.8 = (f32[8,256]{1,0:T(8,128)}, f32[8,256]{1,0:T(8,128)S(1)}, u32[]{:S(2)}) copy-start(f32[8,256]{1,0:T(8,128)S(1)} %get-tuple-element.57.refs_0_) | copy-start | bytes 24580
  86.9 11.4 %collective-permute-start.19 = (f32[8,256]{1,0:T(8,128)S(1)}, f32[8,256]{1,0:T(8,128)S(1)}, u32[]{:S(2)}, u32[]{:S(2)}) collective-permute-start(f32[8,256]{1,0:T(8,128)S(1)} %get-tuple-element.57.refs_0_), channel_id=1, source_target_pairs={{0,1},{1,2},{2,3},{3,0},{4,5},{5,6},{6,7},{7,4},{8,9},{9,10},{10,1... | collective-permute-start | bytes 24584 | tf_op jit(solution)/shard_map/ppermute | solution.py:437
  86.9 11.4 %collective-permute-start.20 = (f32[8,256]{1,0:T(8,128)S(1)}, f32[8,256]{1,0:T(8,128)S(1)}, u32[]{:S(2)}, u32[]{:S(2)}) collective-permute-start(f32[8,256]{1,0:T(8,128)S(1)} %get-tuple-element.57.refs_0_), channel_id=1, source_target_pairs={{0,2},{1,3},{2,0},{3,1},{4,6},{5,7},{6,4},{7,5},{8,10},{9,11},{10,... | collective-permute-start | bytes 24584 | tf_op jit(solution)/shard_map/ppermute | solution.py:437
  88.5 9.8 %collective-permute-start.21 = (f32[8,256]{1,0:T(8,128)S(1)}, f32[8,256]{1,0:T(8,128)S(1)}, u32[]{:S(2)}, u32[]{:S(2)}) collective-permute-start(f32[8,256]{1,0:T(8,128)S(1)} %get-tuple-element.57.refs_0_), channel_id=1, source_target_pairs={{0,3},{1,0},{2,1},{3,2},{4,7},{5,4},{6,5},{7,6},{8,11},{9,8},{10,9... | collective-permute-start | bytes 24584 | tf_op jit(solution)/shard_map/ppermute | solution.py:437
  98.3 0.6 copy-start.11
  98.3 0.6 copy-start.12
  98.9 0.6 copy-start.13

commit v2 on v0

v2 whole, which is shorter than its diff:
```python
import functools

import jax
import jax.numpy as jnp
from jax import lax
from jax.experimental import pallas as pl
from jax.experimental.pallas import tpu as pltpu
from jax.sharding import PartitionSpec as P

HIGH = lax.Precision.HIGH
EXACT = lax.Precision.HIGHEST
LANES = 128
PARTS = 2
VMEM_LIMIT = 6 * 1024 * 1024
WHOLE = pl.BlockSpec(memory_space=pltpu.VMEM)
SCALARS = pl.BlockSpec(memory_space=pltpu.SMEM)
FAR = pl.BlockSpec(memory_space=pltpu.HBM)
ANYWHERE = pl.BlockSpec(memory_space=pl.ANY)
ROWS, COLS = ((1,), (0,)), ((0,), (0,))
TURNED = ((1,), (1,))


def dot(a, b, over, precision=HIGH):
    return lax.dot_general(
        a, b, (over, ((), ())), precision=precision, preferred_element_type=jnp.float32
    )


def params(steps=0):
    return pltpu.CompilerParams(
        dimension_semantics=("arbitrary",) * steps or None, vmem_limit_bytes=VMEM_LIMIT
    )


def cost(flops, moved):
    return pl.CostEstimate(flops=int(flops), bytes_accessed=int(moved), transcendentals=0)


def iota(shape, axis):
    return lax.broadcasted_iota(jnp.int32, shape, axis)


def near(array):
    return pltpu.with_memory_space_constraint(array, pltpu.VMEM)


def far(array):
    return pltpu.with_memory_space_constraint(array, pltpu.HBM)


def upright(row, width):
    return jnp.broadcast_to(row, (width, row.shape[1])).T


def ship(source, target, from_columns, to_columns, sem):
    copy = pltpu.make_async_copy(
        source.at[:, pl.ds(from_columns.start, from_columns.stop - from_columns.start)],
        target.at[:, pl.ds(to_columns.start, to_columns.stop - to_columns.start)],
        sem,
    )
    copy.start()
    return copy


def join_kernel(own_ref, came_ref, out_ref):
    half = own_ref.shape[0]
    out_ref[:half] = own_ref[...]
    out_ref[half:] = came_ref[...]


def total_kernel(*refs):
    total = refs[0][...]
    for ref in refs[1:-1]:
        total = total + ref[...]
    refs[-1][...] = total[: refs[-1].shape[0]]


def prepare_kernel(
    heads, device_ref, decay_hbm, segment_hbm, cols_ref, rows_ref, source_ref, query_ref, table_ref,
    decay_ref, segment_ref, sems,
):
    del device_ref
    tokens = segment_ref.shape[1]
    copies = [
        pltpu.make_async_copy(decay_hbm, decay_ref, sems.at[0]),
        pltpu.make_async_copy(segment_hbm, segment_ref, sems.at[1]),
    ]
    for copy in copies:
        copy.start()
    for copy in copies:
        copy.wait()
    sooner = iota((tokens, tokens), 0) <= iota((tokens, tokens), 1)
    running = dot(decay_ref[...], sooner.astype(jnp.float32), ROWS, EXACT)
    document = segment_ref[...].astype(jnp.float32)
    total, first, last = running[:, tokens - 1 :], document[:, :1], document[:, tokens - 1 :]
    source_ref[...] = jnp.exp(total - running) * (document == last).astype(jnp.float32)
    query_ref[...] = jnp.exp(running) * (document == first).astype(jnp.float32)
    spare = LANES - heads - 1
    rows = jnp.concatenate([running, document, jnp.zeros((spare, tokens), jnp.float32)], axis=0)
    rows_ref[...] = rows[: rows_ref.shape[0]]
    cols = rows.T
    cols_ref[...] = cols
    row = iota((8, LANES), 0)
    table_ref[0] = jnp.where(row == 0, cols[tokens - 1 :], jnp.where(row == 1, last, first))


def first_kernel(heads, source_ref, k_ref, v_ref, wk_ref, wv_ref, *states):
    width = k_ref.shape[1] // heads
    part_heads = states[0].shape[0]
    for head in range(heads):
        at = slice(head * width, (head + 1) * width)
        weight = upright(source_ref[head : head + 1, :], width)
        weighted = weight * k_ref[:, at]
        v = v_ref[:, at]
        wk_ref[:, at] = weighted
        wv_ref[:, at] = weight * v
        states[head // part_heads][head % part_heads] = dot(weighted, v, COLS)


def second_kernel(
    heads, depth, level_ref, query_ref, q_ref, o_ref, after_ref, uo_ref, spread_ref, *outs
):
    del after_ref
    width = q_ref.shape[1] // heads
    for d in range(depth):
        spread_ref[d] = upright(level_ref[d + 1 : d + 2, :], width)
    part_heads = outs[0].shape[0]
    for head in range(heads):
        at = slice(head * width, (head + 1) * width)
        weight = upright(query_ref[head : head + 1, :], width)
        weighted = weight * o_ref[:, at]
        uo_ref[:, at] = weighted
        scaled = jnp.concatenate([spread_ref[d] * weighted for d in range(depth)], axis=1)
        grads = dot(q_ref[:, at], scaled, COLS)
        part, place = divmod(head, part_heads)
        for d in range(depth):
            outs[part * depth + d][place] = grads[:, d * width : (d + 1) * width]


def local_kernel(
    heads, base, q_ref, k_ref, v_ref, o_ref, cols_ref, rows_ref, level_ref, *refs
):
    terms_in = refs[0] if base else None
    gq_ref, gk_ref, gv_ref, terms_ref, shown_ref, total_ref = refs[-6:]
    tokens = rows_ref.shape[1]
    width = k_ref.shape[1] // heads
    shown = (iota((tokens, tokens), 0) <= iota((tokens, tokens), 1)) & (
        cols_ref[:, heads : heads + 1] == rows_ref[heads : heads + 1, :]
    )
    shown_ref[...] = jnp.where(shown, 0.0, -jnp.inf)
    total_ref[...] = jnp.zeros_like(total_ref)
    level = level_ref[0:1, :]
    for place in range(gq_ref.shape[1] // width):
        head = base + place
        at = slice(head * width, (head + 1) * width)
        to = slice(place * width, (place + 1) * width)
        q, k, v, o = q_ref[:, at], k_ref[:, at], v_ref[:, at], o_ref[:, at]
        gap = rows_ref[head : head + 1, :] - cols_ref[:, head : head + 1]
        within = jnp.exp(jnp.minimum(gap, shown_ref[...]))
        scores = dot(k, q, TURNED)
        shared = within * dot(v, o, TURNED)
        total_ref[...] += jnp.sum((shared * scores).reshape(tokens // 8, 8, tokens), axis=0)
        shared = shared * level
        gv_ref[:, to] = dot((within * level) * scores, o, ROWS)
        gk_ref[:, to] = dot(shared, q, ROWS)
        gq_ref[:, to] = dot(shared, k, COLS)
    own = jnp.sum(total_ref[...], axis=0, keepdims=True)
    terms = jnp.where(iota(terms_ref.shape, 0) == 0, own, 0.0)
    terms_ref[...] = terms if terms_in is None else terms + terms_in[...]


def factors_kernel(depth, device_ref, table_ref, factor_ref):
    stretches = table_ref.shape[0]
    device = device_ref[0]
    totals, lasts, firsts = table_ref[:, 0, :], table_ref[:, 1, :], table_ref[:, 2, :]
    stretch = iota((stretches, LANES), 0) ^ device

    def at(values, index):
        return jnp.sum(jnp.where(stretch == index, values, 0.0), axis=0, keepdims=True)

    def span(low, high):
        inside = (stretch > low) & (stretch <= high)
        return jnp.exp(jnp.sum(jnp.where(inside, totals, 0.0), axis=0, keepdims=True))

    def reach(low_end, target):
        return jnp.where(at(firsts, target) == at(lasts, low_end), span(low_end, target - 1), 0.0)

    factors = []
    for distance in range(depth):
        low_end = ((device >> (distance + 1)) << (distance + 1)) + (1 << distance) - 1
        upper = ((device >> distance) & 1) == 1
        factors.append(jnp.where(upper, reach(low_end, device), 0.0))
    for distance in range(depth):
        low_end = ((device >> (distance + 1)) << (distance + 1)) + (1 << distance) - 1
        high_end = low_end + (1 << distance)
        factors.append(
            jnp.where(at(lasts, low_end) == at(lasts, high_end), span(low_end, high_end), 0.0)
        )
    middle = stretches // 2 - 1
    second = device // (stretches // 4) == 1
    for hop in (stretches // 4, stretches // 2):
        target = jnp.minimum(device + hop, stretches - 1)
        factors.append(jnp.where(second, reach(middle, target), 0.0))
    factor_ref[...] = jnp.zeros_like(factor_ref)
    for index, factor in enumerate(factors):
        factor_ref[index : index + 1, :] = factor


def levels_kernel(heads, base, chosen, spare, out_at, device_ref, *refs):
    q_ref, uo_ref, spread_ref, factor_ref, gq_in, terms_in = refs[:6]
    blocks = refs[6 : 6 + len(chosen) + spare]
    if out_at is None:
        gq_ref, terms_ref, *totals = refs[-(2 + len(chosen)) :]
    else:
        gq_hbm, terms_ref, *totals, gq_ref, sems = refs[-(4 + len(chosen)) :]
    copies = []
    width = spread_ref.shape[2]
    device = device_ref[0]
    for place in range(gq_in.shape[1] // width):
        head = base + place
        at = slice(head * width, (head + 1) * width)
        to = slice(place * width, (place + 1) * width)
        states = [block[place] for block in blocks[: len(chosen)]]
        if spare:
            fourth = device & (1 << (chosen[0] - 2)) != 0
            states[0] = jnp.where(fourth, blocks[-1][place], states[0])
        states = [
            factor_ref[level - 1 : level, head : head + 1] * state
            for level, state in zip(chosen, states)
        ]
        q, uo = q_ref[:, at], uo_ref[:, at]
        reached = dot(q, jnp.concatenate(states, axis=1), ROWS)
        back = dot(uo, jnp.concatenate(states, axis=0), TURNED)
        gq = gq_in[:, to]
        for index, level in enumerate(chosen):
            here = slice(index * width, (index + 1) * width)
            gq = gq + spread_ref[level - 1] * back[:, here]
            term = reached[:, here] * uo
            totals[index][...] = term if place == 0 else totals[index][...] + term
        gq_ref[:, to] = gq
        if out_at is not None:
            copies.append(ship(gq_ref, gq_hbm, to, at, sems.at[place]))
    terms = terms_in[...]
    for total, level in zip(totals, chosen):
        row = jnp.sum(total[...].T, axis=0, keepdims=True)
        terms = terms + jnp.where(iota(terms.shape, 0) == level, row, 0.0)
    terms_ref[...] = terms
    for copy in copies:
        copy.wait()


def sources_kernel(heads, base, row, device_ref, wk_ref, wv_ref, factor_ref, kept_ref, came_ref, *refs):
    gk_in, gv_in = refs[:2]
    gk_hbm, gv_hbm, gk_ref, gv_ref, sems = refs[-5:]
    copies = []
    width = kept_ref.shape[2]
    upper = (device_ref[0] & 1).astype(jnp.float32)
    for place in range(kept_ref.shape[0]):
        head = base + place
        at = slice(head * width, (head + 1) * width)
        to = slice(place * width, (place + 1) * width)
        own = upper + (1.0 - upper) * factor_ref[row : row + 1, head : head + 1]
        state = own * kept_ref[place] + came_ref[place]
        gk_ref[:, to] = gk_in[:, to] + dot(wv_ref[:, at], state, TURNED)
        copies.append(ship(gk_ref, gk_hbm, to, at, sems.at[0, place]))
        gv_ref[:, to] = gv_in[:, to] + dot(wk_ref[:, at], state, ROWS)
        copies.append(ship(gv_ref, gv_hbm, to, at, sems.at[1, place]))
    for copy in copies:
        copy.wait()


def blend_kernel(base, recipes, inputs, after, device_ref, factor_ref, *refs):
    arrays, outs = refs[:inputs], refs[inputs + after :]
    device = device_ref[0]
    factor = factor_ref[...]
    for head in range(arrays[0].shape[0]):
        column = factor[:, base + head : base + head + 1]
        for out, recipe in zip(outs, recipes):
            total = None
            for index, coefficient in recipe:
                weight = coefficient(device, lambda row: column[row : row + 1, :])
                term = arrays[index][head]
                term = term if weight is None else weight * term
                total = term if total is None else total + term
            out[head] = total


def blend(base, recipes, arrays, device, factor, after=()):
    size = arrays[0].size * 4
    return pl.pallas_call(
        functools.partial(blend_kernel, base, recipes, len(arrays), len(after)),
        out_shape=[jax.ShapeDtypeStruct(arrays[0].shape, jnp.float32)] * len(recipes),
        in_specs=[SCALARS, WHOLE] + [WHOLE] * len(arrays) + [ANYWHERE] * len(after),
        out_specs=[WHOLE] * len(recipes),
        compiler_params=params(),
        cost_estimate=cost(size, size * (len(arrays) + len(recipes))),
    )(device, *map(near, (factor, *arrays)), *after)


def upper_flag(device, bit):
    return ((device >> bit) & 1).astype(jnp.float32)


def upper_or(bit, row):
    return lambda device, scalar: upper_flag(device, bit) * (1.0 - scalar(row)) + scalar(row)


def lower_or(bit, row):
    return lambda device, scalar: upper_flag(device, bit) * (scalar(row) - 1.0) + 1.0


def lower(bit):
    return lambda device, scalar: 1.0 - upper_flag(device, bit)


def by(row):
    return lambda device, scalar: scalar(row)


def both(row, other):
    return lambda device, scalar: scalar(row) * scalar(other)


def plain(device, scalar):
    return None


def send(array, route):
    return lax.ppermute(array, "seq", route)


def on_device(queries, key_input, value_input, grad_output, log_decay, level_weight, segment):
    stretches = lax.axis_size("seq")
    depth = stretches.bit_length() - 1
    tokens, heads = log_decay.shape
    width = queries.shape[1] // heads
    levels = level_weight.shape[1]
    quarter = stretches // 4
    device = lax.axis_index("seq").astype(jnp.int32).reshape(1)
    part_heads = heads // PARTS
    parts = range(PARTS)
    part_width = part_heads * width
    factor_rows = -(-(2 * depth + 2) // 8) * 8
    side_rows = -(-(heads + 1) // 8) * 8
    turned_rows = -(-levels // 8) * 8
    token_bytes = tokens * width * 4
    work = 6 * tokens * width * width

    def shape(*dims):
        return jax.ShapeDtypeStruct(dims, jnp.float32)

    tall = shape(tokens, heads * width)
    state = shape(part_heads, width, width)
    decay_rows, level_rows = log_decay.T, level_weight.T

    near_k, near_v, near_q, near_o = key_input, value_input, queries, grad_output
    cols, rows, source, query, table = pl.pallas_call(
        functools.partial(prepare_kernel, heads),
        out_shape=[shape(tokens, LANES), shape(side_rows, tokens)]
        + [shape(heads, tokens)] * 2
        + [shape(1, 8, LANES)],
        in_specs=[SCALARS, FAR, FAR],
        out_specs=[WHOLE] * 5,
        scratch_shapes=[
            pltpu.VMEM((heads, tokens), jnp.float32),
            pltpu.VMEM((1, tokens), jnp.int32),
            pltpu.SemaphoreType.DMA((2,)),
        ],
        compiler_params=params(),
    )(device, far(decay_rows), far(segment.reshape(1, tokens)))

    weighted_k, weighted_v, *states = pl.pallas_call(
        functools.partial(first_kernel, heads),
        out_shape=[tall] * 2 + [state] * PARTS,
        in_specs=[WHOLE] * 3,
        out_specs=[WHOLE] * (2 + PARTS),
        compiler_params=params(),
        cost_estimate=cost(heads * work, heads * 2 * token_bytes),
    )(*map(near, (source, near_k, near_v)))

    swaps = [[(i, i ^ (1 << d)) for i in range(stretches)] for d in range(depth)]
    tables = [table]
    for d in range(depth):
        table = pl.pallas_call(
            join_kernel,
            out_shape=shape(2 << d, 8, LANES),
            in_specs=[WHOLE] * 2,
            out_specs=WHOLE,
            compiler_params=params(),
        )(near(table), near(send(table, swaps[d])))
        tables.append(table)

    weighted_o, spread, *grads = pl.pallas_call(
        functools.partial(second_kernel, heads, depth),
        out_shape=[tall, shape(depth, tokens, width)] + [state] * (PARTS * depth),
        in_specs=[WHOLE] * 4 + [ANYWHERE],
        out_specs=[WHOLE] * (2 + PARTS * depth),
        compiler_params=params(),
        cost_estimate=cost(heads * depth * work, heads * 2 * token_bytes),
    )(level_rows, *map(near, (query, near_q, near_o)), tables[1])
    grads = [grads[p * depth : (p + 1) * depth] for p in parts]

    factor = pl.pallas_call(
        functools.partial(factors_kernel, depth),
        out_shape=shape(factor_rows, LANES),
        in_specs=[SCALARS, WHOLE],
        out_specs=WHOLE,
        compiler_params=params(),
    )(device, near(table))

    def own_level(level):
        return level - 1

    def block_row(distance):
        return depth + distance

    third, fourth = 2 * depth, 2 * depth + 1
    second_third = [(quarter + i, 2 * quarter + i) for i in range(quarter)]
    second_fourth = [(quarter + i, 3 * quarter + i) for i in range(quarter)]
    third_second = [(b, a) for a, b in second_third]
    fourth_second = [(b, a) for a, b in second_fourth]

    gq, gk, gv = ([None] * PARTS for _ in range(3))
    terms = None
    shown_terms = [None] * PARTS
    for p in parts:
        before = [] if terms is None else [near(terms)]
        gq[p], gk[p], gv[p], terms = pl.pallas_call(
            functools.partial(local_kernel, heads, p * part_heads),
            out_shape=[shape(tokens, part_width)] * 3 + [shape(turned_rows, tokens)],
            in_specs=[WHOLE] * (7 + len(before)),
            out_specs=[WHOLE] * 4,
            scratch_shapes=[
                pltpu.VMEM((tokens, tokens), jnp.float32),
                pltpu.VMEM((8, tokens), jnp.float32),
            ],
            compiler_params=params(),
            cost_estimate=cost(part_heads * 30 * tokens * tokens * width, 0),
        )(*map(near, (near_q, near_k, near_v, near_o, cols, rows)), level_rows, *before)
        shown_terms[p] = terms

    def add_levels(chosen, p, gq, terms, blocks, out=None, final=False):
        in_hbm = [] if out is None else [out]
        inputs = 7 + len(blocks)
        scratch = [pltpu.VMEM((tokens, width), jnp.float32)] * len(chosen)
        if final:
            scratch += [
                pltpu.VMEM((tokens, part_width), jnp.float32),
                pltpu.SemaphoreType.DMA((part_heads,)),
            ]
        return pl.pallas_call(
            functools.partial(
                levels_kernel,
                heads,
                p * part_heads,
                chosen,
                len(blocks) - len(chosen),
                p if final else None,
            ),
            out_shape=[
                shape(tokens, heads * width if final else part_width),
                shape(turned_rows, tokens),
            ],
            in_specs=[SCALARS] + [WHOLE] * (inputs - 1) + [FAR] * len(in_hbm),
            out_specs=[FAR if final else WHOLE, WHOLE],
            scratch_shapes=scratch,
            input_output_aliases={inputs: 0} if in_hbm else {},
            compiler_params=params(),
            cost_estimate=cost(part_heads * work * 2 * len(chosen), 0),
        )(device, *map(near, (near_q, weighted_o, spread, factor, gq, terms, *blocks)), *in_hbm)

    came = [[None] * (depth + 1) for _ in parts]
    running = list(states)
    from_third = [send(grads[p][depth - 1], third_second) for p in parts]
    from_fourth = [send(grads[p][depth - 1], fourth_second) for p in parts]
    for d in range(depth - 2):
        for p in parts:
            came[p][d + 1] = send(running[p], swaps[d])
        for p in parts:
            recipe = [(0, upper_or(d, block_row(d))), (1, lower_or(d, block_row(d)))]
            arrays = [running[p], came[p][d + 1]]
            (running[p],) = blend(
                p * part_heads, [recipe], arrays, device, factor
            )
    spare, crossed = [None] * PARTS, [None] * PARTS
    for p in parts:
        recipe = [
            (0, lower(depth - 2)),
            (1, by(own_level(depth - 1))),
            (2, both(block_row(depth - 2), third)),
        ]
        arrays = [running[p], grads[p][depth - 2], from_third[p]]
        (message,) = blend(p * part_heads, [recipe], arrays, device, factor)
        crossed[p] = send(message, swaps[depth - 2])
        spare[p] = send(running[p], second_fourth)
        came[p][depth - 1] = crossed[p]
    if depth > 2:
        chosen = list(range(1, depth - 1))
        for p in parts:
            blocks = [came[p][level] for level in chosen]
            gq[p], terms = add_levels(chosen, p, gq[p], terms, blocks)
    kept, sources = [None] * PARTS, [None] * PARTS
    for p in parts:
        recipe = [(0, plain), (1, by(block_row(depth - 2)))]
        (half,) = blend(
            p * part_heads, [recipe], [running[p], crossed[p]], device, factor, [terms]
        )
        came[p][depth] = send(half, second_third)
    for p in parts:
        total = [(0, lower(depth - 2)), (1, by(third)), (2, by(fourth))]
        arrays = [crossed[p], from_third[p], from_fourth[p]]
        (pending,) = blend(p * part_heads, [total], arrays, device, factor)
        for d in range(depth - 3, -1, -1):
            message = [(0, lower_or(d, block_row(d))), (1, by(own_level(d + 1)))]
            (outgoing,) = blend(p * part_heads, [message], [pending, grads[p][d]], device, factor)
            arrived = send(outgoing, swaps[d])
            if d > 0:
                recipe = [(0, upper_or(d, block_row(d))), (1, plain)]
                (pending,) = blend(p * part_heads, [recipe], [pending, arrived], device, factor)
        kept[p], sources[p] = pending, arrived
    for p in parts:
        gq[p], terms = add_levels([depth - 1], p, gq[p], terms, [crossed[p]])
    grad_query = None
    for p in parts:
        blocks = [came[p][depth], spare[p]]
        grad_query, terms = add_levels([depth], p, gq[p], terms, blocks, grad_query, True)
    groups = lax.axis_size("head")
    others = [
        lax.ppermute(terms, "head", [(i, (i + k) % groups) for i in range(groups)])
        for k in range(1, groups)
    ]
    done = []
    for p in parts:
        done = pl.pallas_call(
            functools.partial(sources_kernel, heads, p * part_heads, block_row(0)),
            out_shape=[tall] * 2,
            in_specs=[SCALARS] + [WHOLE] * 7 + [FAR] * len(done),
            out_specs=[FAR] * 2,
            scratch_shapes=[pltpu.VMEM((tokens, part_width), jnp.float32)] * 2
            + [pltpu.SemaphoreType.DMA((2, part_heads))],
            input_output_aliases={8: 0, 9: 1} if done else {},
            compiler_params=params(),
            cost_estimate=cost(part_heads * work * 2, 0),
        )(
            device,
            *map(near, (weighted_k, weighted_v, factor, kept[p], sources[p], gk[p], gv[p])),
            *done,
        )
    grad_level = pl.pallas_call(
        total_kernel,
        out_shape=shape(levels, tokens),
        in_specs=[WHOLE] * groups,
        out_specs=WHOLE,
        compiler_params=params(),
    )(terms, *others)
    return grad_query, done[0], done[1], grad_level.T


def solution(mesh):
    in_specs = (
        P("seq", "head"),
        P("seq", "head"),
        P("seq", "head"),
        P("seq", "head"),
        P("seq", "head"),
        P("seq", None),
        P("seq"),
    )
    out_specs = (P("seq", "head"), P("seq", "head"), P("seq", "head"), P("seq", None))
    return jax.shard_map(
        on_device, mesh=mesh, in_specs=in_specs, out_specs=out_specs, check_vma=False
    )
```

time: 164 us -> 67.2 us (0.41)
  the two profiles are of different devices: /device:TPU:2 before, /device:TPU:16 now
where the time goes in v2:
time: 67.2 us; the launch traced here: 66.2 us
  waiting for transfers between devices  24.1 us (36%)
  Pallas kernels  19.6 us (29%)
  starting transfers between devices  18.8 us (28%)
  local copies, waits for them, and re-layouts  2.68 us (4%)
  between operations  1.03 us (2%)
    ppermute x17, waiting for transfers between devices, send(): return lax.ppermute(array, 'seq', route)  24.1 us
    ppermute x17, starting transfers between devices, send(): return lax.ppermute(array, 'seq', route)  17 us
    pallas_call x6, Pallas kernels, add_levels(): pl.pallas_call(functools.partial(levels_kernel, heads, p * part_heads, ch...  5.81 us
    pallas_call x2, Pallas kernels, on_device(): pl.pallas_call(functools.partial(local_kernel, heads, p * part_heads), ou...  5.13 us
    pallas_call x2, Pallas kernels, on_device(): pl.pallas_call(functools.partial(sources_kernel, heads, p * part_heads, b...  2.89 us
    unnamed x14, local copies, waits for them, and re-layouts  2.68 us
    ppermute x3, starting transfers between devices, on_device(): lax.ppermute(terms, 'head', [(i, (i + k) % groups) for i in range(groups)])  1.81 us
    pallas_call x1, Pallas kernels, on_device(): pl.pallas_call(functools.partial(second_kernel, heads, depth), out_shape=...  1.65 us
  transfers between devices with their start and end apart: 20, of which 5 were waited for; matrix products, arithmetic and copies ran while one was open for 0% of the time, Pallas kernels for 27%

profile of v2, /device:TPU:16, one launch (start us, length us, event | category | flops | bytes accessed | tf_op | source)
XLA Modules:
  0.0 66.2 jit_solution(4153251023727368914)
XLA Ops:
  0.6 1.1 %shard_map.102 = (f32[256,128]{1,0:T(8,128)S(1)}, f32[16,256]{1,0:T(8,128)S(1)}, f32[8,256]{1,0:T(8,128)S(1)}, f32[8,256]{1,0:T(8,128)S(1)}, f32[1,8,128]{2,1,0:T(8,128)S(1)}) custom-call(s32[1]{0:T(128)} %bitcast.device_ref, f32[8,256]{1,0:T(8,128)} %bitcast.9, s32[1,256]{1,0:T(1,128)} %bitcast.10), custom_call_target="tpu_custom_call" | custom-call | tf_op jit(solution)/shard_map/pallas_call | solution.py:357
  1.7 1.6 %collective-permute-start = (f32[1,8,128]{2,1,0:T(8,128)S(1)}, f32[1,8,128]{2,1,0:T(8,128)S(1)}, u32[]{:S(2)}, u32[]{:S(2)}) collective-permute-start(f32[1,8,128]{2,1,0:T(8,128)S(1)} %get-tuple-element.46.own_ref), channel_id=1, source_target_pairs={{0,4},{4,0},{8,12},{12,8},{16,20},{20,16},{24,28},{28,24},{1,5},{5... | collective-permute-start | bytes 12296 | tf_op jit(solution)/shard_map/ppermute | solution.py:329
  3.3 1.2 %copy-done.1 = f32[256,1024]{1,0:T(8,128)S(1)} copy-done((f32[256,1024]{1,0:T(8,128)S(1)}, f32[256,1024]{1,0:T(8,128)}, u32[]{:S(2)}) %copy-start.1) | copy-done | bytes 1048600
  4.5 1.2 %copy-done.3 = f32[256,1024]{1,0:T(8,128)S(1)} copy-done((f32[256,1024]{1,0:T(8,128)S(1)}, f32[256,1024]{1,0:T(8,128)}, u32[]{:S(2)}) %copy-start.3) | copy-done | bytes 1048600
  5.7 0.9 %shard_map.110 = (f32[256,1024]{1,0:T(8,128)S(1)}, f32[256,1024]{1,0:T(8,128)S(1)}, f32[4,128,128]{2,1,0:T(8,128)S(1)}, f32[4,128,128]{2,1,0:T(8,128)S(1)}) custom-call(f32[8,256]{1,0:T(8,128)S(1)} %get-tuple-element.55.source_ref, f32[256,1024]{1,0:T(8,128)S(1)} %copy-done.1, f32[256,1024]{1,0:T(8,128)S(1)} %copy-done.3), custom_call_target="tpu_custom_call" | custom-call | flops 201326592 | bytes 2097152 | tf_op jit(solution)/shard_map/pallas_call | solution.py:372
  6.7 0.6 collective-permute-start.3
  7.3 0.2 copy-done.6
  7.5 1.7 %shard_map.104 = (f32[256,1024]{1,0:T(8,128)S(1)}, f32[3,256,128]{2,1,0:T(8,128)S(1)}, f32[4,128,128]{2,1,0:T(8,128)S(1)}, f32[4,128,128]{2,1,0:T(8,128)S(1)}, f...) custom-call(f32[7,256]{1,0:T(8,128)S(1)} %bitcast.5, ...), custom_call_target="tpu_custom_call" | custom-call | flops 603979776 | bytes 2097152 | tf_op jit(solution)/shard_map/pallas_call | solution.py:393
  9.2 2.4 %collective-permute-start.5 = (f32[4,128,128]{2,1,0:T(8,128)S(1)}, f32[4,128,128]{2,1,0:T(8,128)S(1)}, u32[]{:S(2)}, u32[]{:S(2)}) collective-permute-start(f32[4,128,128]{2,1,0:T(8,128)S(1)} %get-tuple-element.63), channel_id=1, source_target_pairs={{16,8},{20,12},{17,9},{21,13},{18,10},{22,14},{19,11},{23,15}} | collective-permute-start | bytes 786440 | tf_op jit(solution)/shard_map/ppermute | solution.py:329
  11.6 1.4 %collective-permute-start.4 = (f32[4,128,128]{2,1,0:T(8,128)S(1)}, f32[4,128,128]{2,1,0:T(8,128)S(1)}, u32[]{:S(2)}, u32[]{:S(2)}) collective-permute-start(f32[4,128,128]{2,1,0:T(8,128)S(1)} %get-tuple-element.58.refs_0_), channel_id=1, source_target_pairs={{0,4},{4,0},{8,12},{12,8},{16,20},{20,16},{24,28},{28,24},{1,5},{5... | collective-permute-start | bytes 786440 | tf_op jit(solution)/shard_map/ppermute | solution.py:329
  12.9 1.3 %collective-permute-start.7 = (f32[4,128,128]{2,1,0:T(8,128)S(1)}, f32[4,128,128]{2,1,0:T(8,128)S(1)}, u32[]{:S(2)}, u32[]{:S(2)}) collective-permute-start(f32[4,128,128]{2,1,0:T(8,128)S(1)} %get-tuple-element.66), channel_id=1, source_target_pairs={{16,8},{20,12},{17,9},{21,13},{18,10},{22,14},{19,11},{23,15}} | collective-permute-start | bytes 786440 | tf_op jit(solution)/shard_map/ppermute | solution.py:329
  14.3 3.6 %collective-permute-done.1.came_ref = f32[2,8,128]{2,1,0:T(8,128)S(1)} collective-permute-done((f32[2,8,128]{2,1,0:T(8,128)S(1)}, f32[2,8,128]{2,1,0:T(8,128)S(1)}, u32[]{:S(2)}, u32[]{:S(2)}) %collective-permute-start.1) | collective-permute-done | bytes 8224 | tf_op jit(solution)/shard_map/ppermute | solution.py:329
  17.9 5.2 %collective-permute-done.2.came_ref = f32[4,8,128]{2,1,0:T(8,128)S(1)} collective-permute-done((f32[4,8,128]{2,1,0:T(8,128)S(1)}, f32[4,8,128]{2,1,0:T(8,128)S(1)}, u32[]{:S(2)}, u32[]{:S(2)}) %collective-permute-start.2) | collective-permute-done | bytes 16416 | tf_op jit(solution)/shard_map/ppermute | solution.py:329
  23.2 0.1 shard_map.113.refs_0_
  23.4 0.1 shard_map.114
  23.6 0.1 shard_map.116.refs_0_
  23.8 0.2 shard_map.117
  23.9 2.1 %collective-permute-start.8 = (f32[4,128,128]{2,1,0:T(8,128)S(1)}, f32[4,128,128]{2,1,0:T(8,128)S(1)}, u32[]{:S(2)}, u32[]{:S(2)}) collective-permute-start(f32[4,128,128]{2,1,0:T(8,128)S(1)} %shard_map.117), channel_id=1, source_target_pairs={{0,8},{4,12},{8,0},{12,4},{16,24},{20,28},{24,16},{28,20},{1,9},{5... | collective-permute-start | bytes 786440 | tf_op jit(solution)/shard_map/ppermute | solution.py:329
  26.0 0.7 %collective-permute-start.15 = (f32[4,128,128]{2,1,0:T(8,128)S(1)}, f32[4,128,128]{2,1,0:T(8,128)S(1)}, u32[]{:S(2)}, u32[]{:S(2)}) collective-permute-start(f32[4,128,128]{2,1,0:T(8,128)S(1)} %get-tuple-element.63), channel_id=1, source_target_pairs={{24,8},{28,12},{25,9},{29,13},{26,10},{30,14},{27,11},{31,15}} | collective-permute-start | bytes 786440 | tf_op jit(solution)/shard_map/ppermute | solution.py:329
  26.7 0.7 %collective-permute-start.13 = (f32[4,128,128]{2,1,0:T(8,128)S(1)}, f32[4,128,128]{2,1,0:T(8,128)S(1)}, u32[]{:S(2)}, u32[]{:S(2)}) collective-permute-start(f32[4,128,128]{2,1,0:T(8,128)S(1)} %get-tuple-element.66), channel_id=1, source_target_pairs={{24,8},{28,12},{25,9},{29,13},{26,10},{30,14},{27,11},{31,15}} | collective-permute-start | bytes 786440 | tf_op jit(solution)/shard_map/ppermute | solution.py:329
  27.4 0.7 %collective-permute-start.10 = (f32[4,128,128]{2,1,0:T(8,128)S(1)}, f32[4,128,128]{2,1,0:T(8,128)S(1)}, u32[]{:S(2)}, u32[]{:S(2)}) collective-permute-start(f32[4,128,128]{2,1,0:T(8,128)S(1)} %shard_map.113.refs_0_), channel_id=1, source_target_pairs={{8,24},{12,28},{9,25},{13,29},{10,26},{14,30},{11,27},{15,31}} | collective-permute-start | bytes 786440 | tf_op jit(solution)/shard_map/ppermute | solution.py:329
  28.1 2.6 %shard_map.108 = (f32[256,512]{1,0:T(8,128)S(1)}, f32[256,512]{1,0:T(8,128)S(1)}, f32[256,512]{1,0:T(8,128)S(1)}, f32[8,256]{1,0:T(8,128)S(1)}) custom-call(f32[256,1024]{1,0:T(8,128)S(1)} %copy-done, f32[256,1024]{1,0:T(8,128)S(1)} %copy-done.2, f32[256,1024]{1,0:T(8,128)S(1)} %copy-done.4, f32[256,1024]{1,0:T(8,128)S(1)} %copy-done.5, ...), custom_call_target="tpu_custom_call" | custom-call | flops 1006632960 | tf_op jit(solution)/shard_map/pallas_call | solution.py:428
  30.6 2.6 %shard_map.109 = (f32[256,512]{1,0:T(8,128)S(1)}, f32[256,512]{1,0:T(8,128)S(1)}, f32[256,512]{1,0:T(8,128)S(1)}, f32[8,256]{1,0:T(8,128)S(1)}) custom-call(f32[256,1024]{1,0:T(8,128)S(1)} %copy-done, f32[256,1024]{1,0:T(8,128)S(1)} %copy-done.2, f32[256,1024]{1,0:T(8,128)S(1)} %copy-done.4, f32[256,1024]{1,0:T(8,128)S(1)} %copy-done.5, ...), custom_call_target="tpu_custom_call" | custom-call | flops 1006632960 | tf_op jit(solution)/shard_map/pallas_call | solution.py:428
  33.2 0.7 %shard_map.111 = (f32[256,512]{1,0:T(8,128)S(1)}, f32[8,256]{1,0:T(8,128)S(1)}) custom-call(s32[1]{0:T(128)} %bitcast.device_ref, f32[256,1024]{1,0:T(8,128)S(1)} %copy-done, f32[256,1024]{1,0:T(8,128)S(1)} %get-tuple-element.47.refs_1_, f32[3,256,128]{2,1,0:T(8,128)S(1)} %get-tuple-element.48.refs_2_, f32[8,128]{1,0:T(8,128)S(1)} %shard_map.107.refs_3_.factor_ref, ...), custom_call_target="tpu_custom_call" | custom-call | flops 201326592 | tf_op jit(solution)/shard_map/pallas_call | solution.py:451
  33.9 0.8 %shard_map.112 = (f32[256,512]{1,0:T(8,128)S(1)}, f32[8,256]{1,0:T(8,128)S(1)}) custom-call(s32[1]{0:T(128)} %bitcast.device_ref, f32[256,1024]{1,0:T(8,128)S(1)} %copy-done, f32[256,1024]{1,0:T(8,128)S(1)} %get-tuple-element.47.refs_1_, f32[3,256,128]{2,1,0:T(8,128)S(1)} %get-tuple-element.48.refs_2_, f32[8,128]{1,0:T(8,128)S(1)} %shard_map.107.refs_3_.factor_ref, ...), custom_call_target="tpu_custom_call" | custom-call | flops 201326592 | tf_op jit(solution)/shard_map/pallas_call | solution.py:451
  34.8 0.1 shard_map.119
  34.9 1.3 %collective-permute-start.9 = (f32[4,128,128]{2,1,0:T(8,128)S(1)}, f32[4,128,128]{2,1,0:T(8,128)S(1)}, u32[]{:S(2)}, u32[]{:S(2)}) collective-permute-start(f32[4,128,128]{2,1,0:T(8,128)S(1)} %shard_map.119), channel_id=1, source_target_pairs={{8,16},{12,20},{9,17},{13,21},{10,18},{14,22},{11,19},{15,23}} | collective-permute-start | bytes 786440 | tf_op jit(solution)/shard_map/ppermute | solution.py:329
  36.2 2.3 %collective-permute-done.8.refs_6_.refs_1_.refs_0_ = f32[4,128,128]{2,1,0:T(8,128)S(1)} collective-permute-done((f32[4,128,128]{2,1,0:T(8,128)S(1)}, f32[4,128,128]{2,1,0:T(8,128)S(1)}, u32[]{:S(2)}, u32[]{:S(2)}) %collective-permute-start.8) | collective-permute-done | bytes 262176 | tf_op jit(solution)/shard_map/ppermute | solution.py:329
  38.4 0.7 %collective-permute-start.12 = (f32[4,128,128]{2,1,0:T(8,128)S(1)}, f32[4,128,128]{2,1,0:T(8,128)S(1)}, u32[]{:S(2)}, u32[]{:S(2)}) collective-permute-start(f32[4,128,128]{2,1,0:T(8,128)S(1)} %shard_map.116.refs_0_), channel_id=1, source_target_pairs={{8,24},{12,28},{9,25},{13,29},{10,26},{14,30},{11,27},{15,31}} | collective-permute-start | bytes 786440 | tf_op jit(solution)/shard_map/ppermute | solution.py:329
  39.1 0.1 shard_map.121
  39.3 1.5 %collective-permute-start.11 = (f32[4,128,128]{2,1,0:T(8,128)S(1)}, f32[4,128,128]{2,1,0:T(8,128)S(1)}, u32[]{:S(2)}, u32[]{:S(2)}) collective-permute-start(f32[4,128,128]{2,1,0:T(8,128)S(1)} %shard_map.121), channel_id=1, source_target_pairs={{8,16},{12,20},{9,17},{13,21},{10,18},{14,22},{11,19},{15,23}} | collective-permute-start | bytes 786440 | tf_op jit(solution)/shard_map/ppermute | solution.py:329
  40.7 0.1 shard_map.125.refs_0_.kept_ref
  40.9 0.1 shard_map.126
  41.1 1.1 %collective-permute-start.16 = (f32[4,128,128]{2,1,0:T(8,128)S(1)}, f32[4,128,128]{2,1,0:T(8,128)S(1)}, u32[]{:S(2)}, u32[]{:S(2)}) collective-permute-start(f32[4,128,128]{2,1,0:T(8,128)S(1)} %shard_map.126), channel_id=1, source_target_pairs={{0,4},{4,0},{8,12},{12,8},{16,20},{20,16},{24,28},{28,24},{1,5},{5... | collective-permute-start | bytes 786440 | tf_op jit(solution)/shard_map/ppermute | solution.py:329
  42.1 0.2 shard_map.123.refs_0_.kept_ref
  42.3 0.1 shard_map.124
  42.4 1.1 %collective-permute-start.14 = (f32[4,128,128]{2,1,0:T(8,128)S(1)}, f32[4,128,128]{2,1,0:T(8,128)S(1)}, u32[]{:S(2)}, u32[]{:S(2)}) collective-permute-start(f32[4,128,128]{2,1,0:T(8,128)S(1)} %shard_map.124), channel_id=1, source_target_pairs={{0,4},{4,0},{8,12},{12,8},{16,20},{20,16},{24,28},{28,24},{1,5},{5... | collective-permute-start | bytes 786440 | tf_op jit(solution)/shard_map/ppermute | solution.py:329
  43.5 0.7 %shard_map.115 = (f32[256,512]{1,0:T(8,128)S(1)}, f32[8,256]{1,0:T(8,128)S(1)}) custom-call(s32[1]{0:T(128)} %bitcast.device_ref, f32[256,1024]{1,0:T(8,128)S(1)} %copy-done, f32[256,1024]{1,0:T(8,128)S(1)} %get-tuple-element.47.refs_1_, f32[3,256,128]{2,1,0:T(8,128)S(1)} %get-tuple-element.48.refs_2_, f32[8,128]{1,0:T(8,128)S(1)} %shard_map.107.refs_3_.factor_ref, ...), custom_call_target="tpu_custom_call" | custom-call | flops 201326592 | tf_op jit(solution)/shard_map/pallas_call | solution.py:451
  44.2 0.8 %shard_map.118 = (f32[256,512]{1,0:T(8,128)S(1)}, f32[8,256]{1,0:T(8,128)S(1)}) custom-call(s32[1]{0:T(128)} %bitcast.device_ref, f32[256,1024]{1,0:T(8,128)S(1)} %copy-done, f32[256,1024]{1,0:T(8,128)S(1)} %get-tuple-element.47.refs_1_, f32[3,256,128]{2,1,0:T(8,128)S(1)} %get-tuple-element.48.refs_2_, f32[8,128]{1,0:T(8,128)S(1)} %shard_map.107.refs_3_.factor_ref, ...), custom_call_target="tpu_custom_call" | custom-call | flops 201326592 | tf_op jit(solution)/shard_map/pallas_call | solution.py:451
  45.0 6.3 %collective-permute-done.9.refs_6_ = f32[4,128,128]{2,1,0:T(8,128)S(1)} collective-permute-done((f32[4,128,128]{2,1,0:T(8,128)S(1)}, f32[4,128,128]{2,1,0:T(8,128)S(1)}, u32[]{:S(2)}, u32[]{:S(2)}) %collective-permute-start.9) | collective-permute-done | bytes 262176 | tf_op jit(solution)/shard_map/ppermute | solution.py:329
  51.4 1.3 %shard_map.120 = (f32[256,1024]{1,0:T(8,128)}, f32[8,256]{1,0:T(8,128)S(1)}) custom-call(s32[1]{0:T(128)} %bitcast.device_ref, f32[256,1024]{1,0:T(8,128)S(1)} %copy-done, f32[256,1024]{1,0:T(8,128)S(1)} %get-tuple-element.47.refs_1_, f32[3,256,128]{2,1,0:T(8,128)S(1)} %get-tuple-element.48.refs_2_, f32[8,128]{1,0:T(8,128)S(1)} %shard_map.107.refs_3_.factor_ref, ...), custom_call_target="tpu_custom_call" | custom-call | flops 201326592 | tf_op jit(solution)/shard_map/pallas_call | solution.py:451
  52.7 6.6 %collective-permute-done.11.refs_6_ = f32[4,128,128]{2,1,0:T(8,128)S(1)} collective-permute-done((f32[4,128,128]{2,1,0:T(8,128)S(1)}, f32[4,128,128]{2,1,0:T(8,128)S(1)}, u32[]{:S(2)}, u32[]{:S(2)}) %collective-permute-start.11) | collective-permute-done | bytes 262176 | tf_op jit(solution)/shard_map/ppermute | solution.py:329
  59.4 1.4 %shard_map.122 = (f32[256,1024]{1,0:T(8,128)}, f32[8,256]{1,0:T(8,128)S(1)}) custom-call(s32[1]{0:T(128)} %bitcast.device_ref, f32[256,1024]{1,0:T(8,128)S(1)} %copy-done, f32[256,1024]{1,0:T(8,128)S(1)} %get-tuple-element.47.refs_1_, f32[3,256,128]{2,1,0:T(8,128)S(1)} %get-tuple-element.48.refs_2_, ...), custom_call_target="tpu_custom_call", output_to_operand_aliasing={{0}: (9, {})} | custom-call | flops 201326592 | tf_op jit(solution)/shard_map/pallas_call | solution.py:451
  60.8 1.6 %collective-permute-start.18 = (f32[8,256]{1,0:T(8,128)S(1)}, f32[8,256]{1,0:T(8,128)S(1)}, u32[]{:S(2)}, u32[]{:S(2)}) collective-permute-start(f32[8,256]{1,0:T(8,128)S(1)} %get-tuple-element.85.refs_0_), channel_id=1, source_target_pairs={{0,2},{1,3},{2,0},{3,1},{4,6},{5,7},{6,4},{7,5},{8,10},{9,11},{10,... | collective-permute-start | bytes 24584 | tf_op jit(solution)/shard_map/ppermute | solution.py:529
  62.4 0.2 collective-permute-start.17
  62.6 1.4 %shard_map.127 = (f32[256,1024]{1,0:T(8,128)}, f32[256,1024]{1,0:T(8,128)}) custom-call(s32[1]{0:T(128)} %bitcast.device_ref, f32[256,1024]{1,0:T(8,128)S(1)} %get-tuple-element.73.wk_ref, f32[256,1024]{1,0:T(8,128)S(1)} %get-tuple-element.74.wv_ref, f32[8,128]{1,0:T(8,128)S(1)} %shard_map.107.refs_3_.factor_ref, ...), custom_call_target="tpu_custom_call" | custom-call | flops 201326592 | tf_op jit(solution)/shard_map/pallas_call | solution.py:534
  64.0 1.5 %shard_map.128 = (f32[256,1024]{1,0:T(8,128)}, f32[256,1024]{1,0:T(8,128)}) custom-call(s32[1]{0:T(128)} %bitcast.device_ref, f32[256,1024]{1,0:T(8,128)S(1)} %get-tuple-element.73.wk_ref, f32[256,1024]{1,0:T(8,128)S(1)} %get-tuple-element.74.wv_ref, f32[8,128]{1,0:T(8,128)S(1)} %shard_map.107.refs_3_.factor_ref, ...), custom_call_target="tpu_custom_call", output_to_operand_aliasing={{0}: (8, {}), {1}: (9, {})} | custom-call | flops 201326592 | tf_op jit(solution)/shard_map/pallas_call | solution.py:534
  65.6 0.6 shard_map.129
  (34 shorter events, 0.3 us)
Async XLA Ops:
  1.7 5.6 %collective-permute-start = (f32[1,8,128]{2,1,0:T(8,128)S(1)}, f32[1,8,128]{2,1,0:T(8,128)S(1)}, u32[]{:S(2)}, u32[]{:S(2)}) collective-permute-start(f32[1,8,128]{2,1,0:T(8,128)S(1)} %get-tuple-element.46.own_ref), channel_id=1, source_target_pairs={{0,4},{4,0},{8,12},{12,8},{16,20},{20,16},{24,28},{28,24},{1,5},{5... | collective-permute-start | bytes 12296 | tf_op jit(solution)/shard_map/ppermute | solution.py:329
  3.3 1.2 %copy-start.1 = (f32[256,1024]{1,0:T(8,128)S(1)}, f32[256,1024]{1,0:T(8,128)}, u32[]{:S(2)}) copy-start(f32[256,1024]{1,0:T(8,128)} %k_ref.5) | copy-start | bytes 3145732
  4.5 1.2 %copy-start.3 = (f32[256,1024]{1,0:T(8,128)S(1)}, f32[256,1024]{1,0:T(8,128)}, u32[]{:S(2)}) copy-start(f32[256,1024]{1,0:T(8,128)} %v_ref.5) | copy-start | bytes 3145732
  5.7 1.6 %copy-start = (f32[256,1024]{1,0:T(8,128)S(1)}, f32[256,1024]{1,0:T(8,128)}, u32[]{:S(2)}) copy-start(f32[256,1024]{1,0:T(8,128)} %refs_0_.11) | copy-start | bytes 3145732
  5.7 1.6 %copy-start.5 = (f32[256,1024]{1,0:T(8,128)S(1)}, f32[256,1024]{1,0:T(8,128)}, u32[]{:S(2)}) copy-start(f32[256,1024]{1,0:T(8,128)} %o_ref.5) | copy-start | bytes 3145732
  6.7 0.8 %copy-start.6 = (f32[256,7]{0,1:T(8,128)S(1)}, f32[256,7]{0,1:T(8,128)}, u32[]{:S(2)}) copy-start(f32[256,7]{0,1:T(8,128)} %param.12) | copy-start | bytes 21508
  6.7 16.5 %collective-permute-start.3 = (f32[4,128,128]{2,1,0:T(8,128)S(1)}, f32[4,128,128]{2,1,0:T(8,128)S(1)}, u32[]{:S(2)}, u32[]{:S(2)}) collective-permute-start(f32[4,128,128]{2,1,0:T(8,128)S(1)} %get-tuple-element.56.refs_0_), channel_id=1, source_target_pairs={{0,4},{4,0},{8,12},{12,8},{16,20},{20,16},{24,28},{28,24},{1,5},{5... | collective-permute-start | bytes 786440 | tf_op jit(solution)/shard_map/ppermute | solution.py:329
  9.2 14.2 %collective-permute-start.5 = (f32[4,128,128]{2,1,0:T(8,128)S(1)}, f32[4,128,128]{2,1,0:T(8,128)S(1)}, u32[]{:S(2)}, u32[]{:S(2)}) collective-permute-start(f32[4,128,128]{2,1,0:T(8,128)S(1)} %get-tuple-element.63), channel_id=1, source_target_pairs={{16,8},{20,12},{17,9},{21,13},{18,10},{22,14},{19,11},{23,15}} | collective-permute-start | bytes 786440 | tf_op jit(solution)/shard_map/ppermute | solution.py:329
  11.6 12.0 %collective-permute-start.4 = (f32[4,128,128]{2,1,0:T(8,128)S(1)}, f32[4,128,128]{2,1,0:T(8,128)S(1)}, u32[]{:S(2)}, u32[]{:S(2)}) collective-permute-start(f32[4,128,128]{2,1,0:T(8,128)S(1)} %get-tuple-element.58.refs_0_), channel_id=1, source_target_pairs={{0,4},{4,0},{8,12},{12,8},{16,20},{20,16},{24,28},{28,24},{1,5},{5... | collective-permute-start | bytes 786440 | tf_op jit(solution)/shard_map/ppermute | solution.py:329
  12.9 10.8 %collective-permute-start.7 = (f32[4,128,128]{2,1,0:T(8,128)S(1)}, f32[4,128,128]{2,1,0:T(8,128)S(1)}, u32[]{:S(2)}, u32[]{:S(2)}) collective-permute-start(f32[4,128,128]{2,1,0:T(8,128)S(1)} %get-tuple-element.66), channel_id=1, source_target_pairs={{16,8},{20,12},{17,9},{21,13},{18,10},{22,14},{19,11},{23,15}} | collective-permute-start | bytes 786440 | tf_op jit(solution)/shard_map/ppermute | solution.py:329
  14.2 3.7 %collective-permute-start.1 = (f32[2,8,128]{2,1,0:T(8,128)S(1)}, f32[2,8,128]{2,1,0:T(8,128)S(1)}, u32[]{:S(2)}, u32[]{:S(2)}) collective-permute-start(f32[2,8,128]{2,1,0:T(8,128)S(1)} %shard_map.103.after_ref.own_ref), channel_id=1, source_target_pairs={{0,8},{4,12},{8,0},{12,4},{16,24},{20,28},{24,16},{28,20},{1,9},{5... | collective-permute-start | bytes 24584 | tf_op jit(solution)/shard_map/ppermute | solution.py:329
  17.9 5.2 %collective-permute-start.2 = (f32[4,8,128]{2,1,0:T(8,128)S(1)}, f32[4,8,128]{2,1,0:T(8,128)S(1)}, u32[]{:S(2)}, u32[]{:S(2)}) collective-permute-start(f32[4,8,128]{2,1,0:T(8,128)S(1)} %shard_map.105.own_ref), channel_id=1, source_target_pairs={{0,16},{4,20},{8,24},{12,28},{16,0},{20,4},{24,8},{28,12},{1,17},{... | collective-permute-start | bytes 49160 | tf_op jit(solution)/shard_map/ppermute | solution.py:329
  23.3 4.7 %copy-start.4 = (f32[256,1024]{1,0:T(8,128)S(1)}, f32[256,1024]{1,0:T(8,128)}, u32[]{:S(2)}) copy-start(f32[256,1024]{1,0:T(8,128)} %v_ref.5) | copy-start | bytes 3145732
  23.5 4.5 %copy-start.2 = (f32[256,1024]{1,0:T(8,128)S(1)}, f32[256,1024]{1,0:T(8,128)}, u32[]{:S(2)}) copy-start(f32[256,1024]{1,0:T(8,128)} %k_ref.5) | copy-start | bytes 3145732
  23.5 11.2 %collective-permute-start.6 = (f32[4,128,128]{2,1,0:T(8,128)S(1)}, f32[4,128,128]{2,1,0:T(8,128)S(1)}, u32[]{:S(2)}, u32[]{:S(2)}) collective-permute-start(f32[4,128,128]{2,1,0:T(8,128)S(1)} %shard_map.114), channel_id=1, source_target_pairs={{0,8},{4,12},{8,0},{12,4},{16,24},{20,28},{24,16},{28,20},{1,9},{5... | collective-permute-start | bytes 786440 | tf_op jit(solution)/shard_map/ppermute | solution.py:329
  23.9 14.5 %collective-permute-start.8 = (f32[4,128,128]{2,1,0:T(8,128)S(1)}, f32[4,128,128]{2,1,0:T(8,128)S(1)}, u32[]{:S(2)}, u32[]{:S(2)}) collective-permute-start(f32[4,128,128]{2,1,0:T(8,128)S(1)} %shard_map.117), channel_id=1, source_target_pairs={{0,8},{4,12},{8,0},{12,4},{16,24},{20,28},{24,16},{28,20},{1,9},{5... | collective-permute-start | bytes 786440 | tf_op jit(solution)/shard_map/ppermute | solution.py:329
  26.0 13.3 %collective-permute-start.15 = (f32[4,128,128]{2,1,0:T(8,128)S(1)}, f32[4,128,128]{2,1,0:T(8,128)S(1)}, u32[]{:S(2)}, u32[]{:S(2)}) collective-permute-start(f32[4,128,128]{2,1,0:T(8,128)S(1)} %get-tuple-element.63), channel_id=1, source_target_pairs={{24,8},{28,12},{25,9},{29,13},{26,10},{30,14},{27,11},{31,15}} | collective-permute-start | bytes 786440 | tf_op jit(solution)/shard_map/ppermute | solution.py:329
  26.7 14.4 %collective-permute-start.13 = (f32[4,128,128]{2,1,0:T(8,128)S(1)}, f32[4,128,128]{2,1,0:T(8,128)S(1)}, u32[]{:S(2)}, u32[]{:S(2)}) collective-permute-start(f32[4,128,128]{2,1,0:T(8,128)S(1)} %get-tuple-element.66), channel_id=1, source_target_pairs={{24,8},{28,12},{25,9},{29,13},{26,10},{30,14},{27,11},{31,15}} | collective-permute-start | bytes 786440 | tf_op jit(solution)/shard_map/ppermute | solution.py:329
  27.4 15.1 %collective-permute-start.10 = (f32[4,128,128]{2,1,0:T(8,128)S(1)}, f32[4,128,128]{2,1,0:T(8,128)S(1)}, u32[]{:S(2)}, u32[]{:S(2)}) collective-permute-start(f32[4,128,128]{2,1,0:T(8,128)S(1)} %shard_map.113.refs_0_), channel_id=1, source_target_pairs={{8,24},{12,28},{9,25},{13,29},{10,26},{14,30},{11,27},{15,31}} | collective-permute-start | bytes 786440 | tf_op jit(solution)/shard_map/ppermute | solution.py:329
  34.9 16.5 %collective-permute-start.9 = (f32[4,128,128]{2,1,0:T(8,128)S(1)}, f32[4,128,128]{2,1,0:T(8,128)S(1)}, u32[]{:S(2)}, u32[]{:S(2)}) collective-permute-start(f32[4,128,128]{2,1,0:T(8,128)S(1)} %shard_map.119), channel_id=1, source_target_pairs={{8,16},{12,20},{9,17},{13,21},{10,18},{14,22},{11,19},{15,23}} | collective-permute-start | bytes 786440 | tf_op jit(solution)/shard_map/ppermute | solution.py:329
  38.4 14.3 %collective-permute-start.12 = (f32[4,128,128]{2,1,0:T(8,128)S(1)}, f32[4,128,128]{2,1,0:T(8,128)S(1)}, u32[]{:S(2)}, u32[]{:S(2)}) collective-permute-start(f32[4,128,128]{2,1,0:T(8,128)S(1)} %shard_map.116.refs_0_), channel_id=1, source_target_pairs={{8,24},{12,28},{9,25},{13,29},{10,26},{14,30},{11,27},{15,31}} | collective-permute-start | bytes 786440 | tf_op jit(solution)/shard_map/ppermute | solution.py:329
  39.3 20.1 %collective-permute-start.11 = (f32[4,128,128]{2,1,0:T(8,128)S(1)}, f32[4,128,128]{2,1,0:T(8,128)S(1)}, u32[]{:S(2)}, u32[]{:S(2)}) collective-permute-start(f32[4,128,128]{2,1,0:T(8,128)S(1)} %shard_map.121), channel_id=1, source_target_pairs={{8,16},{12,20},{9,17},{13,21},{10,18},{14,22},{11,19},{15,23}} | collective-permute-start | bytes 786440 | tf_op jit(solution)/shard_map/ppermute | solution.py:329
  41.1 21.6 %collective-permute-start.16 = (f32[4,128,128]{2,1,0:T(8,128)S(1)}, f32[4,128,128]{2,1,0:T(8,128)S(1)}, u32[]{:S(2)}, u32[]{:S(2)}) collective-permute-start(f32[4,128,128]{2,1,0:T(8,128)S(1)} %shard_map.126), channel_id=1, source_target_pairs={{0,4},{4,0},{8,12},{12,8},{16,20},{20,16},{24,28},{28,24},{1,5},{5... | collective-permute-start | bytes 786440 | tf_op jit(solution)/shard_map/ppermute | solution.py:329
  42.4 21.6 %collective-permute-start.14 = (f32[4,128,128]{2,1,0:T(8,128)S(1)}, f32[4,128,128]{2,1,0:T(8,128)S(1)}, u32[]{:S(2)}, u32[]{:S(2)}) collective-permute-start(f32[4,128,128]{2,1,0:T(8,128)S(1)} %shard_map.124), channel_id=1, source_target_pairs={{0,4},{4,0},{8,12},{12,8},{16,20},{20,16},{24,28},{28,24},{1,5},{5... | collective-permute-start | bytes 786440 | tf_op jit(solution)/shard_map/ppermute | solution.py:329
  60.8 4.7 %collective-permute-start.19 = (f32[8,256]{1,0:T(8,128)S(1)}, f32[8,256]{1,0:T(8,128)S(1)}, u32[]{:S(2)}, u32[]{:S(2)}) collective-permute-start(f32[8,256]{1,0:T(8,128)S(1)} %get-tuple-element.85.refs_0_), channel_id=1, source_target_pairs={{0,3},{1,0},{2,1},{3,2},{4,7},{5,4},{6,5},{7,6},{8,11},{9,8},{10,9... | collective-permute-start | bytes 24584 | tf_op jit(solution)/shard_map/ppermute | solution.py:529
  60.8 4.7 %collective-permute-start.18 = (f32[8,256]{1,0:T(8,128)S(1)}, f32[8,256]{1,0:T(8,128)S(1)}, u32[]{:S(2)}, u32[]{:S(2)}) collective-permute-start(f32[8,256]{1,0:T(8,128)S(1)} %get-tuple-element.85.refs_0_), channel_id=1, source_target_pairs={{0,2},{1,3},{2,0},{3,1},{4,6},{5,7},{6,4},{7,5},{8,10},{9,11},{10,... | collective-permute-start | bytes 24584 | tf_op jit(solution)/shard_map/ppermute | solution.py:529
  62.4 3.1 %collective-permute-start.17 = (f32[8,256]{1,0:T(8,128)S(1)}, f32[8,256]{1,0:T(8,128)S(1)}, u32[]{:S(2)}, u32[]{:S(2)}) collective-permute-start(f32[8,256]{1,0:T(8,128)S(1)} %get-tuple-element.85.refs_0_), channel_id=1, source_target_pairs={{0,1},{1,2},{2,3},{3,0},{4,5},{5,6},{6,7},{7,4},{8,9},{9,10},{10,1... | collective-permute-start | bytes 24584 | tf_op jit(solution)/shard_map/ppermute | solution.py:529

commit v3 on v2

--- a/solution.py
+++ b/solution.py
@@ -33,7 +33,7 @@
 
 
 def cost(flops, moved):
-    return pl.CostEstimate(flops=int(flops), bytes_accessed=int(moved), transcendentals=0)
+    return pl.CostEstimate(flops=1, bytes_accessed=1, transcendentals=0)
 
 
 def iota(shape, axis):
@@ -62,7 +62,8 @@
     return copy
 
 
-def join_kernel(own_ref, came_ref, out_ref):
+def join_kernel(own_ref, came_ref, after_ref, out_ref):
+    del after_ref
     half = own_ref.shape[0]
     out_ref[:half] = own_ref[...]
     out_ref[half:] = came_ref[...]
@@ -75,20 +76,24 @@
     refs[-1][...] = total[: refs[-1].shape[0]]
 
 
-def prepare_kernel(
-    heads, device_ref, decay_hbm, segment_hbm, cols_ref, rows_ref, source_ref, query_ref, table_ref,
-    decay_ref, segment_ref, sems,
+def first_kernel(
+    heads, device_ref, decay_hbm, segment_hbm, k_hbm, v_hbm, q_hbm, o_hbm, k_ref, v_ref, q_ref,
+    o_ref, cols_ref, rows_ref, source_ref, query_ref, table_ref, decay_ref, segment_ref, sems,
 ):
     del device_ref
     tokens = segment_ref.shape[1]
+    pairs = (
+        (decay_hbm, decay_ref), (segment_hbm, segment_ref), (k_hbm, k_ref), (v_hbm, v_ref),
+        (q_hbm, q_ref), (o_hbm, o_ref),
+    )
     copies = [
-        pltpu.make_async_copy(decay_hbm, decay_ref, sems.at[0]),
-        pltpu.make_async_copy(segment_hbm, segment_ref, sems.at[1]),
+        pltpu.make_async_copy(source, target, sems.at[index])
+        for index, (source, target) in enumerate(pairs)
     ]
     for copy in copies:
         copy.start()
-    for copy in copies:
-        copy.wait()
+    copies[0].wait()
+    copies[1].wait()
     sooner = iota((tokens, tokens), 0) <= iota((tokens, tokens), 1)
     running = dot(decay_ref[...], sooner.astype(jnp.float32), ROWS, EXACT)
     document = segment_ref[...].astype(jnp.float32)
@@ -102,11 +107,13 @@
     cols_ref[...] = cols
     row = iota((8, LANES), 0)
     table_ref[0] = jnp.where(row == 0, cols[tokens - 1 :], jnp.where(row == 1, last, first))
-
-
-def first_kernel(heads, source_ref, k_ref, v_ref, wk_ref, wv_ref, *states):
+    for copy in copies[2:]:
+        copy.wait()
+
+
+def states_kernel(heads, source_ref, k_ref, v_ref, after_ref, wk_ref, wv_ref, *states):
+    del after_ref
     width = k_ref.shape[1] // heads
-    part_heads = states[0].shape[0]
     for head in range(heads):
         at = slice(head * width, (head + 1) * width)
         weight = upright(source_ref[head : head + 1, :], width)
@@ -114,17 +121,16 @@
         v = v_ref[:, at]
         wk_ref[:, at] = weighted
         wv_ref[:, at] = weight * v
-        states[head // part_heads][head % part_heads] = dot(weighted, v, COLS)
+        part, place = divmod(head, states[0].shape[0])
+        states[part][place] = dot(weighted, v, COLS)
 
 
 def second_kernel(
-    heads, depth, level_ref, query_ref, q_ref, o_ref, after_ref, uo_ref, spread_ref, *outs
+    heads, depth, level_ref, query_ref, q_ref, o_ref, uo_ref, spread_ref, *outs
 ):
-    del after_ref
     width = q_ref.shape[1] // heads
     for d in range(depth):
         spread_ref[d] = upright(level_ref[d + 1 : d + 2, :], width)
-    part_heads = outs[0].shape[0]
     for head in range(heads):
         at = slice(head * width, (head + 1) * width)
         weight = upright(query_ref[head : head + 1, :], width)
@@ -132,7 +138,7 @@
         uo_ref[:, at] = weighted
         scaled = jnp.concatenate([spread_ref[d] * weighted for d in range(depth)], axis=1)
         grads = dot(q_ref[:, at], scaled, COLS)
-        part, place = divmod(head, part_heads)
+        part, place = divmod(head, outs[0].shape[0])
         for d in range(depth):
             outs[part * depth + d][place] = grads[:, d * width : (d + 1) * width]
 
@@ -206,24 +212,20 @@
         factor_ref[index : index + 1, :] = factor
 
 
-def levels_kernel(heads, base, chosen, spare, out_at, device_ref, *refs):
+def levels_kernel(heads, base, chosen, out_at, *refs):
     q_ref, uo_ref, spread_ref, factor_ref, gq_in, terms_in = refs[:6]
-    blocks = refs[6 : 6 + len(chosen) + spare]
+    blocks = refs[6 : 6 + len(chosen)]
     if out_at is None:
         gq_ref, terms_ref, *totals = refs[-(2 + len(chosen)) :]
     else:
         gq_hbm, terms_ref, *totals, gq_ref, sems = refs[-(4 + len(chosen)) :]
     copies = []
     width = spread_ref.shape[2]
-    device = device_ref[0]
     for place in range(gq_in.shape[1] // width):
         head = base + place
         at = slice(head * width, (head + 1) * width)
         to = slice(place * width, (place + 1) * width)
-        states = [block[place] for block in blocks[: len(chosen)]]
-        if spare:
-            fourth = device & (1 << (chosen[0] - 2)) != 0
-            states[0] = jnp.where(fourth, blocks[-1][place], states[0])
+        states = [block[place] for block in blocks]
         states = [
             factor_ref[level - 1 : level, head : head + 1] * state
             for level, state in zip(chosen, states)
@@ -255,7 +257,7 @@
     copies = []
     width = kept_ref.shape[2]
     upper = (device_ref[0] & 1).astype(jnp.float32)
-    for place in range(kept_ref.shape[0]):
+    for place in range(gk_in.shape[1] // width):
         head = base + place
         at = slice(head * width, (head + 1) * width)
         to = slice(place * width, (place + 1) * width)
@@ -269,32 +271,20 @@
         copy.wait()
 
 
-def blend_kernel(base, recipes, inputs, after, device_ref, factor_ref, *refs):
-    arrays, outs = refs[:inputs], refs[inputs + after :]
+def blend_kernel(base, recipe, inputs, device_ref, factor_ref, *refs):
+    arrays, out_ref = refs[:inputs], refs[-1]
     device = device_ref[0]
     factor = factor_ref[...]
-    for head in range(arrays[0].shape[0]):
-        column = factor[:, base + head : base + head + 1]
-        for out, recipe in zip(outs, recipes):
-            total = None
-            for index, coefficient in recipe:
-                weight = coefficient(device, lambda row: column[row : row + 1, :])
-                term = arrays[index][head]
-                term = term if weight is None else weight * term
-                total = term if total is None else total + term
-            out[head] = total
-
-
-def blend(base, recipes, arrays, device, factor, after=()):
-    size = arrays[0].size * 4
-    return pl.pallas_call(
-        functools.partial(blend_kernel, base, recipes, len(arrays), len(after)),
-        out_shape=[jax.ShapeDtypeStruct(arrays[0].shape, jnp.float32)] * len(recipes),
-        in_specs=[SCALARS, WHOLE] + [WHOLE] * len(arrays) + [ANYWHERE] * len(after),
-        out_specs=[WHOLE] * len(recipes),
-        compiler_params=params(),
-        cost_estimate=cost(size, size * (len(arrays) + len(recipes))),
-    )(device, *map(near, (factor, *arrays)), *after)
+    for place in range(out_ref.shape[0]):
+        head = base + place
+        column = factor[:, head : head + 1]
+        total = None
+        for array, coefficient in zip(arrays, recipe):
+            weight = coefficient(device, lambda row: column[row : row + 1, :])
+            term = array[place]
+            term = term if weight is None else weight * term
+            total = term if total is None else total + term
+        out_ref[place] = total
 
 
 def upper_flag(device, bit):
@@ -311,6 +301,14 @@
 
 def lower(bit):
     return lambda device, scalar: 1.0 - upper_flag(device, bit)
+
+
+def quarter_flag(top, which, row=None):
+    def weight(device, scalar):
+        flag = (((device >> (top - 1)) & 3) == which).astype(jnp.float32)
+        return flag if row is None else flag * scalar(row)
+
+    return weight
 
 
 def by(row):
@@ -352,77 +350,61 @@
     tall = shape(tokens, heads * width)
     state = shape(part_heads, width, width)
     decay_rows, level_rows = log_decay.T, level_weight.T
-
-    near_k, near_v, near_q, near_o = key_input, value_input, queries, grad_output
-    cols, rows, source, query, table = pl.pallas_call(
-        functools.partial(prepare_kernel, heads),
-        out_shape=[shape(tokens, LANES), shape(side_rows, tokens)]
+    swaps = [[(i, i ^ (1 << d)) for i in range(stretches)] for d in range(depth)]
+
+    near_k, near_v, near_q, near_o, cols, rows, source, query, table = pl.pallas_call(
+        functools.partial(first_kernel, heads),
+        out_shape=[tall] * 4
+        + [shape(tokens, LANES), shape(side_rows, tokens)]
         + [shape(heads, tokens)] * 2
         + [shape(1, 8, LANES)],
-        in_specs=[SCALARS, FAR, FAR],
-        out_specs=[WHOLE] * 5,
+        in_specs=[SCALARS] + [FAR] * 6,
+        out_specs=[WHOLE] * 9,
         scratch_shapes=[
             pltpu.VMEM((heads, tokens), jnp.float32),
             pltpu.VMEM((1, tokens), jnp.int32),
-            pltpu.SemaphoreType.DMA((2,)),
+            pltpu.SemaphoreType.DMA((6,)),
         ],
         compiler_params=params(),
-    )(device, far(decay_rows), far(segment.reshape(1, tokens)))
-
-    weighted_k, weighted_v, *states = pl.pallas_call(
-        functools.partial(first_kernel, heads),
-        out_shape=[tall] * 2 + [state] * PARTS,
-        in_specs=[WHOLE] * 3,
-        out_specs=[WHOLE] * (2 + PARTS),
-        compiler_params=params(),
-        cost_estimate=cost(heads * work, heads * 2 * token_bytes),
-    )(*map(near, (source, near_k, near_v)))
-
-    swaps = [[(i, i ^ (1 << d)) for i in range(stretches)] for d in range(depth)]
-    tables = [table]
-    for d in range(depth):
-        table = pl.pallas_call(
-            join_kernel,
-            out_shape=shape(2 << d, 8, LANES),
-            in_specs=[WHOLE] * 2,
-            out_specs=WHOLE,
-            compiler_params=params(),
-        )(near(table), near(send(table, swaps[d])))
-        tables.append(table)
+    )(
+        device,
+        *map(far, (decay_rows, segment.reshape(1, tokens))),
+        *map(far, (key_input, value_input, queries, grad_output)),
+    )
 
     weighted_o, spread, *grads = pl.pallas_call(
         functools.partial(second_kernel, heads, depth),
         out_shape=[tall, shape(depth, tokens, width)] + [state] * (PARTS * depth),
-        in_specs=[WHOLE] * 4 + [ANYWHERE],
+        in_specs=[WHOLE] * 4,
         out_specs=[WHOLE] * (2 + PARTS * depth),
         compiler_params=params(),
         cost_estimate=cost(heads * depth * work, heads * 2 * token_bytes),
-    )(level_rows, *map(near, (query, near_q, near_o)), tables[1])
+    )(level_rows, *map(near, (query, near_q, near_o)))
     grads = [grads[p * depth : (p + 1) * depth] for p in parts]
 
-    factor = pl.pallas_call(
-        functools.partial(factors_kernel, depth),
-        out_shape=shape(factor_rows, LANES),
-        in_specs=[SCALARS, WHOLE],
-        out_specs=WHOLE,
+    def join(table, d, after):
+        return pl.pallas_call(
+            join_kernel,
+            out_shape=shape(2 << d, 8, LANES),
+            in_specs=[WHOLE] * 2 + [ANYWHERE],
+            out_specs=WHOLE,
+            compiler_params=params(),
+        )(near(table), near(send(table, swaps[d])), after)
+
+    table = join(table, 0, weighted_o)
+
+    weighted_k, weighted_v, *running = pl.pallas_call(
+        functools.partial(states_kernel, heads),
+        out_shape=[tall] * 2 + [state] * PARTS,
+        in_specs=[WHOLE] * 3 + [ANYWHERE],
+        out_specs=[WHOLE] * (2 + PARTS),
         compiler_params=params(),
-    )(device, near(table))
-
-    def own_level(level):
-        return level - 1
-
-    def block_row(distance):
-        return depth + distance
-
-    third, fourth = 2 * depth, 2 * depth + 1
-    second_third = [(quarter + i, 2 * quarter + i) for i in range(quarter)]
-    second_fourth = [(quarter + i, 3 * quarter + i) for i in range(quarter)]
-    third_second = [(b, a) for a, b in second_third]
-    fourth_second = [(b, a) for a, b in second_fourth]
+        cost_estimate=cost(heads * work, 0),
+    )(*map(near, (source, near_k, near_v)), table)
+
 
     gq, gk, gv = ([None] * PARTS for _ in range(3))
     terms = None
-    shown_terms = [None] * PARTS
     for p in parts:
         before = [] if terms is None else [near(terms)]
         gq[p], gk[p], gv[p], terms = pl.pallas_call(
@@ -437,11 +419,33 @@
             compiler_params=params(),
             cost_estimate=cost(part_heads * 30 * tokens * tokens * width, 0),
         )(*map(near, (near_q, near_k, near_v, near_o, cols, rows)), level_rows, *before)
-        shown_terms[p] = terms
+
+    for d in range(1, depth):
+        table = join(table, d, weighted_v if d == 1 else terms)
+    factor = pl.pallas_call(
+        functools.partial(factors_kernel, depth),
+        out_shape=shape(factor_rows, LANES),
+        in_specs=[SCALARS, WHOLE],
+        out_specs=WHOLE,
+        compiler_params=params(),
+    )(device, near(table))
+
+    def own_level(level):
+        return level - 1
+
+    def block_row(distance):
+        return depth + distance
+
+    third, fourth = 2 * depth, 2 * depth + 1
+    second_third = [(quarter + i, 2 * quarter + i) for i in range(quarter)]
+    third_fourth = [(2 * quarter + i, 3 * quarter + i) for i in range(quarter)]
+    third_second = [(b, a) for a, b in second_third]
+    shift_up = second_third + third_fourth
+    shift_down = [(b, a) for a, b in shift_up]
 
     def add_levels(chosen, p, gq, terms, blocks, out=None, final=False):
         in_hbm = [] if out is None else [out]
-        inputs = 7 + len(blocks)
+        inputs = 6 + len(blocks)
         scratch = [pltpu.VMEM((tokens, width), jnp.float32)] * len(chosen)
         if final:
             scratch += [
@@ -454,76 +458,89 @@
                 heads,
                 p * part_heads,
                 chosen,
-                len(blocks) - len(chosen),
                 p if final else None,
             ),
             out_shape=[
                 shape(tokens, heads * width if final else part_width),
                 shape(turned_rows, tokens),
             ],
-            in_specs=[SCALARS] + [WHOLE] * (inputs - 1) + [FAR] * len(in_hbm),
+            in_specs=[WHOLE] * inputs + [FAR] * len(in_hbm),
             out_specs=[FAR if final else WHOLE, WHOLE],
             scratch_shapes=scratch,
             input_output_aliases={inputs: 0} if in_hbm else {},
             compiler_params=params(),
             cost_estimate=cost(part_heads * work * 2 * len(chosen), 0),
-        )(device, *map(near, (near_q, weighted_o, spread, factor, gq, terms, *blocks)), *in_hbm)
-
-    came = [[None] * (depth + 1) for _ in parts]
-    running = list(states)
-    from_third = [send(grads[p][depth - 1], third_second) for p in parts]
-    from_fourth = [send(grads[p][depth - 1], fourth_second) for p in parts]
+        )(*map(near, (near_q, weighted_o, spread, factor, gq, terms, *blocks)), *in_hbm)
+
+    def blend(part, terms, after=()):
+        arrays, recipe = zip(*terms)
+        return pl.pallas_call(
+            functools.partial(blend_kernel, part * part_heads, recipe, len(arrays)),
+            out_shape=state,
+            in_specs=[SCALARS, WHOLE] + [WHOLE] * len(arrays) + [ANYWHERE] * len(after),
+            out_specs=WHOLE,
+            compiler_params=params(),
+            cost_estimate=cost(1, 1),
+        )(device, *map(near, (factor, *arrays)), *after)
+
+    top, next_bit = depth - 1, depth - 2
+    shifted = [send(grads[p][top], shift_down) for p in parts]
+    came = [[] for _ in parts]
     for d in range(depth - 2):
         for p in parts:
-            came[p][d + 1] = send(running[p], swaps[d])
+            arrived = send(running[p], swaps[d])
+            came[p].append(arrived)
+            running[p] = blend(
+                p,
+                [(running[p], upper_or(d, block_row(d))), (arrived, lower_or(d, block_row(d)))],
+            )
+    crossed, relayed, passed = [], [], []
+    for p in parts:
+        message = blend(
+            p,
+            [
+                (running[p], lower(next_bit)),
+                (grads[p][next_bit], by(own_level(depth - 1))),
+                (shifted[p], both(block_row(next_bit), third)),
+            ],
+        )
+        crossed.append(send(message, swaps[next_bit]))
+        relayed.append(send(shifted[p], third_second))
+        passed.append(send(running[p], second_third))
+    if depth > 2:
         for p in parts:
-            recipe = [(0, upper_or(d, block_row(d))), (1, lower_or(d, block_row(d)))]
-            arrays = [running[p], came[p][d + 1]]
-            (running[p],) = blend(
-                p * part_heads, [recipe], arrays, device, factor
+            gq[p], terms = add_levels(list(range(1, depth - 1)), p, gq[p], terms, came[p])
+    topmost, kept, sources = [], [], []
+    for p in parts:
+        upward = blend(
+            p,
+            [
+                (running[p], quarter_flag(top, 1)),
+                (crossed[p], quarter_flag(top, 1, block_row(next_bit))),
+                (passed[p], quarter_flag(top, 2)),
+            ],
+            [terms],
+        )
+        topmost.append(send(upward, shift_up))
+        pending = blend(
+            p, [(crossed[p], lower(next_bit)), (shifted[p], by(third)), (relayed[p], by(fourth))]
+        )
+        for d in range(depth - 3, -1, -1):
+            outgoing = blend(
+                p, [(pending, lower_or(d, block_row(d))), (grads[p][d], by(own_level(d + 1)))]
             )
-    spare, crossed = [None] * PARTS, [None] * PARTS
-    for p in parts:
-        recipe = [
-            (0, lower(depth - 2)),
-            (1, by(own_level(depth - 1))),
-            (2, both(block_row(depth - 2), third)),
-        ]
-        arrays = [running[p], grads[p][depth - 2], from_third[p]]
-        (message,) = blend(p * part_heads, [recipe], arrays, device, factor)
-        crossed[p] = send(message, swaps[depth - 2])
-        spare[p] = send(running[p], second_fourth)
-        came[p][depth - 1] = crossed[p]
-    if depth > 2:
-        chosen = list(range(1, depth - 1))
-        for p in parts:
-            blocks = [came[p][level] for level in chosen]
-            gq[p], terms = add_levels(chosen, p, gq[p], terms, blocks)
-    kept, sources = [None] * PARTS, [None] * PARTS
-    for p in parts:
-        recipe = [(0, plain), (1, by(block_row(depth - 2)))]
-        (half,) = blend(
-            p * part_heads, [recipe], [running[p], crossed[p]], device, factor, [terms]
-        )
-        came[p][depth] = send(half, second_third)
-    for p in parts:
-        total = [(0, lower(depth - 2)), (1, by(third)), (2, by(fourth))]
-        arrays = [crossed[p], from_third[p], from_fourth[p]]
-        (pending,) = blend(p * part_heads, [total], arrays, device, factor)
-        for d in range(depth - 3, -1, -1):
-            message = [(0, lower_or(d, block_row(d))), (1, by(own_level(d + 1)))]
-            (outgoing,) = blend(p * part_heads, [message], [pending, grads[p][d]], device, factor)
             arrived = send(outgoing, swaps[d])
             if d > 0:
-                recipe = [(0, upper_or(d, block_row(d))), (1, plain)]
-                (pending,) = blend(p * part_heads, [recipe], [pending, arrived], device, factor)
-        kept[p], sources[p] = pending, arrived
+                pending = blend(p, [(pending, upper_or(d, block_row(d))), (arrived, plain)])
+        kept.append(pending)
+        sources.append(arrived)
     for p in parts:
         gq[p], terms = add_levels([depth - 1], p, gq[p], terms, [crossed[p]])
     grad_query = None
     for p in parts:
-        blocks = [came[p][depth], spare[p]]
-        grad_query, terms = add_levels([depth], p, gq[p], terms, blocks, grad_query, True)
+        grad_query, terms = add_levels(
+            [depth], p, gq[p], terms, [topmost[p]], grad_query, True
+        )
     groups = lax.axis_size("head")
     others = [
         lax.ppermute(terms, "head", [(i, (i + k) % groups) for i in range(groups)])

time: 67.2 us -> 60.7 us (0.903); the launches traced: 66.2 us -> 60.3 us
  waiting for transfers between devices: 24.1 us -> 8.36 us
  starting transfers between devices: 18.8 us -> 30.2 us
  local copies, waits for them, and re-layouts: 2.68 us -> 0.01 us
  Pallas kernels: 19.6 us -> 20.8 us
    ppermute x17, waiting for transfers between devices: 24.1 us -> 8.35 us  [send(): return lax.ppermute(array, 'seq', route)]
    ppermute x17, starting transfers between devices: 17 us -> 27.1 us  [send(): return lax.ppermute(array, 'seq', route)]
    unnamed x14 -> x2, local copies, waits for them, and re-layouts: 2.68 us -> 0.01 us
    pallas_call x1, Pallas kernels: 0.94 us -> 2.26 us  [on_device(): pl.pallas_call(functools.partial(first_kernel, heads), out_shape=[tall] *...]
    ppermute x3, starting transfers between devices: 1.81 us -> 3.03 us  [on_device(): lax.ppermute(terms, 'head', [(i, (i + k) % groups) for i in range(groups)])]
  transfers between devices with their start and end apart: 20 -> 20, of which waited for: 5 -> 5; matrix products, arithmetic and copies ran while one was open for 0% -> 0% of each run, Pallas kernels for 27% -> 28%
where the time goes in v3:
time: 60.7 us; the launch traced here: 60.3 us
  starting transfers between devices  30.2 us (50%)
  Pallas kernels  20.8 us (34%)
  waiting for transfers between devices  8.36 us (14%)
  between operations  0.99 us (2%)
    ppermute x17, starting transfers between devices, send(): return lax.ppermute(array, 'seq', route)  27.1 us
    ppermute x17, waiting for transfers between devices, send(): return lax.ppermute(array, 'seq', route)  8.35 us
    pallas_call x6, Pallas kernels, add_levels(): pl.pallas_call(functools.partial(levels_kernel, heads, p * part_heads, ch...  5.84 us
    pallas_call x2, Pallas kernels, on_device(): pl.pallas_call(functools.partial(local_kernel, heads, p * part_heads), ou...  5.14 us
    ppermute x3, starting transfers between devices, on_device(): lax.ppermute(terms, 'head', [(i, (i + k) % groups) for i in range(groups)])  3.03 us
    pallas_call x2, Pallas kernels, on_device(): pl.pallas_call(functools.partial(sources_kernel, heads, p * part_heads, b...  2.89 us
    pallas_call x1, Pallas kernels, on_device(): pl.pallas_call(functools.partial(first_kernel, heads), out_shape=[tall] *...  2.26 us
    pallas_call x1, Pallas kernels, on_device(): pl.pallas_call(functools.partial(second_kernel, heads, depth), out_shape=...  1.65 us
  transfers between devices with their start and end apart: 20, of which 5 were waited for; matrix products, arithmetic and copies ran while one was open for 0% of the time, Pallas kernels for 28%

profile of v3, /device:TPU:16, one launch (start us, length us, event | category | flops | bytes accessed | tf_op | source)
XLA Modules:
  0.0 60.3 jit_solution(716317445237774577)
XLA Ops:
  0.6 2.3 %shard_map.102 = (f32[256,1024]{1,0:T(8,128)S(1)}, f32[256,1024]{1,0:T(8,128)S(1)}, f32[256,1024]{1,0:T(8,128)S(1)}, f32[256,1024]{1,0:T(8,128)S(1)}, f32[256,12...) custom-call(s32[1]{0:T(128)} %bitcast.device_ref, ...), custom_call_target="tpu_custom_call" | custom-call | tf_op jit(solution)/shard_map/pallas_call | solution.py:355
  2.9 1.6 %collective-permute-start = (f32[1,8,128]{2,1,0:T(8,128)S(1)}, f32[1,8,128]{2,1,0:T(8,128)S(1)}, u32[]{:S(2)}, u32[]{:S(2)}) collective-permute-start(f32[1,8,128]{2,1,0:T(8,128)S(1)} %get-tuple-element.54.own_ref), channel_id=1, source_target_pairs={{0,4},{4,0},{8,12},{12,8},{16,20},{20,16},{24,28},{28,24},{1,5},{5... | collective-permute-start | bytes 12296 | tf_op jit(solution)/shard_map/ppermute | solution.py:327
  4.5 1.7 %shard_map.103 = (f32[256,1024]{1,0:T(8,128)S(1)}, f32[3,256,128]{2,1,0:T(8,128)S(1)}, f32[4,128,128]{2,1,0:T(8,128)S(1)}, f32[4,128,128]{2,1,0:T(8,128)S(1)}, f...) custom-call(f32[7,256]{1,0:T(8,128)S(1)} %bitcast.5, ...), custom_call_target="tpu_custom_call" | custom-call | flops 1 | bytes 1 | tf_op jit(solution)/shard_map/pallas_call | solution.py:375
  6.1 0.5 collective-permute-done.came_ref
  6.6 0.9 %shard_map.105 = (f32[256,1024]{1,0:T(8,128)S(1)}, f32[256,1024]{1,0:T(8,128)S(1)}, f32[4,128,128]{2,1,0:T(8,128)S(1)}, f32[4,128,128]{2,1,0:T(8,128)S(1)}) custom-call(f32[8,256]{1,0:T(8,128)S(1)} %get-tuple-element.55.source_ref, f32[256,1024]{1,0:T(8,128)S(1)} %get-tuple-element.56.k_ref, f32[256,1024]{1,0:T(8,128)S(1)} %get-tuple-element.57.v_ref, ...), custom_call_target="tpu_custom_call" | custom-call | flops 1 | bytes 1 | tf_op jit(solution)/shard_map/pallas_call | solution.py:396
  7.5 1.6 %collective-permute-start.3 = (f32[4,128,128]{2,1,0:T(8,128)S(1)}, f32[4,128,128]{2,1,0:T(8,128)S(1)}, u32[]{:S(2)}, u32[]{:S(2)}) collective-permute-start(f32[4,128,128]{2,1,0:T(8,128)S(1)} %get-tuple-element.65.refs_0_), channel_id=1, source_target_pairs={{0,4},{4,0},{8,12},{12,8},{16,20},{20,16},{24,28},{28,24},{1,5},{5... | collective-permute-start | bytes 786440 | tf_op jit(solution)/shard_map/ppermute | solution.py:327
  9.1 2.4 %collective-permute-start.5 = (f32[4,128,128]{2,1,0:T(8,128)S(1)}, f32[4,128,128]{2,1,0:T(8,128)S(1)}, u32[]{:S(2)}, u32[]{:S(2)}) collective-permute-start(f32[4,128,128]{2,1,0:T(8,128)S(1)} %get-tuple-element.72), channel_id=1, source_target_pairs={{16,8},{20,12},{24,16},{28,20},{17,9},{21,13},{25,17},{29,21},{18,... | collective-permute-start | bytes 786440 | tf_op jit(solution)/shard_map/ppermute | solution.py:327
  11.5 1.6 %collective-permute-start.1 = (f32[2,8,128]{2,1,0:T(8,128)S(1)}, f32[2,8,128]{2,1,0:T(8,128)S(1)}, u32[]{:S(2)}, u32[]{:S(2)}) collective-permute-start(f32[2,8,128]{2,1,0:T(8,128)S(1)} %shard_map.104.after_ref.own_ref), channel_id=1, source_target_pairs={{0,8},{4,12},{8,0},{12,4},{16,24},{20,28},{24,16},{28,20},{1,9},{5... | collective-permute-start | bytes 24584 | tf_op jit(solution)/shard_map/ppermute | solution.py:327
  13.1 4.8 %collective-permute-done.1.came_ref = f32[2,8,128]{2,1,0:T(8,128)S(1)} collective-permute-done((f32[2,8,128]{2,1,0:T(8,128)S(1)}, f32[2,8,128]{2,1,0:T(8,128)S(1)}, u32[]{:S(2)}, u32[]{:S(2)}) %collective-permute-start.1) | collective-permute-done | bytes 8224 | tf_op jit(solution)/shard_map/ppermute | solution.py:327
  18.0 1.0 %collective-permute-start.4 = (f32[4,128,128]{2,1,0:T(8,128)S(1)}, f32[4,128,128]{2,1,0:T(8,128)S(1)}, u32[]{:S(2)}, u32[]{:S(2)}) collective-permute-start(f32[4,128,128]{2,1,0:T(8,128)S(1)} %get-tuple-element.67.refs_0_), channel_id=1, source_target_pairs={{0,4},{4,0},{8,12},{12,8},{16,20},{20,16},{24,28},{28,24},{1,5},{5... | collective-permute-start | bytes 786440 | tf_op jit(solution)/shard_map/ppermute | solution.py:327
  18.9 2.9 %collective-permute-start.7 = (f32[4,128,128]{2,1,0:T(8,128)S(1)}, f32[4,128,128]{2,1,0:T(8,128)S(1)}, u32[]{:S(2)}, u32[]{:S(2)}) collective-permute-start(f32[4,128,128]{2,1,0:T(8,128)S(1)} %get-tuple-element.75), channel_id=1, source_target_pairs={{16,8},{20,12},{24,16},{28,20},{17,9},{21,13},{25,17},{29,21},{18,... | collective-permute-start | bytes 786440 | tf_op jit(solution)/shard_map/ppermute | solution.py:327
  21.8 2.6 %shard_map.107 = (f32[256,512]{1,0:T(8,128)S(1)}, f32[256,512]{1,0:T(8,128)S(1)}, f32[256,512]{1,0:T(8,128)S(1)}, f32[8,256]{1,0:T(8,128)S(1)}) custom-call(f32[256,1024]{1,0:T(8,128)S(1)} %get-tuple-element.49.q_ref.refs_0_, f32[256,1024]{1,0:T(8,128)S(1)} %get-tuple-element.56.k_ref, f32[256,1024]{1,0:T(8,128)S(1)} %get-tuple-element.57.v_ref, ...), custom_call_target="tpu_custom_call" | custom-call | flops 1 | bytes 1 | tf_op jit(solution)/shard_map/pallas_call | solution.py:410
  24.4 2.6 %shard_map.108 = (f32[256,512]{1,0:T(8,128)S(1)}, f32[256,512]{1,0:T(8,128)S(1)}, f32[256,512]{1,0:T(8,128)S(1)}, f32[8,256]{1,0:T(8,128)S(1)}) custom-call(f32[256,1024]{1,0:T(8,128)S(1)} %get-tuple-element.49.q_ref.refs_0_, f32[256,1024]{1,0:T(8,128)S(1)} %get-tuple-element.56.k_ref, f32[256,1024]{1,0:T(8,128)S(1)} %get-tuple-element.57.v_ref, ...), custom_call_target="tpu_custom_call" | custom-call | flops 1 | bytes 1 | tf_op jit(solution)/shard_map/pallas_call | solution.py:410
  27.1 0.1 shard_map.113.refs_0_
  27.2 0.1 shard_map.114
  27.4 1.1 %collective-permute-start.6 = (f32[4,128,128]{2,1,0:T(8,128)S(1)}, f32[4,128,128]{2,1,0:T(8,128)S(1)}, u32[]{:S(2)}, u32[]{:S(2)}) collective-permute-start(f32[4,128,128]{2,1,0:T(8,128)S(1)} %shard_map.114), channel_id=1, source_target_pairs={{0,8},{4,12},{8,0},{12,4},{16,24},{20,28},{24,16},{28,20},{1,9},{5... | collective-permute-start | bytes 786440 | tf_op jit(solution)/shard_map/ppermute | solution.py:327
  28.5 1.3 %collective-permute-start.9 = (f32[4,128,128]{2,1,0:T(8,128)S(1)}, f32[4,128,128]{2,1,0:T(8,128)S(1)}, u32[]{:S(2)}, u32[]{:S(2)}) collective-permute-start(f32[4,128,128]{2,1,0:T(8,128)S(1)} %shard_map.113.refs_0_), channel_id=1, source_target_pairs={{8,16},{12,20},{9,17},{13,21},{10,18},{14,22},{11,19},{15,23}} | collective-permute-start | bytes 786440 | tf_op jit(solution)/shard_map/ppermute | solution.py:327
  29.8 0.1 shard_map.116.refs_0_
  29.9 0.2 shard_map.117
  30.1 0.4 collective-permute-start.8
  30.5 1.3 %collective-permute-start.11 = (f32[4,128,128]{2,1,0:T(8,128)S(1)}, f32[4,128,128]{2,1,0:T(8,128)S(1)}, u32[]{:S(2)}, u32[]{:S(2)}) collective-permute-start(f32[4,128,128]{2,1,0:T(8,128)S(1)} %shard_map.116.refs_0_), channel_id=1, source_target_pairs={{8,16},{12,20},{9,17},{13,21},{10,18},{14,22},{11,19},{15,23}} | collective-permute-start | bytes 786440 | tf_op jit(solution)/shard_map/ppermute | solution.py:327
  31.8 4.6 %collective-permute-start.15 = (f32[4,128,128]{2,1,0:T(8,128)S(1)}, f32[4,128,128]{2,1,0:T(8,128)S(1)}, u32[]{:S(2)}, u32[]{:S(2)}) collective-permute-start(f32[4,128,128]{2,1,0:T(8,128)S(1)} %collective-permute-done.5.refs_2_.refs_1_), channel_id=1, source_target_pairs={{16,8},{20,12},{17,9},{21,13},{18,10},{22,14},{19,11},{23,15}} | collective-permute-start | bytes 786440 | tf_op jit(solution)/shard_map/ppermute | solution.py:327
  36.4 1.3 %collective-permute-start.13 = (f32[4,128,128]{2,1,0:T(8,128)S(1)}, f32[4,128,128]{2,1,0:T(8,128)S(1)}, u32[]{:S(2)}, u32[]{:S(2)}) collective-permute-start(f32[4,128,128]{2,1,0:T(8,128)S(1)} %collective-permute-done.7.refs_2_.refs_1_), channel_id=1, source_target_pairs={{16,8},{20,12},{17,9},{21,13},{18,10},{22,14},{19,11},{23,15}} | collective-permute-start | bytes 786440 | tf_op jit(solution)/shard_map/ppermute | solution.py:327
  37.7 0.7 %shard_map.111 = (f32[256,512]{1,0:T(8,128)S(1)}, f32[8,256]{1,0:T(8,128)S(1)}) custom-call(f32[256,1024]{1,0:T(8,128)S(1)} %get-tuple-element.49.q_ref.refs_0_, f32[256,1024]{1,0:T(8,128)S(1)} %get-tuple-element.52.after_ref.refs_1_, f32[3,256,128]{2,1,0:T(8,128)S(1)} %get-tuple-element.53.refs_2_, f32[8,128]{1,0:T(8,128)S(1)} %shard_map.110.refs_3_.factor_ref, ...), custom_call_target="tpu_custom_call" | custom-call | flops 1 | bytes 1 | tf_op jit(solution)/shard_map/pallas_call | solution.py:455
  38.5 0.8 %shard_map.112 = (f32[256,512]{1,0:T(8,128)S(1)}, f32[8,256]{1,0:T(8,128)S(1)}) custom-call(f32[256,1024]{1,0:T(8,128)S(1)} %get-tuple-element.49.q_ref.refs_0_, f32[256,1024]{1,0:T(8,128)S(1)} %get-tuple-element.52.after_ref.refs_1_, f32[3,256,128]{2,1,0:T(8,128)S(1)} %get-tuple-element.53.refs_2_, f32[8,128]{1,0:T(8,128)S(1)} %shard_map.110.refs_3_.factor_ref, ...), custom_call_target="tpu_custom_call" | custom-call | flops 1 | bytes 1 | tf_op jit(solution)/shard_map/pallas_call | solution.py:455
  39.3 0.1 shard_map.119
  39.4 1.9 %collective-permute-start.10 = (f32[4,128,128]{2,1,0:T(8,128)S(1)}, f32[4,128,128]{2,1,0:T(8,128)S(1)}, u32[]{:S(2)}, u32[]{:S(2)}) collective-permute-start(f32[4,128,128]{2,1,0:T(8,128)S(1)} %shard_map.119), channel_id=1, source_target_pairs={{8,16},{12,20},{16,24},{20,28},{9,17},{13,21},{17,25},{21,29},{10,... | collective-permute-start | bytes 786440 | tf_op jit(solution)/shard_map/ppermute | solution.py:327
  41.4 0.8 %collective-permute-done.11.refs_2_ = f32[4,128,128]{2,1,0:T(8,128)S(1)} collective-permute-done((f32[4,128,128]{2,1,0:T(8,128)S(1)}, f32[4,128,128]{2,1,0:T(8,128)S(1)}, u32[]{:S(2)}, u32[]{:S(2)}) %collective-permute-start.11) | collective-permute-done | bytes 262176 | tf_op jit(solution)/shard_map/ppermute | solution.py:327
  42.2 0.1 shard_map.121
  42.3 2.1 %collective-permute-start.12 = (f32[4,128,128]{2,1,0:T(8,128)S(1)}, f32[4,128,128]{2,1,0:T(8,128)S(1)}, u32[]{:S(2)}, u32[]{:S(2)}) collective-permute-start(f32[4,128,128]{2,1,0:T(8,128)S(1)} %shard_map.121), channel_id=1, source_target_pairs={{8,16},{12,20},{16,24},{20,28},{9,17},{13,21},{17,25},{21,29},{10,... | collective-permute-start | bytes 786440 | tf_op jit(solution)/shard_map/ppermute | solution.py:327
  44.4 0.1 shard_map.125.refs_0_.kept_ref
  44.6 0.1 shard_map.126
  44.7 0.7 %collective-permute-start.16 = (f32[4,128,128]{2,1,0:T(8,128)S(1)}, f32[4,128,128]{2,1,0:T(8,128)S(1)}, u32[]{:S(2)}, u32[]{:S(2)}) collective-permute-start(f32[4,128,128]{2,1,0:T(8,128)S(1)} %shard_map.126), channel_id=1, source_target_pairs={{0,4},{4,0},{8,12},{12,8},{16,20},{20,16},{24,28},{28,24},{1,5},{5... | collective-permute-start | bytes 786440 | tf_op jit(solution)/shard_map/ppermute | solution.py:327
  45.4 0.1 shard_map.123.refs_0_.kept_ref
  45.6 0.1 shard_map.124
  45.7 1.5 %collective-permute-start.14 = (f32[4,128,128]{2,1,0:T(8,128)S(1)}, f32[4,128,128]{2,1,0:T(8,128)S(1)}, u32[]{:S(2)}, u32[]{:S(2)}) collective-permute-start(f32[4,128,128]{2,1,0:T(8,128)S(1)} %shard_map.124), channel_id=1, source_target_pairs={{0,4},{4,0},{8,12},{12,8},{16,20},{20,16},{24,28},{28,24},{1,5},{5... | collective-permute-start | bytes 786440 | tf_op jit(solution)/shard_map/ppermute | solution.py:327
  47.2 0.7 %shard_map.115 = (f32[256,512]{1,0:T(8,128)S(1)}, f32[8,256]{1,0:T(8,128)S(1)}) custom-call(f32[256,1024]{1,0:T(8,128)S(1)} %get-tuple-element.49.q_ref.refs_0_, f32[256,1024]{1,0:T(8,128)S(1)} %get-tuple-element.52.after_ref.refs_1_, f32[3,256,128]{2,1,0:T(8,128)S(1)} %get-tuple-element.53.refs_2_, f32[8,128]{1,0:T(8,128)S(1)} %shard_map.110.refs_3_.factor_ref, ...), custom_call_target="tpu_custom_call" | custom-call | flops 1 | bytes 1 | tf_op jit(solution)/shard_map/pallas_call | solution.py:455
  47.9 0.8 %shard_map.118 = (f32[256,512]{1,0:T(8,128)S(1)}, f32[8,256]{1,0:T(8,128)S(1)}) custom-call(f32[256,1024]{1,0:T(8,128)S(1)} %get-tuple-element.49.q_ref.refs_0_, f32[256,1024]{1,0:T(8,128)S(1)} %get-tuple-element.52.after_ref.refs_1_, f32[3,256,128]{2,1,0:T(8,128)S(1)} %get-tuple-element.53.refs_2_, f32[8,128]{1,0:T(8,128)S(1)} %shard_map.110.refs_3_.factor_ref, ...), custom_call_target="tpu_custom_call" | custom-call | flops 1 | bytes 1 | tf_op jit(solution)/shard_map/pallas_call | solution.py:455
  48.7 0.8 %collective-permute-done.10.refs_6_ = f32[4,128,128]{2,1,0:T(8,128)S(1)} collective-permute-done((f32[4,128,128]{2,1,0:T(8,128)S(1)}, f32[4,128,128]{2,1,0:T(8,128)S(1)}, u32[]{:S(2)}, u32[]{:S(2)}) %collective-permute-start.10) | collective-permute-done | bytes 262176 | tf_op jit(solution)/shard_map/ppermute | solution.py:327
  49.5 1.3 %shard_map.120 = (f32[256,1024]{1,0:T(8,128)}, f32[8,256]{1,0:T(8,128)S(1)}) custom-call(f32[256,1024]{1,0:T(8,128)S(1)} %get-tuple-element.49.q_ref.refs_0_, f32[256,1024]{1,0:T(8,128)S(1)} %get-tuple-element.52.after_ref.refs_1_, f32[3,256,128]{2,1,0:T(8,128)S(1)} %get-tuple-element.53.refs_2_, f32[8,128]{1,0:T(8,128)S(1)} %shard_map.110.refs_3_.factor_ref, ...), custom_call_target="tpu_custom_call" | custom-call | flops 1 | bytes 1 | tf_op jit(solution)/shard_map/pallas_call | solution.py:455
  50.9 1.5 %collective-permute-done.12.refs_6_ = f32[4,128,128]{2,1,0:T(8,128)S(1)} collective-permute-done((f32[4,128,128]{2,1,0:T(8,128)S(1)}, f32[4,128,128]{2,1,0:T(8,128)S(1)}, u32[]{:S(2)}, u32[]{:S(2)}) %collective-permute-start.12) | collective-permute-done | bytes 262176 | tf_op jit(solution)/shard_map/ppermute | solution.py:327
  52.3 1.4 %shard_map.122 = (f32[256,1024]{1,0:T(8,128)}, f32[8,256]{1,0:T(8,128)S(1)}) custom-call(f32[256,1024]{1,0:T(8,128)S(1)} %get-tuple-element.49.q_ref.refs_0_, f32[256,1024]{1,0:T(8,128)S(1)} %get-tuple-element.52.after_ref.refs_1_, f32[3,256,128]{2,1,0:T(8,128)S(1)} %get-tuple-element.53.refs_2_, ...), custom_call_target="tpu_custom_call", output_to_operand_aliasing={{0}: (7, {})} | custom-call | flops 1 | bytes 1 | tf_op jit(solution)/shard_map/pallas_call | solution.py:455
  53.7 0.1 collective-permute-start.17
  53.8 1.6 %collective-permute-start.18 = (f32[8,256]{1,0:T(8,128)S(1)}, f32[8,256]{1,0:T(8,128)S(1)}, u32[]{:S(2)}, u32[]{:S(2)}) collective-permute-start(f32[8,256]{1,0:T(8,128)S(1)} %get-tuple-element.93.refs_0_), channel_id=1, source_target_pairs={{0,2},{1,3},{2,0},{3,1},{4,6},{5,7},{6,4},{7,5},{8,10},{9,11},{10,... | collective-permute-start | bytes 24584 | tf_op jit(solution)/shard_map/ppermute | solution.py:546
  55.4 1.4 %collective-permute-start.19 = (f32[8,256]{1,0:T(8,128)S(1)}, f32[8,256]{1,0:T(8,128)S(1)}, u32[]{:S(2)}, u32[]{:S(2)}) collective-permute-start(f32[8,256]{1,0:T(8,128)S(1)} %get-tuple-element.93.refs_0_), channel_id=1, source_target_pairs={{0,3},{1,0},{2,1},{3,2},{4,7},{5,4},{6,5},{7,6},{8,11},{9,8},{10,9... | collective-permute-start | bytes 24584 | tf_op jit(solution)/shard_map/ppermute | solution.py:546
  56.8 1.4 %shard_map.127 = (f32[256,1024]{1,0:T(8,128)}, f32[256,1024]{1,0:T(8,128)}) custom-call(s32[1]{0:T(128)} %bitcast.device_ref, f32[256,1024]{1,0:T(8,128)S(1)} %get-tuple-element.82.wk_ref, f32[256,1024]{1,0:T(8,128)S(1)} %get-tuple-element.58.after_ref.wv_ref, f32[8,128]{1,0:T(8,128)S(1)} %shard_map.110.refs_3_.factor_ref, ...), custom_call_target="tpu_custom_call" | custom-call | flops 1 | bytes 1 | tf_op jit(solution)/shard_map/pallas_call | solution.py:551
  58.2 1.5 %shard_map.128 = (f32[256,1024]{1,0:T(8,128)}, f32[256,1024]{1,0:T(8,128)}) custom-call(s32[1]{0:T(128)} %bitcast.device_ref, f32[256,1024]{1,0:T(8,128)S(1)} %get-tuple-element.82.wk_ref, f32[256,1024]{1,0:T(8,128)S(1)} %get-tuple-element.58.after_ref.wv_ref, ...), custom_call_target="tpu_custom_call", output_to_operand_aliasing={{0}: (8, {}), {1}: (9, {})} | custom-call | flops 1 | bytes 1 | tf_op jit(solution)/shard_map/pallas_call | solution.py:551
  59.7 0.6 %shard_map.129 = f32[7,256]{1,0:T(8,128)} custom-call(f32[8,256]{1,0:T(8,128)S(1)} %get-tuple-element.93.refs_0_, f32[8,256]{1,0:T(8,128)S(1)} %collective-permute-done.17.refs_1_, f32[8,256]{1,0:T(8,128)S(1)} %collective-permute-done.18.refs_2_, f32[8,256]{1,0:T(8,128)S(1)} %collective-permute-done.19.refs_3_), custom_call_target="tpu_custom_call" | custom-call | tf_op jit(solution)/shard_map/pallas_call | solution.py:566
  (22 shorter events, 0.1 us)
Async XLA Ops:
  2.9 1.6 %copy-start = (f32[256,7]{0,1:T(8,128)S(1)}, f32[256,7]{0,1:T(8,128)}, u32[]{:S(2)}) copy-start(f32[256,7]{0,1:T(8,128)} %param.12) | copy-start | bytes 21508
  2.9 3.7 %collective-permute-start = (f32[1,8,128]{2,1,0:T(8,128)S(1)}, f32[1,8,128]{2,1,0:T(8,128)S(1)}, u32[]{:S(2)}, u32[]{:S(2)}) collective-permute-start(f32[1,8,128]{2,1,0:T(8,128)S(1)} %get-tuple-element.54.own_ref), channel_id=1, source_target_pairs={{0,4},{4,0},{8,12},{12,8},{16,20},{20,16},{24,28},{28,24},{1,5},{5... | collective-permute-start | bytes 12296 | tf_op jit(solution)/shard_map/ppermute | solution.py:327
  7.5 19.5 %collective-permute-start.3 = (f32[4,128,128]{2,1,0:T(8,128)S(1)}, f32[4,128,128]{2,1,0:T(8,128)S(1)}, u32[]{:S(2)}, u32[]{:S(2)}) collective-permute-start(f32[4,128,128]{2,1,0:T(8,128)S(1)} %get-tuple-element.65.refs_0_), channel_id=1, source_target_pairs={{0,4},{4,0},{8,12},{12,8},{16,20},{20,16},{24,28},{28,24},{1,5},{5... | collective-permute-start | bytes 786440 | tf_op jit(solution)/shard_map/ppermute | solution.py:327
  9.1 18.1 %collective-permute-start.5 = (f32[4,128,128]{2,1,0:T(8,128)S(1)}, f32[4,128,128]{2,1,0:T(8,128)S(1)}, u32[]{:S(2)}, u32[]{:S(2)}) collective-permute-start(f32[4,128,128]{2,1,0:T(8,128)S(1)} %get-tuple-element.72), channel_id=1, source_target_pairs={{16,8},{20,12},{24,16},{28,20},{17,9},{21,13},{25,17},{29,21},{18,... | collective-permute-start | bytes 786440 | tf_op jit(solution)/shard_map/ppermute | solution.py:327
  11.5 6.5 %collective-permute-start.1 = (f32[2,8,128]{2,1,0:T(8,128)S(1)}, f32[2,8,128]{2,1,0:T(8,128)S(1)}, u32[]{:S(2)}, u32[]{:S(2)}) collective-permute-start(f32[2,8,128]{2,1,0:T(8,128)S(1)} %shard_map.104.after_ref.own_ref), channel_id=1, source_target_pairs={{0,8},{4,12},{8,0},{12,4},{16,24},{20,28},{24,16},{28,20},{1,9},{5... | collective-permute-start | bytes 24584 | tf_op jit(solution)/shard_map/ppermute | solution.py:327
  18.0 9.0 %collective-permute-start.2 = (f32[4,8,128]{2,1,0:T(8,128)S(1)}, f32[4,8,128]{2,1,0:T(8,128)S(1)}, u32[]{:S(2)}, u32[]{:S(2)}) collective-permute-start(f32[4,8,128]{2,1,0:T(8,128)S(1)} %shard_map.106.own_ref), channel_id=1, source_target_pairs={{0,16},{4,20},{8,24},{12,28},{16,0},{20,4},{24,8},{28,12},{1,17},{... | collective-permute-start | bytes 49160 | tf_op jit(solution)/shard_map/ppermute | solution.py:327
  18.0 11.8 %collective-permute-start.4 = (f32[4,128,128]{2,1,0:T(8,128)S(1)}, f32[4,128,128]{2,1,0:T(8,128)S(1)}, u32[]{:S(2)}, u32[]{:S(2)}) collective-permute-start(f32[4,128,128]{2,1,0:T(8,128)S(1)} %get-tuple-element.67.refs_0_), channel_id=1, source_target_pairs={{0,4},{4,0},{8,12},{12,8},{16,20},{20,16},{24,28},{28,24},{1,5},{5... | collective-permute-start | bytes 786440 | tf_op jit(solution)/shard_map/ppermute | solution.py:327
  18.9 11.0 %collective-permute-start.7 = (f32[4,128,128]{2,1,0:T(8,128)S(1)}, f32[4,128,128]{2,1,0:T(8,128)S(1)}, u32[]{:S(2)}, u32[]{:S(2)}) collective-permute-start(f32[4,128,128]{2,1,0:T(8,128)S(1)} %get-tuple-element.75), channel_id=1, source_target_pairs={{16,8},{20,12},{24,16},{28,20},{17,9},{21,13},{25,17},{29,21},{18,... | collective-permute-start | bytes 786440 | tf_op jit(solution)/shard_map/ppermute | solution.py:327
  27.4 9.0 %collective-permute-start.6 = (f32[4,128,128]{2,1,0:T(8,128)S(1)}, f32[4,128,128]{2,1,0:T(8,128)S(1)}, u32[]{:S(2)}, u32[]{:S(2)}) collective-permute-start(f32[4,128,128]{2,1,0:T(8,128)S(1)} %shard_map.114), channel_id=1, source_target_pairs={{0,8},{4,12},{8,0},{12,4},{16,24},{20,28},{24,16},{28,20},{1,9},{5... | collective-permute-start | bytes 786440 | tf_op jit(solution)/shard_map/ppermute | solution.py:327
  28.5 10.8 %collective-permute-start.9 = (f32[4,128,128]{2,1,0:T(8,128)S(1)}, f32[4,128,128]{2,1,0:T(8,128)S(1)}, u32[]{:S(2)}, u32[]{:S(2)}) collective-permute-start(f32[4,128,128]{2,1,0:T(8,128)S(1)} %shard_map.113.refs_0_), channel_id=1, source_target_pairs={{8,16},{12,20},{9,17},{13,21},{10,18},{14,22},{11,19},{15,23}} | collective-permute-start | bytes 786440 | tf_op jit(solution)/shard_map/ppermute | solution.py:327
  30.1 11.3 %collective-permute-start.8 = (f32[4,128,128]{2,1,0:T(8,128)S(1)}, f32[4,128,128]{2,1,0:T(8,128)S(1)}, u32[]{:S(2)}, u32[]{:S(2)}) collective-permute-start(f32[4,128,128]{2,1,0:T(8,128)S(1)} %shard_map.117), channel_id=1, source_target_pairs={{0,8},{4,12},{8,0},{12,4},{16,24},{20,28},{24,16},{28,20},{1,9},{5... | collective-permute-start | bytes 786440 | tf_op jit(solution)/shard_map/ppermute | solution.py:327
  30.5 11.6 %collective-permute-start.11 = (f32[4,128,128]{2,1,0:T(8,128)S(1)}, f32[4,128,128]{2,1,0:T(8,128)S(1)}, u32[]{:S(2)}, u32[]{:S(2)}) collective-permute-start(f32[4,128,128]{2,1,0:T(8,128)S(1)} %shard_map.116.refs_0_), channel_id=1, source_target_pairs={{8,16},{12,20},{9,17},{13,21},{10,18},{14,22},{11,19},{15,23}} | collective-permute-start | bytes 786440 | tf_op jit(solution)/shard_map/ppermute | solution.py:327
  31.8 12.6 %collective-permute-start.15 = (f32[4,128,128]{2,1,0:T(8,128)S(1)}, f32[4,128,128]{2,1,0:T(8,128)S(1)}, u32[]{:S(2)}, u32[]{:S(2)}) collective-permute-start(f32[4,128,128]{2,1,0:T(8,128)S(1)} %collective-permute-done.5.refs_2_.refs_1_), channel_id=1, source_target_pairs={{16,8},{20,12},{17,9},{21,13},{18,10},{22,14},{19,11},{23,15}} | collective-permute-start | bytes 786440 | tf_op jit(solution)/shard_map/ppermute | solution.py:327
  36.4 9.0 %collective-permute-start.13 = (f32[4,128,128]{2,1,0:T(8,128)S(1)}, f32[4,128,128]{2,1,0:T(8,128)S(1)}, u32[]{:S(2)}, u32[]{:S(2)}) collective-permute-start(f32[4,128,128]{2,1,0:T(8,128)S(1)} %collective-permute-done.7.refs_2_.refs_1_), channel_id=1, source_target_pairs={{16,8},{20,12},{17,9},{21,13},{18,10},{22,14},{19,11},{23,15}} | collective-permute-start | bytes 786440 | tf_op jit(solution)/shard_map/ppermute | solution.py:327
  39.4 10.1 %collective-permute-start.10 = (f32[4,128,128]{2,1,0:T(8,128)S(1)}, f32[4,128,128]{2,1,0:T(8,128)S(1)}, u32[]{:S(2)}, u32[]{:S(2)}) collective-permute-start(f32[4,128,128]{2,1,0:T(8,128)S(1)} %shard_map.119), channel_id=1, source_target_pairs={{8,16},{12,20},{16,24},{20,28},{9,17},{13,21},{17,25},{21,29},{10,... | collective-permute-start | bytes 786440 | tf_op jit(solution)/shard_map/ppermute | solution.py:327
  42.3 10.0 %collective-permute-start.12 = (f32[4,128,128]{2,1,0:T(8,128)S(1)}, f32[4,128,128]{2,1,0:T(8,128)S(1)}, u32[]{:S(2)}, u32[]{:S(2)}) collective-permute-start(f32[4,128,128]{2,1,0:T(8,128)S(1)} %shard_map.121), channel_id=1, source_target_pairs={{8,16},{12,20},{16,24},{20,28},{9,17},{13,21},{17,25},{21,29},{10,... | collective-permute-start | bytes 786440 | tf_op jit(solution)/shard_map/ppermute | solution.py:327
  44.7 12.0 %collective-permute-start.16 = (f32[4,128,128]{2,1,0:T(8,128)S(1)}, f32[4,128,128]{2,1,0:T(8,128)S(1)}, u32[]{:S(2)}, u32[]{:S(2)}) collective-permute-start(f32[4,128,128]{2,1,0:T(8,128)S(1)} %shard_map.126), channel_id=1, source_target_pairs={{0,4},{4,0},{8,12},{12,8},{16,20},{20,16},{24,28},{28,24},{1,5},{5... | collective-permute-start | bytes 786440 | tf_op jit(solution)/shard_map/ppermute | solution.py:327
  45.7 12.5 %collective-permute-start.14 = (f32[4,128,128]{2,1,0:T(8,128)S(1)}, f32[4,128,128]{2,1,0:T(8,128)S(1)}, u32[]{:S(2)}, u32[]{:S(2)}) collective-permute-start(f32[4,128,128]{2,1,0:T(8,128)S(1)} %shard_map.124), channel_id=1, source_target_pairs={{0,4},{4,0},{8,12},{12,8},{16,20},{20,16},{24,28},{28,24},{1,5},{5... | collective-permute-start | bytes 786440 | tf_op jit(solution)/shard_map/ppermute | solution.py:327
  53.7 6.0 %collective-permute-start.17 = (f32[8,256]{1,0:T(8,128)S(1)}, f32[8,256]{1,0:T(8,128)S(1)}, u32[]{:S(2)}, u32[]{:S(2)}) collective-permute-start(f32[8,256]{1,0:T(8,128)S(1)} %get-tuple-element.93.refs_0_), channel_id=1, source_target_pairs={{0,1},{1,2},{2,3},{3,0},{4,5},{5,6},{6,7},{7,4},{8,9},{9,10},{10,1... | collective-permute-start | bytes 24584 | tf_op jit(solution)/shard_map/ppermute | solution.py:546
  53.8 5.9 %collective-permute-start.18 = (f32[8,256]{1,0:T(8,128)S(1)}, f32[8,256]{1,0:T(8,128)S(1)}, u32[]{:S(2)}, u32[]{:S(2)}) collective-permute-start(f32[8,256]{1,0:T(8,128)S(1)} %get-tuple-element.93.refs_0_), channel_id=1, source_target_pairs={{0,2},{1,3},{2,0},{3,1},{4,6},{5,7},{6,4},{7,5},{8,10},{9,11},{10,... | collective-permute-start | bytes 24584 | tf_op jit(solution)/shard_map/ppermute | solution.py:546
  55.4 4.3 %collective-permute-start.19 = (f32[8,256]{1,0:T(8,128)S(1)}, f32[8,256]{1,0:T(8,128)S(1)}, u32[]{:S(2)}, u32[]{:S(2)}) collective-permute-start(f32[8,256]{1,0:T(8,128)S(1)} %get-tuple-element.93.refs_0_), channel_id=1, source_target_pairs={{0,3},{1,0},{2,1},{3,2},{4,7},{5,4},{6,5},{7,6},{8,11},{9,8},{10,9... | collective-permute-start | bytes 24584 | tf_op jit(solution)/shard_map/ppermute | solution.py:546

commit v4 on v3

--- a/solution.py
+++ b/solution.py
@@ -62,11 +62,16 @@
     return copy
 
 
-def join_kernel(own_ref, came_ref, after_ref, out_ref):
+def join_kernel(bit, device_ref, own_ref, came_ref, after_ref, out_ref):
     del after_ref
     half = own_ref.shape[0]
-    out_ref[:half] = own_ref[...]
-    out_ref[half:] = came_ref[...]
+    upper = ((device_ref[0] >> bit) & 1) == 1
+    out_ref[:half] = jnp.where(upper, came_ref[...], own_ref[...])
+    out_ref[half:] = jnp.where(upper, own_ref[...], came_ref[...])
+
+
+def rows_of(place, width):
+    return slice(place * width, (place + 1) * width)
 
 
 def total_kernel(*refs):
@@ -106,12 +111,12 @@
     cols = rows.T
     cols_ref[...] = cols
     row = iota((8, LANES), 0)
-    table_ref[0] = jnp.where(row == 0, cols[tokens - 1 :], jnp.where(row == 1, last, first))
+    table_ref[...] = jnp.where(row == 0, cols[tokens - 1 :], jnp.where(row == 1, last, first))
     for copy in copies[2:]:
         copy.wait()
 
 
-def states_kernel(heads, source_ref, k_ref, v_ref, after_ref, wk_ref, wv_ref, *states):
+def states_kernel(heads, part_heads, source_ref, k_ref, v_ref, after_ref, wk_ref, wv_ref, *states):
     del after_ref
     width = k_ref.shape[1] // heads
     for head in range(heads):
@@ -121,12 +126,12 @@
         v = v_ref[:, at]
         wk_ref[:, at] = weighted
         wv_ref[:, at] = weight * v
-        part, place = divmod(head, states[0].shape[0])
-        states[part][place] = dot(weighted, v, COLS)
+        part, place = divmod(head, part_heads)
+        states[part][rows_of(place, width), :] = dot(weighted, v, COLS)
 
 
 def second_kernel(
-    heads, depth, level_ref, query_ref, q_ref, o_ref, uo_ref, spread_ref, *outs
+    heads, depth, part_heads, level_ref, query_ref, q_ref, o_ref, table_ref, uo_ref, spread_ref, *outs
 ):
     width = q_ref.shape[1] // heads
     for d in range(depth):
@@ -138,9 +143,11 @@
         uo_ref[:, at] = weighted
         scaled = jnp.concatenate([spread_ref[d] * weighted for d in range(depth)], axis=1)
         grads = dot(q_ref[:, at], scaled, COLS)
-        part, place = divmod(head, outs[0].shape[0])
+        part, place = divmod(head, part_heads)
         for d in range(depth):
-            outs[part * depth + d][place] = grads[:, d * width : (d + 1) * width]
+            outs[part * depth + d][rows_of(place, width), :] = grads[:, d * width : (d + 1) * width]
+    for out in outs[depth - 1 :: depth]:
+        out[part_heads * width :, :] = table_ref[...]
 
 
 def local_kernel(
@@ -175,11 +182,30 @@
     terms_ref[...] = terms if terms_in is None else terms + terms_in[...]
 
 
-def factors_kernel(depth, device_ref, table_ref, factor_ref):
+def factors_kernel(depth, known, device_ref, *refs):
+    own_ref, factor_ref, table_ref = refs[0], refs[-2], refs[-1]
     stretches = table_ref.shape[0]
+    size = stretches // 4
     device = device_ref[0]
+    quarter = device // size
+
+    def put(where, values):
+        @pl.when((where >= 0) & (where < 4))
+        def _():
+            table_ref[pl.ds(where * size, size)] = values.reshape(size, 8, LANES)
+
+    table_ref[...] = jnp.zeros_like(table_ref)
+    from_where = {
+        "second": jnp.int32(1),
+        "next": quarter + 1,
+        "over": quarter + 2,
+        "beside": quarter ^ 1,
+    }
+    for name, ref in zip(known, refs[1:-2]):
+        put(from_where[name], ref[ref.shape[0] - 8 * size :, :])
+    put(quarter, own_ref[...])
     totals, lasts, firsts = table_ref[:, 0, :], table_ref[:, 1, :], table_ref[:, 2, :]
-    stretch = iota((stretches, LANES), 0) ^ device
+    stretch = iota((stretches, LANES), 0)
 
     def at(values, index):
         return jnp.sum(jnp.where(stretch == index, values, 0.0), axis=0, keepdims=True)
@@ -207,6 +233,16 @@
     for hop in (stretches // 4, stretches // 2):
         target = jnp.minimum(device + hop, stretches - 1)
         factors.append(jnp.where(second, reach(middle, target), 0.0))
+    low_end = ((device >> (depth - 1)) << (depth - 1)) + size - 1
+    upper = ((device >> (depth - 2)) & 1) == 1
+    factors.append(jnp.where(upper, span(low_end, device - 1), 0.0))
+    carried = jnp.where(
+        at(firsts, device) == at(lasts, low_end + size), span(low_end, low_end + size), 0.0
+    )
+    factors.append(carried * factors[2 * depth])
+    target = jnp.minimum(device + size, stretches - 1)
+    linked = (at(firsts, target) == at(lasts, low_end)).astype(jnp.float32)
+    factors.append(jnp.where(upper, 0.0, linked))
     factor_ref[...] = jnp.zeros_like(factor_ref)
     for index, factor in enumerate(factors):
         factor_ref[index : index + 1, :] = factor
@@ -225,7 +261,7 @@
         head = base + place
         at = slice(head * width, (head + 1) * width)
         to = slice(place * width, (place + 1) * width)
-        states = [block[place] for block in blocks]
+        states = [block[rows_of(place, width), :] for block in blocks]
         states = [
             factor_ref[level - 1 : level, head : head + 1] * state
             for level, state in zip(chosen, states)
@@ -255,14 +291,14 @@
     gk_in, gv_in = refs[:2]
     gk_hbm, gv_hbm, gk_ref, gv_ref, sems = refs[-5:]
     copies = []
-    width = kept_ref.shape[2]
+    width = kept_ref.shape[1]
     upper = (device_ref[0] & 1).astype(jnp.float32)
     for place in range(gk_in.shape[1] // width):
         head = base + place
         at = slice(head * width, (head + 1) * width)
         to = slice(place * width, (place + 1) * width)
         own = upper + (1.0 - upper) * factor_ref[row : row + 1, head : head + 1]
-        state = own * kept_ref[place] + came_ref[place]
+        state = own * kept_ref[rows_of(place, width), :] + came_ref[rows_of(place, width), :]
         gk_ref[:, to] = gk_in[:, to] + dot(wv_ref[:, at], state, TURNED)
         copies.append(ship(gk_ref, gk_hbm, to, at, sems.at[0, place]))
         gv_ref[:, to] = gv_in[:, to] + dot(wk_ref[:, at], state, ROWS)
@@ -271,20 +307,25 @@
         copy.wait()
 
 
-def blend_kernel(base, recipe, inputs, device_ref, factor_ref, *refs):
+def blend_kernel(base, recipe, inputs, relay, top, device_ref, factor_ref, table_ref, *refs):
     arrays, out_ref = refs[:inputs], refs[-1]
     device = device_ref[0]
     factor = factor_ref[...]
-    for place in range(out_ref.shape[0]):
-        head = base + place
-        column = factor[:, head : head + 1]
+    width = out_ref.shape[1]
+    states = out_ref.shape[0] - table_ref.shape[0]
+    for place in range(states // width):
+        column = factor[:, base + place : base + place + 1]
         total = None
         for array, coefficient in zip(arrays, recipe):
             weight = coefficient(device, lambda row: column[row : row + 1, :])
-            term = array[place]
+            term = array[rows_of(place, width), :]
             term = term if weight is None else weight * term
             total = term if total is None else total + term
-        out_ref[place] = total
+        out_ref[rows_of(place, width), :] = total
+    table = table_ref[...]
+    if relay is not None:
+        table = jnp.where(((device >> (top - 1)) & 3) == 2, arrays[relay][states:, :], table)
+    out_ref[states:, :] = table
 
 
 def upper_flag(device, bit):
@@ -338,7 +379,7 @@
     part_heads = heads // PARTS
     parts = range(PARTS)
     part_width = part_heads * width
-    factor_rows = -(-(2 * depth + 2) // 8) * 8
+    factor_rows = -(-(2 * depth + 5) // 8) * 8
     side_rows = -(-(heads + 1) // 8) * 8
     turned_rows = -(-levels // 8) * 8
     token_bytes = tokens * width * 4
@@ -348,7 +389,7 @@
         return jax.ShapeDtypeStruct(dims, jnp.float32)
 
     tall = shape(tokens, heads * width)
-    state = shape(part_heads, width, width)
+    state = shape(part_heads * width + 8 * quarter, width)
     decay_rows, level_rows = log_decay.T, level_weight.T
     swaps = [[(i, i ^ (1 << d)) for i in range(stretches)] for d in range(depth)]
 
@@ -357,7 +398,7 @@
         out_shape=[tall] * 4
         + [shape(tokens, LANES), shape(side_rows, tokens)]
         + [shape(heads, tokens)] * 2
-        + [shape(1, 8, LANES)],
+        + [shape(8, LANES)],
         in_specs=[SCALARS] + [FAR] * 6,
         out_specs=[WHOLE] * 9,
         scratch_shapes=[
@@ -371,37 +412,6 @@
         *map(far, (decay_rows, segment.reshape(1, tokens))),
         *map(far, (key_input, value_input, queries, grad_output)),
     )
-
-    weighted_o, spread, *grads = pl.pallas_call(
-        functools.partial(second_kernel, heads, depth),
-        out_shape=[tall, shape(depth, tokens, width)] + [state] * (PARTS * depth),
-        in_specs=[WHOLE] * 4,
-        out_specs=[WHOLE] * (2 + PARTS * depth),
-        compiler_params=params(),
-        cost_estimate=cost(heads * depth * work, heads * 2 * token_bytes),
-    )(level_rows, *map(near, (query, near_q, near_o)))
-    grads = [grads[p * depth : (p + 1) * depth] for p in parts]
-
-    def join(table, d, after):
-        return pl.pallas_call(
-            join_kernel,
-            out_shape=shape(2 << d, 8, LANES),
-            in_specs=[WHOLE] * 2 + [ANYWHERE],
-            out_specs=WHOLE,
-            compiler_params=params(),
-        )(near(table), near(send(table, swaps[d])), after)
-
-    table = join(table, 0, weighted_o)
-
-    weighted_k, weighted_v, *running = pl.pallas_call(
-        functools.partial(states_kernel, heads),
-        out_shape=[tall] * 2 + [state] * PARTS,
-        in_specs=[WHOLE] * 3 + [ANYWHERE],
-        out_specs=[WHOLE] * (2 + PARTS),
-        compiler_params=params(),
-        cost_estimate=cost(heads * work, 0),
-    )(*map(near, (source, near_k, near_v)), table)
-
 
     gq, gk, gv = ([None] * PARTS for _ in range(3))
     terms = None
@@ -419,16 +429,48 @@
             compiler_params=params(),
             cost_estimate=cost(part_heads * 30 * tokens * tokens * width, 0),
         )(*map(near, (near_q, near_k, near_v, near_o, cols, rows)), level_rows, *before)
-
-    for d in range(1, depth):
-        table = join(table, d, weighted_v if d == 1 else terms)
-    factor = pl.pallas_call(
-        functools.partial(factors_kernel, depth),
-        out_shape=shape(factor_rows, LANES),
-        in_specs=[SCALARS, WHOLE],
-        out_specs=WHOLE,
+        if p == 0:
+            first_terms = terms
+
+    for d in range(depth - 2):
+        table = pl.pallas_call(
+            functools.partial(join_kernel, d),
+            out_shape=shape(16 << d, LANES),
+            in_specs=[SCALARS] + [WHOLE] * 2 + [ANYWHERE],
+            out_specs=WHOLE,
+            compiler_params=params(),
+        )(device, near(table), near(send(table, swaps[d])), first_terms)
+
+    def factors(*known):
+        names, arrays = [k[0] for k in known], [k[1] for k in known]
+        return pl.pallas_call(
+            functools.partial(factors_kernel, depth, names),
+            out_shape=shape(factor_rows, LANES),
+            in_specs=[SCALARS] + [WHOLE] * (1 + len(arrays)),
+            out_specs=WHOLE,
+            scratch_shapes=[pltpu.VMEM((stretches, 8, LANES), jnp.float32)],
+            compiler_params=params(),
+        )(device, *map(near, (table, *arrays)))
+
+    weighted_k, weighted_v, *running = pl.pallas_call(
+        functools.partial(states_kernel, heads, part_heads),
+        out_shape=[tall] * 2 + [state] * PARTS,
+        in_specs=[WHOLE] * 3 + [ANYWHERE],
+        out_specs=[WHOLE] * (2 + PARTS),
         compiler_params=params(),
-    )(device, near(table))
+        cost_estimate=cost(heads * work, 0),
+    )(*map(near, (source, near_k, near_v)), table)
+
+
+    weighted_o, spread, *grads = pl.pallas_call(
+        functools.partial(second_kernel, heads, depth, part_heads),
+        out_shape=[tall, shape(depth, tokens, width)] + [state] * (PARTS * depth),
+        in_specs=[WHOLE] * 5,
+        out_specs=[WHOLE] * (2 + PARTS * depth),
+        compiler_params=params(),
+        cost_estimate=cost(heads * depth * work, heads * 2 * token_bytes),
+    )(level_rows, *map(near, (query, near_q, near_o, table)))
+    grads = [grads[p * depth : (p + 1) * depth] for p in parts]
 
     def own_level(level):
         return level - 1
@@ -436,14 +478,14 @@
     def block_row(distance):
         return depth + distance
 
-    third, fourth = 2 * depth, 2 * depth + 1
+    third, fourth, ahead, carried, linked = (2 * depth + i for i in range(5))
     second_third = [(quarter + i, 2 * quarter + i) for i in range(quarter)]
     third_fourth = [(2 * quarter + i, 3 * quarter + i) for i in range(quarter)]
     third_second = [(b, a) for a, b in second_third]
     shift_up = second_third + third_fourth
     shift_down = [(b, a) for a, b in shift_up]
 
-    def add_levels(chosen, p, gq, terms, blocks, out=None, final=False):
+    def add_levels(chosen, p, factor, gq, terms, blocks, out=None, final=False):
         in_hbm = [] if out is None else [out]
         inputs = 6 + len(blocks)
         scratch = [pltpu.VMEM((tokens, width), jnp.float32)] * len(chosen)
@@ -472,36 +514,44 @@
             cost_estimate=cost(part_heads * work * 2 * len(chosen), 0),
         )(*map(near, (near_q, weighted_o, spread, factor, gq, terms, *blocks)), *in_hbm)
 
-    def blend(part, terms, after=()):
-        arrays, recipe = zip(*terms)
+    top, next_bit = depth - 1, depth - 2
+
+    def blend(part, factor, weighted, after=(), relay=None):
+        arrays, recipe = zip(*weighted)
         return pl.pallas_call(
-            functools.partial(blend_kernel, part * part_heads, recipe, len(arrays)),
+            functools.partial(
+                blend_kernel, part * part_heads, recipe, len(arrays), relay, top
+            ),
             out_shape=state,
-            in_specs=[SCALARS, WHOLE] + [WHOLE] * len(arrays) + [ANYWHERE] * len(after),
+            in_specs=[SCALARS] + [WHOLE] * (2 + len(arrays)) + [ANYWHERE] * len(after),
             out_specs=WHOLE,
             compiler_params=params(),
             cost_estimate=cost(1, 1),
-        )(device, *map(near, (factor, *arrays)), *after)
-
-    top, next_bit = depth - 1, depth - 2
+        )(device, *map(near, (factor, table, *arrays)), *after)
+
     shifted = [send(grads[p][top], shift_down) for p in parts]
     came = [[] for _ in parts]
+    inside = factors()
     for d in range(depth - 2):
         for p in parts:
             arrived = send(running[p], swaps[d])
             came[p].append(arrived)
             running[p] = blend(
                 p,
+                inside,
                 [(running[p], upper_or(d, block_row(d))), (arrived, lower_or(d, block_row(d)))],
+                [terms],
             )
+    after_shift = factors(("next", shifted[0]))
     crossed, relayed, passed = [], [], []
     for p in parts:
         message = blend(
             p,
+            after_shift,
             [
                 (running[p], lower(next_bit)),
-                (grads[p][next_bit], by(own_level(depth - 1))),
-                (shifted[p], both(block_row(next_bit), third)),
+                (grads[p][next_bit], by(ahead)),
+                (shifted[p], by(carried)),
             ],
         )
         crossed.append(send(message, swaps[next_bit]))
@@ -509,37 +559,50 @@
         passed.append(send(running[p], second_third))
     if depth > 2:
         for p in parts:
-            gq[p], terms = add_levels(list(range(1, depth - 1)), p, gq[p], terms, came[p])
+            gq[p], terms = add_levels(
+                list(range(1, depth - 1)), p, inside, gq[p], terms, came[p]
+            )
+    after_cross = factors(("next", shifted[0]), ("beside", crossed[0]))
+    after_relay = factors(("next", shifted[0]), ("over", relayed[0]), ("beside", crossed[0]))
     topmost, kept, sources = [], [], []
     for p in parts:
         upward = blend(
             p,
+            after_cross,
             [
                 (running[p], quarter_flag(top, 1)),
                 (crossed[p], quarter_flag(top, 1, block_row(next_bit))),
                 (passed[p], quarter_flag(top, 2)),
             ],
             [terms],
+            2,
         )
         topmost.append(send(upward, shift_up))
         pending = blend(
-            p, [(crossed[p], lower(next_bit)), (shifted[p], by(third)), (relayed[p], by(fourth))]
+            p,
+            after_relay,
+            [(crossed[p], by(linked)), (shifted[p], by(third)), (relayed[p], by(fourth))],
         )
         for d in range(depth - 3, -1, -1):
             outgoing = blend(
-                p, [(pending, lower_or(d, block_row(d))), (grads[p][d], by(own_level(d + 1)))]
+                p,
+                inside,
+                [(pending, lower_or(d, block_row(d))), (grads[p][d], by(own_level(d + 1)))],
             )
             arrived = send(outgoing, swaps[d])
             if d > 0:
-                pending = blend(p, [(pending, upper_or(d, block_row(d))), (arrived, plain)])
+                pending = blend(
+                    p, inside, [(pending, upper_or(d, block_row(d))), (arrived, plain)]
+                )
         kept.append(pending)
         sources.append(arrived)
     for p in parts:
-        gq[p], terms = add_levels([depth - 1], p, gq[p], terms, [crossed[p]])
+        gq[p], terms = add_levels([depth - 1], p, after_cross, gq[p], terms, [crossed[p]])
+    after_top = factors(("second", topmost[0]), ("beside", crossed[0]))
     grad_query = None
     for p in parts:
         grad_query, terms = add_levels(
-            [depth], p, gq[p], terms, [topmost[p]], grad_query, True
+            [depth], p, after_top, gq[p], terms, [topmost[p]], grad_query, True
         )
     groups = lax.axis_size("head")
     others = [
@@ -560,7 +623,7 @@
             cost_estimate=cost(part_heads * work * 2, 0),
         )(
             device,
-            *map(near, (weighted_k, weighted_v, factor, kept[p], sources[p], gk[p], gv[p])),
+            *map(near, (weighted_k, weighted_v, inside, kept[p], sources[p], gk[p], gv[p])),
             *done,
         )
     grad_level = pl.pallas_call(

time: 60.7 us -> 57.6 us (0.949)
  starting transfers between devices: 30.2 us -> 25.6 us
  waiting for transfers between devices: 8.36 us -> 9.31 us
    ppermute x17 -> x15, starting transfers between devices: 27.1 us -> 22.6 us  [send(): return lax.ppermute(array, 'seq', route)]
    ppermute x17 -> x15, waiting for transfers between devices: 8.35 us -> 9.3 us  [send(): return lax.ppermute(array, 'seq', route)]
    pallas_call x6 -> x8, Pallas kernels: 2.65 us -> 3.11 us  [the longest x1 1.65 us: on_device(): pl.pallas_call(functools.partial(second_kernel, heads, depth, part_heads)...]
  transfers between devices with their start and end apart: 20 -> 18, of which waited for: 5 -> 4; matrix products, arithmetic and copies ran while one was open for 0% -> 0% of each run, Pallas kernels for 28% -> 31%
where the time goes in v4:
time: 57.6 us; the launch traced here: 57.2 us
  starting transfers between devices  25.6 us (44%)
  Pallas kernels  21.3 us (37%)
  waiting for transfers between devices  9.31 us (16%)
  between operations  1.01 us (2%)
    ppermute x15, starting transfers between devices, send(): return lax.ppermute(array, 'seq', route)  22.6 us
    ppermute x15, waiting for transfers between devices, send(): return lax.ppermute(array, 'seq', route)  9.3 us
    pallas_call x6, Pallas kernels, add_levels(): pl.pallas_call(functools.partial(levels_kernel, heads, p * part_heads, ch...  5.85 us
    pallas_call x2, Pallas kernels, on_device(): pl.pallas_call(functools.partial(local_kernel, heads, p * part_heads), ou...  5.13 us
    ppermute x3, starting transfers between devices, on_device(): lax.ppermute(terms, 'head', [(i, (i + k) % groups) for i in range(groups)])  3.01 us
    pallas_call x2, Pallas kernels, on_device(): pl.pallas_call(functools.partial(sources_kernel, heads, p * part_heads, b...  2.93 us
    pallas_call x1, Pallas kernels, on_device(): pl.pallas_call(functools.partial(first_kernel, heads), out_shape=[tall] *...  2.26 us
    pallas_call x1, Pallas kernels, on_device(): pl.pallas_call(functools.partial(second_kernel, heads, depth, part_heads)...  1.65 us
  transfers between devices with their start and end apart: 18, of which 4 were waited for; matrix products, arithmetic and copies ran while one was open for 0% of the time, Pallas kernels for 31%

profile of v4, /device:TPU:16, one launch (start us, length us, event | category | flops | bytes accessed | tf_op | source)
XLA Modules:
  0.0 57.2 jit_solution(9305171404007054708)
XLA Ops:
  0.6 2.3 %shard_map.102 = (f32[256,1024]{1,0:T(8,128)S(1)}, f32[256,1024]{1,0:T(8,128)S(1)}, f32[256,1024]{1,0:T(8,128)S(1)}, f32[256,1024]{1,0:T(8,128)S(1)}, f32[256,12...) custom-call(s32[1]{0:T(128)} %bitcast.device_ref, ...), custom_call_target="tpu_custom_call" | custom-call | tf_op jit(solution)/shard_map/pallas_call | solution.py:396
  2.9 1.6 %collective-permute-start = (f32[8,128]{1,0:T(8,128)S(1)}, f32[8,128]{1,0:T(8,128)S(1)}, u32[]{:S(2)}, u32[]{:S(2)}) collective-permute-start(f32[8,128]{1,0:T(8,128)S(1)} %get-tuple-element.52.own_ref), channel_id=1, source_target_pairs={{0,4},{4,0},{8,12},{12,8},{16,20},{20,16},{24,28},{28,24},{1,5},{5... | collective-permute-start | bytes 12296 | tf_op jit(solution)/shard_map/ppermute | solution.py:368
  4.5 2.6 %shard_map.103 = (f32[256,512]{1,0:T(8,128)S(1)}, f32[256,512]{1,0:T(8,128)S(1)}, f32[256,512]{1,0:T(8,128)S(1)}, f32[8,256]{1,0:T(8,128)S(1)}) custom-call(f32[256,1024]{1,0:T(8,128)S(1)} %get-tuple-element.49.q_ref.refs_0_, f32[256,1024]{1,0:T(8,128)S(1)} %get-tuple-element.53.k_ref, f32[256,1024]{1,0:T(8,128)S(1)} %get-tuple-element.54.v_ref, ...), custom_call_target="tpu_custom_call" | custom-call | flops 1 | bytes 1 | tf_op jit(solution)/shard_map/pallas_call | solution.py:420
  7.1 1.0 %shard_map.108 = (f32[256,1024]{1,0:T(8,128)S(1)}, f32[256,1024]{1,0:T(8,128)S(1)}, f32[528,128]{1,0:T(8,128)S(1)}, f32[528,128]{1,0:T(8,128)S(1)}) custom-call(f32[8,256]{1,0:T(8,128)S(1)} %get-tuple-element.61.source_ref, f32[256,1024]{1,0:T(8,128)S(1)} %get-tuple-element.53.k_ref, f32[256,1024]{1,0:T(8,128)S(1)} %get-tuple-element.54.v_ref, ...), custom_call_target="tpu_custom_call" | custom-call | flops 1 | bytes 1 | tf_op jit(solution)/shard_map/pallas_call | solution.py:455
  8.0 1.1 %collective-permute-start.2 = (f32[528,128]{1,0:T(8,128)S(1)}, f32[528,128]{1,0:T(8,128)S(1)}, u32[]{:S(2)}, u32[]{:S(2)}) collective-permute-start(f32[528,128]{1,0:T(8,128)S(1)} %get-tuple-element.62.refs_0_), channel_id=1, source_target_pairs={{0,4},{4,0},{8,12},{12,8},{16,20},{20,16},{24,28},{28,24},{1,5},{5... | collective-permute-start | bytes 811016 | tf_op jit(solution)/shard_map/ppermute | solution.py:368
  9.1 1.6 %shard_map.105 = (f32[256,1024]{1,0:T(8,128)S(1)}, f32[3,256,128]{2,1,0:T(8,128)S(1)}, f32[528,128]{1,0:T(8,128)S(1)}, f32[528,128]{1,0:T(8,128)S(1)}, f32[528,1...) custom-call(f32[7,256]{1,0:T(8,128)S(1)} %bitcast.6, ...), custom_call_target="tpu_custom_call" | custom-call | flops 1 | bytes 1 | tf_op jit(solution)/shard_map/pallas_call | solution.py:465
  10.8 2.4 %collective-permute-start.1 = (f32[528,128]{1,0:T(8,128)S(1)}, f32[528,128]{1,0:T(8,128)S(1)}, u32[]{:S(2)}, u32[]{:S(2)}) collective-permute-start(f32[528,128]{1,0:T(8,128)S(1)} %get-tuple-element.60), channel_id=1, source_target_pairs={{16,8},{20,12},{24,16},{28,20},{17,9},{21,13},{25,17},{29,21},{18,... | collective-permute-start | bytes 811016 | tf_op jit(solution)/shard_map/ppermute | solution.py:368
  13.1 1.1 %collective-permute-start.5 = (f32[528,128]{1,0:T(8,128)S(1)}, f32[528,128]{1,0:T(8,128)S(1)}, u32[]{:S(2)}, u32[]{:S(2)}) collective-permute-start(f32[528,128]{1,0:T(8,128)S(1)} %get-tuple-element.68.refs_0_), channel_id=1, source_target_pairs={{0,4},{4,0},{8,12},{12,8},{16,20},{20,16},{24,28},{28,24},{1,5},{5... | collective-permute-start | bytes 811016 | tf_op jit(solution)/shard_map/ppermute | solution.py:368
  14.2 1.9 %collective-permute-start.7 = (f32[528,128]{1,0:T(8,128)S(1)}, f32[528,128]{1,0:T(8,128)S(1)}, u32[]{:S(2)}, u32[]{:S(2)}) collective-permute-start(f32[528,128]{1,0:T(8,128)S(1)} %get-tuple-element.74), channel_id=1, source_target_pairs={{16,8},{20,12},{24,16},{28,20},{17,9},{21,13},{25,17},{29,21},{18,... | collective-permute-start | bytes 811016 | tf_op jit(solution)/shard_map/ppermute | solution.py:368
  16.1 2.6 %shard_map.109 = (f32[256,512]{1,0:T(8,128)S(1)}, f32[256,512]{1,0:T(8,128)S(1)}, f32[256,512]{1,0:T(8,128)S(1)}, f32[8,256]{1,0:T(8,128)S(1)}) custom-call(f32[256,1024]{1,0:T(8,128)S(1)} %get-tuple-element.49.q_ref.refs_0_, f32[256,1024]{1,0:T(8,128)S(1)} %get-tuple-element.53.k_ref, f32[256,1024]{1,0:T(8,128)S(1)} %get-tuple-element.54.v_ref, ...), custom_call_target="tpu_custom_call" | custom-call | flops 1 | bytes 1 | tf_op jit(solution)/shard_map/pallas_call | solution.py:420
  18.7 0.1 shard_map.107.factor_ref.refs_3_
  18.8 0.1 shard_map.110.refs_0_
  18.9 3.2 %collective-permute-done.1.refs_1_.refs_2_ = f32[528,128]{1,0:T(8,128)S(1)} collective-permute-done((f32[528,128]{1,0:T(8,128)S(1)}, f32[528,128]{1,0:T(8,128)S(1)}, u32[]{:S(2)}, u32[]{:S(2)}) %collective-permute-start.1) | collective-permute-done | bytes 270368 | tf_op jit(solution)/shard_map/ppermute | solution.py:368
  22.1 0.1 shard_map.111
  22.3 0.1 collective-permute-start.3
  22.4 1.3 %collective-permute-start.4 = (f32[528,128]{1,0:T(8,128)S(1)}, f32[528,128]{1,0:T(8,128)S(1)}, u32[]{:S(2)}, u32[]{:S(2)}) collective-permute-start(f32[528,128]{1,0:T(8,128)S(1)} %shard_map.110.refs_0_), channel_id=1, source_target_pairs={{8,16},{12,20},{9,17},{13,21},{10,18},{14,22},{11,19},{15,23}} | collective-permute-start | bytes 811016 | tf_op jit(solution)/shard_map/ppermute | solution.py:368
  23.7 0.1 shard_map.118.refs_0_
  23.8 4.0 %collective-permute-done.7.refs_2_.refs_1_ = f32[528,128]{1,0:T(8,128)S(1)} collective-permute-done((f32[528,128]{1,0:T(8,128)S(1)}, f32[528,128]{1,0:T(8,128)S(1)}, u32[]{:S(2)}, u32[]{:S(2)}) %collective-permute-start.7) | collective-permute-done | bytes 270368 | tf_op jit(solution)/shard_map/ppermute | solution.py:368
  27.9 0.1 shard_map.119
  28.0 0.1 collective-permute-start.8
  28.1 1.3 %collective-permute-start.9 = (f32[528,128]{1,0:T(8,128)S(1)}, f32[528,128]{1,0:T(8,128)S(1)}, u32[]{:S(2)}, u32[]{:S(2)}) collective-permute-start(f32[528,128]{1,0:T(8,128)S(1)} %shard_map.118.refs_0_), channel_id=1, source_target_pairs={{8,16},{12,20},{9,17},{13,21},{10,18},{14,22},{11,19},{15,23}} | collective-permute-start | bytes 811016 | tf_op jit(solution)/shard_map/ppermute | solution.py:368
  29.4 4.6 %collective-permute-start.11 = (f32[528,128]{1,0:T(8,128)S(1)}, f32[528,128]{1,0:T(8,128)S(1)}, u32[]{:S(2)}, u32[]{:S(2)}) collective-permute-start(f32[528,128]{1,0:T(8,128)S(1)} %collective-permute-done.1.refs_1_.refs_2_), channel_id=1, source_target_pairs={{16,8},{20,12},{17,9},{21,13},{18,10},{22,14},{19,11},{23,15}} | collective-permute-start | bytes 811016 | tf_op jit(solution)/shard_map/ppermute | solution.py:368
  34.0 1.3 %collective-permute-start.12 = (f32[528,128]{1,0:T(8,128)S(1)}, f32[528,128]{1,0:T(8,128)S(1)}, u32[]{:S(2)}, u32[]{:S(2)}) collective-permute-start(f32[528,128]{1,0:T(8,128)S(1)} %collective-permute-done.7.refs_2_.refs_1_), channel_id=1, source_target_pairs={{16,8},{20,12},{17,9},{21,13},{18,10},{22,14},{19,11},{23,15}} | collective-permute-start | bytes 811016 | tf_op jit(solution)/shard_map/ppermute | solution.py:368
  35.3 0.7 %shard_map.113 = (f32[256,512]{1,0:T(8,128)S(1)}, f32[8,256]{1,0:T(8,128)S(1)}) custom-call(f32[256,1024]{1,0:T(8,128)S(1)} %get-tuple-element.49.q_ref.refs_0_, f32[256,1024]{1,0:T(8,128)S(1)} %get-tuple-element.58.refs_1_, f32[3,256,128]{2,1,0:T(8,128)S(1)} %get-tuple-element.59.refs_2_, f32[16,128]{1,0:T(8,128)S(1)} %shard_map.107.factor_ref.refs_3_, ...), custom_call_target="tpu_custom_call" | custom-call | flops 1 | bytes 1 | tf_op jit(solution)/shard_map/pallas_call | solution.py:497
  36.0 0.8 %shard_map.114 = (f32[256,512]{1,0:T(8,128)S(1)}, f32[8,256]{1,0:T(8,128)S(1)}) custom-call(f32[256,1024]{1,0:T(8,128)S(1)} %get-tuple-element.49.q_ref.refs_0_, f32[256,1024]{1,0:T(8,128)S(1)} %get-tuple-element.58.refs_1_, f32[3,256,128]{2,1,0:T(8,128)S(1)} %get-tuple-element.59.refs_2_, f32[16,128]{1,0:T(8,128)S(1)} %shard_map.107.factor_ref.refs_3_, ...), custom_call_target="tpu_custom_call" | custom-call | flops 1 | bytes 1 | tf_op jit(solution)/shard_map/pallas_call | solution.py:497
  36.9 0.1 shard_map.112.factor_ref.refs_3_
  36.9 0.1 shard_map.115
  37.1 1.9 %collective-permute-start.6 = (f32[528,128]{1,0:T(8,128)S(1)}, f32[528,128]{1,0:T(8,128)S(1)}, u32[]{:S(2)}, u32[]{:S(2)}) collective-permute-start(f32[528,128]{1,0:T(8,128)S(1)} %shard_map.115), channel_id=1, source_target_pairs={{8,16},{12,20},{16,24},{20,28},{9,17},{13,21},{17,25},{21,29},{10,... | collective-permute-start | bytes 811016 | tf_op jit(solution)/shard_map/ppermute | solution.py:368
  39.0 0.1 shard_map.122
  39.2 1.9 %collective-permute-start.10 = (f32[528,128]{1,0:T(8,128)S(1)}, f32[528,128]{1,0:T(8,128)S(1)}, u32[]{:S(2)}, u32[]{:S(2)}) collective-permute-start(f32[528,128]{1,0:T(8,128)S(1)} %shard_map.122), channel_id=1, source_target_pairs={{8,16},{12,20},{16,24},{20,28},{9,17},{13,21},{17,25},{21,29},{10,... | collective-permute-start | bytes 811016 | tf_op jit(solution)/shard_map/ppermute | solution.py:368
  41.1 0.3 shard_map.124.factor_ref
  41.4 0.1 shard_map.127.refs_0_.kept_ref
  41.6 0.1 shard_map.128
  41.7 1.1 %collective-permute-start.14 = (f32[528,128]{1,0:T(8,128)S(1)}, f32[528,128]{1,0:T(8,128)S(1)}, u32[]{:S(2)}, u32[]{:S(2)}) collective-permute-start(f32[528,128]{1,0:T(8,128)S(1)} %shard_map.128), channel_id=1, source_target_pairs={{0,4},{4,0},{8,12},{12,8},{16,20},{20,16},{24,28},{28,24},{1,5},{5... | collective-permute-start | bytes 811016 | tf_op jit(solution)/shard_map/ppermute | solution.py:368
  42.8 0.2 shard_map.125.refs_0_.kept_ref
  42.9 0.1 shard_map.126
  43.1 1.1 %collective-permute-start.13 = (f32[528,128]{1,0:T(8,128)S(1)}, f32[528,128]{1,0:T(8,128)S(1)}, u32[]{:S(2)}, u32[]{:S(2)}) collective-permute-start(f32[528,128]{1,0:T(8,128)S(1)} %shard_map.126), channel_id=1, source_target_pairs={{0,4},{4,0},{8,12},{12,8},{16,20},{20,16},{24,28},{28,24},{1,5},{5... | collective-permute-start | bytes 811016 | tf_op jit(solution)/shard_map/ppermute | solution.py:368
  44.2 0.7 %shard_map.117 = (f32[256,512]{1,0:T(8,128)S(1)}, f32[8,256]{1,0:T(8,128)S(1)}) custom-call(f32[256,1024]{1,0:T(8,128)S(1)} %get-tuple-element.49.q_ref.refs_0_, f32[256,1024]{1,0:T(8,128)S(1)} %get-tuple-element.58.refs_1_, f32[3,256,128]{2,1,0:T(8,128)S(1)} %get-tuple-element.59.refs_2_, f32[16,128]{1,0:T(8,128)S(1)} %shard_map.112.factor_ref.refs_3_, ...), custom_call_target="tpu_custom_call" | custom-call | flops 1 | bytes 1 | tf_op jit(solution)/shard_map/pallas_call | solution.py:497
  44.9 0.8 %shard_map.120 = (f32[256,512]{1,0:T(8,128)S(1)}, f32[8,256]{1,0:T(8,128)S(1)}) custom-call(f32[256,1024]{1,0:T(8,128)S(1)} %get-tuple-element.49.q_ref.refs_0_, f32[256,1024]{1,0:T(8,128)S(1)} %get-tuple-element.58.refs_1_, f32[3,256,128]{2,1,0:T(8,128)S(1)} %get-tuple-element.59.refs_2_, f32[16,128]{1,0:T(8,128)S(1)} %shard_map.112.factor_ref.refs_3_, ...), custom_call_target="tpu_custom_call" | custom-call | flops 1 | bytes 1 | tf_op jit(solution)/shard_map/pallas_call | solution.py:497
  45.7 0.6 %collective-permute-done.6.refs_1_.refs_6_ = f32[528,128]{1,0:T(8,128)S(1)} collective-permute-done((f32[528,128]{1,0:T(8,128)S(1)}, f32[528,128]{1,0:T(8,128)S(1)}, u32[]{:S(2)}, u32[]{:S(2)}) %collective-permute-start.6) | collective-permute-done | bytes 270368 | tf_op jit(solution)/shard_map/ppermute | solution.py:368
  46.4 1.4 %shard_map.121 = (f32[256,1024]{1,0:T(8,128)}, f32[8,256]{1,0:T(8,128)S(1)}) custom-call(f32[256,1024]{1,0:T(8,128)S(1)} %get-tuple-element.49.q_ref.refs_0_, f32[256,1024]{1,0:T(8,128)S(1)} %get-tuple-element.58.refs_1_, f32[3,256,128]{2,1,0:T(8,128)S(1)} %get-tuple-element.59.refs_2_, f32[16,128]{1,0:T(8,128)S(1)} %shard_map.116.refs_3_, ...), custom_call_target="tpu_custom_call" | custom-call | flops 1 | bytes 1 | tf_op jit(solution)/shard_map/pallas_call | solution.py:497
  47.7 1.5 %collective-permute-done.10.refs_6_ = f32[528,128]{1,0:T(8,128)S(1)} collective-permute-done((f32[528,128]{1,0:T(8,128)S(1)}, f32[528,128]{1,0:T(8,128)S(1)}, u32[]{:S(2)}, u32[]{:S(2)}) %collective-permute-start.10) | collective-permute-done | bytes 270368 | tf_op jit(solution)/shard_map/ppermute | solution.py:368
  49.2 1.4 %shard_map.123 = (f32[256,1024]{1,0:T(8,128)}, f32[8,256]{1,0:T(8,128)S(1)}) custom-call(f32[256,1024]{1,0:T(8,128)S(1)} %get-tuple-element.49.q_ref.refs_0_, f32[256,1024]{1,0:T(8,128)S(1)} %get-tuple-element.58.refs_1_, f32[3,256,128]{2,1,0:T(8,128)S(1)} %get-tuple-element.59.refs_2_, ...), custom_call_target="tpu_custom_call", output_to_operand_aliasing={{0}: (7, {})} | custom-call | flops 1 | bytes 1 | tf_op jit(solution)/shard_map/pallas_call | solution.py:497
  50.7 1.6 %collective-permute-start.16 = (f32[8,256]{1,0:T(8,128)S(1)}, f32[8,256]{1,0:T(8,128)S(1)}, u32[]{:S(2)}, u32[]{:S(2)}) collective-permute-start(f32[8,256]{1,0:T(8,128)S(1)} %get-tuple-element.93.refs_0_), channel_id=1, source_target_pairs={{0,2},{1,3},{2,0},{3,1},{4,6},{5,7},{6,4},{7,5},{8,10},{9,11},{10,... | collective-permute-start | bytes 24584 | tf_op jit(solution)/shard_map/ppermute | solution.py:609
  52.3 1.4 %collective-permute-start.17 = (f32[8,256]{1,0:T(8,128)S(1)}, f32[8,256]{1,0:T(8,128)S(1)}, u32[]{:S(2)}, u32[]{:S(2)}) collective-permute-start(f32[8,256]{1,0:T(8,128)S(1)} %get-tuple-element.93.refs_0_), channel_id=1, source_target_pairs={{0,3},{1,0},{2,1},{3,2},{4,7},{5,4},{6,5},{7,6},{8,11},{9,8},{10,9... | collective-permute-start | bytes 24584 | tf_op jit(solution)/shard_map/ppermute | solution.py:609
  53.6 1.4 %shard_map.129 = (f32[256,1024]{1,0:T(8,128)}, f32[256,1024]{1,0:T(8,128)}) custom-call(s32[1]{0:T(128)} %bitcast.device_ref, f32[256,1024]{1,0:T(8,128)S(1)} %get-tuple-element.81.wk_ref, f32[256,1024]{1,0:T(8,128)S(1)} %get-tuple-element.82.wv_ref, f32[16,128]{1,0:T(8,128)S(1)} %shard_map.107.factor_ref.refs_3_, ...), custom_call_target="tpu_custom_call" | custom-call | flops 1 | bytes 1 | tf_op jit(solution)/shard_map/pallas_call | solution.py:614
  55.1 1.5 %shard_map.130 = (f32[256,1024]{1,0:T(8,128)}, f32[256,1024]{1,0:T(8,128)}) custom-call(s32[1]{0:T(128)} %bitcast.device_ref, f32[256,1024]{1,0:T(8,128)S(1)} %get-tuple-element.81.wk_ref, f32[256,1024]{1,0:T(8,128)S(1)} %get-tuple-element.82.wv_ref, f32[16,128]{1,0:T(8,128)S(1)} %shard_map.107.factor_ref.refs_3_, ...), custom_call_target="tpu_custom_call", output_to_operand_aliasing={{0}: (8, {}), {1}: (9, {})} | custom-call | flops 1 | bytes 1 | tf_op jit(solution)/shard_map/pallas_call | solution.py:614
  56.6 0.6 %shard_map.131 = f32[7,256]{1,0:T(8,128)} custom-call(f32[8,256]{1,0:T(8,128)S(1)} %get-tuple-element.93.refs_0_, f32[8,256]{1,0:T(8,128)S(1)} %collective-permute-done.15.refs_1_, f32[8,256]{1,0:T(8,128)S(1)} %collective-permute-done.16.refs_2_, f32[8,256]{1,0:T(8,128)S(1)} %collective-permute-done.17.refs_3_), custom_call_target="tpu_custom_call" | custom-call | tf_op jit(solution)/shard_map/pallas_call | solution.py:629
  (20 shorter events, 0.2 us)
Async XLA Ops:
  2.9 1.6 %copy-start = (f32[256,7]{0,1:T(8,128)S(1)}, f32[256,7]{0,1:T(8,128)}, u32[]{:S(2)}) copy-start(f32[256,7]{0,1:T(8,128)} %param.12) | copy-start | bytes 21508
  2.9 4.1 %collective-permute-start = (f32[8,128]{1,0:T(8,128)S(1)}, f32[8,128]{1,0:T(8,128)S(1)}, u32[]{:S(2)}, u32[]{:S(2)}) collective-permute-start(f32[8,128]{1,0:T(8,128)S(1)} %get-tuple-element.52.own_ref), channel_id=1, source_target_pairs={{0,4},{4,0},{8,12},{12,8},{16,20},{20,16},{24,28},{28,24},{1,5},{5... | collective-permute-start | bytes 12296 | tf_op jit(solution)/shard_map/ppermute | solution.py:368
  8.0 10.7 %collective-permute-start.2 = (f32[528,128]{1,0:T(8,128)S(1)}, f32[528,128]{1,0:T(8,128)S(1)}, u32[]{:S(2)}, u32[]{:S(2)}) collective-permute-start(f32[528,128]{1,0:T(8,128)S(1)} %get-tuple-element.62.refs_0_), channel_id=1, source_target_pairs={{0,4},{4,0},{8,12},{12,8},{16,20},{20,16},{24,28},{28,24},{1,5},{5... | collective-permute-start | bytes 811016 | tf_op jit(solution)/shard_map/ppermute | solution.py:368
  10.8 11.3 %collective-permute-start.1 = (f32[528,128]{1,0:T(8,128)S(1)}, f32[528,128]{1,0:T(8,128)S(1)}, u32[]{:S(2)}, u32[]{:S(2)}) collective-permute-start(f32[528,128]{1,0:T(8,128)S(1)} %get-tuple-element.60), channel_id=1, source_target_pairs={{16,8},{20,12},{24,16},{28,20},{17,9},{21,13},{25,17},{29,21},{18,... | collective-permute-start | bytes 811016 | tf_op jit(solution)/shard_map/ppermute | solution.py:368
  13.1 10.5 %collective-permute-start.5 = (f32[528,128]{1,0:T(8,128)S(1)}, f32[528,128]{1,0:T(8,128)S(1)}, u32[]{:S(2)}, u32[]{:S(2)}) collective-permute-start(f32[528,128]{1,0:T(8,128)S(1)} %get-tuple-element.68.refs_0_), channel_id=1, source_target_pairs={{0,4},{4,0},{8,12},{12,8},{16,20},{20,16},{24,28},{28,24},{1,5},{5... | collective-permute-start | bytes 811016 | tf_op jit(solution)/shard_map/ppermute | solution.py:368
  14.2 13.7 %collective-permute-start.7 = (f32[528,128]{1,0:T(8,128)S(1)}, f32[528,128]{1,0:T(8,128)S(1)}, u32[]{:S(2)}, u32[]{:S(2)}) collective-permute-start(f32[528,128]{1,0:T(8,128)S(1)} %get-tuple-element.74), channel_id=1, source_target_pairs={{16,8},{20,12},{24,16},{28,20},{17,9},{21,13},{25,17},{29,21},{18,... | collective-permute-start | bytes 811016 | tf_op jit(solution)/shard_map/ppermute | solution.py:368
  22.3 11.7 %collective-permute-start.3 = (f32[528,128]{1,0:T(8,128)S(1)}, f32[528,128]{1,0:T(8,128)S(1)}, u32[]{:S(2)}, u32[]{:S(2)}) collective-permute-start(f32[528,128]{1,0:T(8,128)S(1)} %shard_map.111), channel_id=1, source_target_pairs={{0,8},{4,12},{8,0},{12,4},{16,24},{20,28},{24,16},{28,20},{1,9},{5... | collective-permute-start | bytes 811016 | tf_op jit(solution)/shard_map/ppermute | solution.py:368
  22.4 14.6 %collective-permute-start.4 = (f32[528,128]{1,0:T(8,128)S(1)}, f32[528,128]{1,0:T(8,128)S(1)}, u32[]{:S(2)}, u32[]{:S(2)}) collective-permute-start(f32[528,128]{1,0:T(8,128)S(1)} %shard_map.110.refs_0_), channel_id=1, source_target_pairs={{8,16},{12,20},{9,17},{13,21},{10,18},{14,22},{11,19},{15,23}} | collective-permute-start | bytes 811016 | tf_op jit(solution)/shard_map/ppermute | solution.py:368
  28.0 11.0 %collective-permute-start.8 = (f32[528,128]{1,0:T(8,128)S(1)}, f32[528,128]{1,0:T(8,128)S(1)}, u32[]{:S(2)}, u32[]{:S(2)}) collective-permute-start(f32[528,128]{1,0:T(8,128)S(1)} %shard_map.119), channel_id=1, source_target_pairs={{0,8},{4,12},{8,0},{12,4},{16,24},{20,28},{24,16},{28,20},{1,9},{5... | collective-permute-start | bytes 811016 | tf_op jit(solution)/shard_map/ppermute | solution.py:368
  28.1 10.9 %collective-permute-start.9 = (f32[528,128]{1,0:T(8,128)S(1)}, f32[528,128]{1,0:T(8,128)S(1)}, u32[]{:S(2)}, u32[]{:S(2)}) collective-permute-start(f32[528,128]{1,0:T(8,128)S(1)} %shard_map.118.refs_0_), channel_id=1, source_target_pairs={{8,16},{12,20},{9,17},{13,21},{10,18},{14,22},{11,19},{15,23}} | collective-permute-start | bytes 811016 | tf_op jit(solution)/shard_map/ppermute | solution.py:368
  29.4 11.7 %collective-permute-start.11 = (f32[528,128]{1,0:T(8,128)S(1)}, f32[528,128]{1,0:T(8,128)S(1)}, u32[]{:S(2)}, u32[]{:S(2)}) collective-permute-start(f32[528,128]{1,0:T(8,128)S(1)} %collective-permute-done.1.refs_1_.refs_2_), channel_id=1, source_target_pairs={{16,8},{20,12},{17,9},{21,13},{18,10},{22,14},{19,11},{23,15}} | collective-permute-start | bytes 811016 | tf_op jit(solution)/shard_map/ppermute | solution.py:368
  34.0 8.8 %collective-permute-start.12 = (f32[528,128]{1,0:T(8,128)S(1)}, f32[528,128]{1,0:T(8,128)S(1)}, u32[]{:S(2)}, u32[]{:S(2)}) collective-permute-start(f32[528,128]{1,0:T(8,128)S(1)} %collective-permute-done.7.refs_2_.refs_1_), channel_id=1, source_target_pairs={{16,8},{20,12},{17,9},{21,13},{18,10},{22,14},{19,11},{23,15}} | collective-permute-start | bytes 811016 | tf_op jit(solution)/shard_map/ppermute | solution.py:368
  37.1 9.2 %collective-permute-start.6 = (f32[528,128]{1,0:T(8,128)S(1)}, f32[528,128]{1,0:T(8,128)S(1)}, u32[]{:S(2)}, u32[]{:S(2)}) collective-permute-start(f32[528,128]{1,0:T(8,128)S(1)} %shard_map.115), channel_id=1, source_target_pairs={{8,16},{12,20},{16,24},{20,28},{9,17},{13,21},{17,25},{21,29},{10,... | collective-permute-start | bytes 811016 | tf_op jit(solution)/shard_map/ppermute | solution.py:368
  39.2 10.0 %collective-permute-start.10 = (f32[528,128]{1,0:T(8,128)S(1)}, f32[528,128]{1,0:T(8,128)S(1)}, u32[]{:S(2)}, u32[]{:S(2)}) collective-permute-start(f32[528,128]{1,0:T(8,128)S(1)} %shard_map.122), channel_id=1, source_target_pairs={{8,16},{12,20},{16,24},{20,28},{9,17},{13,21},{17,25},{21,29},{10,... | collective-permute-start | bytes 811016 | tf_op jit(solution)/shard_map/ppermute | solution.py:368
  41.7 11.9 %collective-permute-start.14 = (f32[528,128]{1,0:T(8,128)S(1)}, f32[528,128]{1,0:T(8,128)S(1)}, u32[]{:S(2)}, u32[]{:S(2)}) collective-permute-start(f32[528,128]{1,0:T(8,128)S(1)} %shard_map.128), channel_id=1, source_target_pairs={{0,4},{4,0},{8,12},{12,8},{16,20},{20,16},{24,28},{28,24},{1,5},{5... | collective-permute-start | bytes 811016 | tf_op jit(solution)/shard_map/ppermute | solution.py:368
  43.1 12.0 %collective-permute-start.13 = (f32[528,128]{1,0:T(8,128)S(1)}, f32[528,128]{1,0:T(8,128)S(1)}, u32[]{:S(2)}, u32[]{:S(2)}) collective-permute-start(f32[528,128]{1,0:T(8,128)S(1)} %shard_map.126), channel_id=1, source_target_pairs={{0,4},{4,0},{8,12},{12,8},{16,20},{20,16},{24,28},{28,24},{1,5},{5... | collective-permute-start | bytes 811016 | tf_op jit(solution)/shard_map/ppermute | solution.py:368
  50.6 6.0 %collective-permute-start.15 = (f32[8,256]{1,0:T(8,128)S(1)}, f32[8,256]{1,0:T(8,128)S(1)}, u32[]{:S(2)}, u32[]{:S(2)}) collective-permute-start(f32[8,256]{1,0:T(8,128)S(1)} %get-tuple-element.93.refs_0_), channel_id=1, source_target_pairs={{0,1},{1,2},{2,3},{3,0},{4,5},{5,6},{6,7},{7,4},{8,9},{9,10},{10,1... | collective-permute-start | bytes 24584 | tf_op jit(solution)/shard_map/ppermute | solution.py:609
  50.7 5.9 %collective-permute-start.16 = (f32[8,256]{1,0:T(8,128)S(1)}, f32[8,256]{1,0:T(8,128)S(1)}, u32[]{:S(2)}, u32[]{:S(2)}) collective-permute-start(f32[8,256]{1,0:T(8,128)S(1)} %get-tuple-element.93.refs_0_), channel_id=1, source_target_pairs={{0,2},{1,3},{2,0},{3,1},{4,6},{5,7},{6,4},{7,5},{8,10},{9,11},{10,... | collective-permute-start | bytes 24584 | tf_op jit(solution)/shard_map/ppermute | solution.py:609
  52.3 4.4 %collective-permute-start.17 = (f32[8,256]{1,0:T(8,128)S(1)}, f32[8,256]{1,0:T(8,128)S(1)}, u32[]{:S(2)}, u32[]{:S(2)}) collective-permute-start(f32[8,256]{1,0:T(8,128)S(1)} %get-tuple-element.93.refs_0_), channel_id=1, source_target_pairs={{0,3},{1,0},{2,1},{3,2},{4,7},{5,4},{6,5},{7,6},{8,11},{9,8},{10,9... | collective-permute-start | bytes 24584 | tf_op jit(solution)/shard_map/ppermute | solution.py:609

commit v5 on v4

--- a/solution.py
+++ b/solution.py
@@ -543,7 +543,7 @@
                 [terms],
             )
     after_shift = factors(("next", shifted[0]))
-    crossed, relayed, passed = [], [], []
+    crossed, middle = [], []
     for p in parts:
         message = blend(
             p,
@@ -555,15 +555,20 @@
             ],
         )
         crossed.append(send(message, swaps[next_bit]))
-        relayed.append(send(shifted[p], third_second))
-        passed.append(send(running[p], second_third))
+        payload = blend(
+            p,
+            after_shift,
+            [(running[p], quarter_flag(top, 1)), (shifted[p], quarter_flag(top, 2))],
+            relay=1,
+        )
+        middle.append(send(payload, second_third + third_second))
     if depth > 2:
         for p in parts:
             gq[p], terms = add_levels(
                 list(range(1, depth - 1)), p, inside, gq[p], terms, came[p]
             )
     after_cross = factors(("next", shifted[0]), ("beside", crossed[0]))
-    after_relay = factors(("next", shifted[0]), ("over", relayed[0]), ("beside", crossed[0]))
+    after_relay = factors(("next", shifted[0]), ("over", middle[0]), ("beside", crossed[0]))
     topmost, kept, sources = [], [], []
     for p in parts:
         upward = blend(
@@ -572,7 +577,7 @@
             [
                 (running[p], quarter_flag(top, 1)),
                 (crossed[p], quarter_flag(top, 1, block_row(next_bit))),
-                (passed[p], quarter_flag(top, 2)),
+                (middle[p], quarter_flag(top, 2)),
             ],
             [terms],
             2,
@@ -581,7 +586,7 @@
         pending = blend(
             p,
             after_relay,
-            [(crossed[p], by(linked)), (shifted[p], by(third)), (relayed[p], by(fourth))],
+            [(crossed[p], by(linked)), (shifted[p], by(third)), (middle[p], by(fourth))],
         )
         for d in range(depth - 3, -1, -1):
             outgoing = blend(

time: 57.6 us -> 56.2 us (0.976)
  starting transfers between devices: 25.6 us -> 21.7 us
  waiting for transfers between devices: 9.31 us -> 11.3 us
    ppermute x15 -> x13, starting transfers between devices: 22.6 us -> 19.9 us  [send(): return lax.ppermute(array, 'seq', route)]
    ppermute x15 -> x13, waiting for transfers between devices: 9.3 us -> 11.3 us  [send(): return lax.ppermute(array, 'seq', route)]
    ppermute x3, starting transfers between devices: 3.01 us -> 1.8 us  [on_device(): lax.ppermute(terms, 'head', [(i, (i + k) % groups) for i in range(groups)])]
    pallas_call x10 -> x12, Pallas kernels: 1.45 us -> 1.53 us  [blend(): pl.pallas_call(functools.partial(blend_kernel, part * part_heads, recipe,...]
  transfers between devices with their start and end apart: 18 -> 16, of which waited for: 4 -> 5; matrix products, arithmetic and copies ran while one was open for 0% -> 0% of each run, Pallas kernels for 31% -> 32%
where the time goes in v5:
time: 56.2 us; the launch traced here: 55.3 us
  starting transfers between devices  21.7 us (39%)
  Pallas kernels  21.3 us (38%)
  waiting for transfers between devices  11.3 us (20%)
  between operations  0.97 us (2%)
    ppermute x13, starting transfers between devices, send(): return lax.ppermute(array, 'seq', route)  19.9 us
    ppermute x13, waiting for transfers between devices, send(): return lax.ppermute(array, 'seq', route)  11.3 us
    pallas_call x6, Pallas kernels, add_levels(): pl.pallas_call(functools.partial(levels_kernel, heads, p * part_heads, ch...  5.78 us
    pallas_call x2, Pallas kernels, on_device(): pl.pallas_call(functools.partial(local_kernel, heads, p * part_heads), ou...  5.14 us
    pallas_call x2, Pallas kernels, on_device(): pl.pallas_call(functools.partial(sources_kernel, heads, p * part_heads, b...  2.88 us
    pallas_call x1, Pallas kernels, on_device(): pl.pallas_call(functools.partial(first_kernel, heads), out_shape=[tall] *...  2.26 us
    ppermute x3, starting transfers between devices, on_device(): lax.ppermute(terms, 'head', [(i, (i + k) % groups) for i in range(groups)])  1.8 us
    pallas_call x1, Pallas kernels, on_device(): pl.pallas_call(functools.partial(second_kernel, heads, depth, part_heads)...  1.65 us
  transfers between devices with their start and end apart: 16, of which 5 were waited for; matrix products, arithmetic and copies ran while one was open for 0% of the time, Pallas kernels for 32%

profile of v5, /device:TPU:16, one launch (start us, length us, event | category | flops | bytes accessed | tf_op | source)
XLA Modules:
  0.0 55.3 jit_solution(9385839955216745419)
XLA Ops:
  0.6 2.3 %shard_map.102 = (f32[256,1024]{1,0:T(8,128)S(1)}, f32[256,1024]{1,0:T(8,128)S(1)}, f32[256,1024]{1,0:T(8,128)S(1)}, f32[256,1024]{1,0:T(8,128)S(1)}, f32[256,12...) custom-call(s32[1]{0:T(128)} %bitcast.device_ref, ...), custom_call_target="tpu_custom_call" | custom-call | tf_op jit(solution)/shard_map/pallas_call | solution.py:396
  2.9 1.6 %collective-permute-start = (f32[8,128]{1,0:T(8,128)S(1)}, f32[8,128]{1,0:T(8,128)S(1)}, u32[]{:S(2)}, u32[]{:S(2)}) collective-permute-start(f32[8,128]{1,0:T(8,128)S(1)} %get-tuple-element.52.own_ref), channel_id=1, source_target_pairs={{0,4},{4,0},{8,12},{12,8},{16,20},{20,16},{24,28},{28,24},{1,5},{5... | collective-permute-start | bytes 12296 | tf_op jit(solution)/shard_map/ppermute | solution.py:368
  4.5 2.6 %shard_map.103 = (f32[256,512]{1,0:T(8,128)S(1)}, f32[256,512]{1,0:T(8,128)S(1)}, f32[256,512]{1,0:T(8,128)S(1)}, f32[8,256]{1,0:T(8,128)S(1)}) custom-call(f32[256,1024]{1,0:T(8,128)S(1)} %get-tuple-element.49.q_ref.refs_0_, f32[256,1024]{1,0:T(8,128)S(1)} %get-tuple-element.53.k_ref, f32[256,1024]{1,0:T(8,128)S(1)} %get-tuple-element.54.v_ref, ...), custom_call_target="tpu_custom_call" | custom-call | flops 1 | bytes 1 | tf_op jit(solution)/shard_map/pallas_call | solution.py:420
  7.1 1.0 %shard_map.108 = (f32[256,1024]{1,0:T(8,128)S(1)}, f32[256,1024]{1,0:T(8,128)S(1)}, f32[528,128]{1,0:T(8,128)S(1)}, f32[528,128]{1,0:T(8,128)S(1)}) custom-call(f32[8,256]{1,0:T(8,128)S(1)} %get-tuple-element.61.source_ref, f32[256,1024]{1,0:T(8,128)S(1)} %get-tuple-element.53.k_ref, f32[256,1024]{1,0:T(8,128)S(1)} %get-tuple-element.54.v_ref, ...), custom_call_target="tpu_custom_call" | custom-call | flops 1 | bytes 1 | tf_op jit(solution)/shard_map/pallas_call | solution.py:455
  8.0 1.1 %collective-permute-start.2 = (f32[528,128]{1,0:T(8,128)S(1)}, f32[528,128]{1,0:T(8,128)S(1)}, u32[]{:S(2)}, u32[]{:S(2)}) collective-permute-start(f32[528,128]{1,0:T(8,128)S(1)} %get-tuple-element.62.refs_0_), channel_id=1, source_target_pairs={{0,4},{4,0},{8,12},{12,8},{16,20},{20,16},{24,28},{28,24},{1,5},{5... | collective-permute-start | bytes 811016 | tf_op jit(solution)/shard_map/ppermute | solution.py:368
  9.1 1.6 %shard_map.105 = (f32[256,1024]{1,0:T(8,128)S(1)}, f32[3,256,128]{2,1,0:T(8,128)S(1)}, f32[528,128]{1,0:T(8,128)S(1)}, f32[528,128]{1,0:T(8,128)S(1)}, f32[528,1...) custom-call(f32[7,256]{1,0:T(8,128)S(1)} %bitcast.6, ...), custom_call_target="tpu_custom_call" | custom-call | flops 1 | bytes 1 | tf_op jit(solution)/shard_map/pallas_call | solution.py:465
  10.8 2.4 %collective-permute-start.1 = (f32[528,128]{1,0:T(8,128)S(1)}, f32[528,128]{1,0:T(8,128)S(1)}, u32[]{:S(2)}, u32[]{:S(2)}) collective-permute-start(f32[528,128]{1,0:T(8,128)S(1)} %get-tuple-element.60), channel_id=1, source_target_pairs={{16,8},{20,12},{24,16},{28,20},{17,9},{21,13},{25,17},{29,21},{18,... | collective-permute-start | bytes 811016 | tf_op jit(solution)/shard_map/ppermute | solution.py:368
  13.1 1.1 %collective-permute-start.5 = (f32[528,128]{1,0:T(8,128)S(1)}, f32[528,128]{1,0:T(8,128)S(1)}, u32[]{:S(2)}, u32[]{:S(2)}) collective-permute-start(f32[528,128]{1,0:T(8,128)S(1)} %get-tuple-element.68.refs_0_), channel_id=1, source_target_pairs={{0,4},{4,0},{8,12},{12,8},{16,20},{20,16},{24,28},{28,24},{1,5},{5... | collective-permute-start | bytes 811016 | tf_op jit(solution)/shard_map/ppermute | solution.py:368
  14.2 1.9 %collective-permute-start.7 = (f32[528,128]{1,0:T(8,128)S(1)}, f32[528,128]{1,0:T(8,128)S(1)}, u32[]{:S(2)}, u32[]{:S(2)}) collective-permute-start(f32[528,128]{1,0:T(8,128)S(1)} %get-tuple-element.74), channel_id=1, source_target_pairs={{16,8},{20,12},{24,16},{28,20},{17,9},{21,13},{25,17},{29,21},{18,... | collective-permute-start | bytes 811016 | tf_op jit(solution)/shard_map/ppermute | solution.py:368
  16.1 2.6 %shard_map.109 = (f32[256,512]{1,0:T(8,128)S(1)}, f32[256,512]{1,0:T(8,128)S(1)}, f32[256,512]{1,0:T(8,128)S(1)}, f32[8,256]{1,0:T(8,128)S(1)}) custom-call(f32[256,1024]{1,0:T(8,128)S(1)} %get-tuple-element.49.q_ref.refs_0_, f32[256,1024]{1,0:T(8,128)S(1)} %get-tuple-element.53.k_ref, f32[256,1024]{1,0:T(8,128)S(1)} %get-tuple-element.54.v_ref, ...), custom_call_target="tpu_custom_call" | custom-call | flops 1 | bytes 1 | tf_op jit(solution)/shard_map/pallas_call | solution.py:420
  18.7 0.1 shard_map.107.factor_ref.refs_3_
  18.8 0.1 shard_map.110.refs_0_
  18.9 3.2 %collective-permute-done.1.refs_1_.refs_2_ = f32[528,128]{1,0:T(8,128)S(1)} collective-permute-done((f32[528,128]{1,0:T(8,128)S(1)}, f32[528,128]{1,0:T(8,128)S(1)}, u32[]{:S(2)}, u32[]{:S(2)}) %collective-permute-start.1) | collective-permute-done | bytes 270368 | tf_op jit(solution)/shard_map/ppermute | solution.py:368
  22.2 2.4 %collective-permute-start.4 = (f32[528,128]{1,0:T(8,128)S(1)}, f32[528,128]{1,0:T(8,128)S(1)}, u32[]{:S(2)}, u32[]{:S(2)}) collective-permute-start(f32[528,128]{1,0:T(8,128)S(1)} %shard_map.113), channel_id=1, source_target_pairs={{8,16},{12,20},{16,8},{20,12},{9,17},{13,21},{17,9},{21,13},{10,18... | collective-permute-start | bytes 811016 | tf_op jit(solution)/shard_map/ppermute | solution.py:368
  24.5 0.1 shard_map.111
  24.7 0.1 collective-permute-start.3
  24.8 0.1 shard_map.119.refs_0_
  24.9 2.9 %collective-permute-done.7.refs_2_.refs_1_ = f32[528,128]{1,0:T(8,128)S(1)} collective-permute-done((f32[528,128]{1,0:T(8,128)S(1)}, f32[528,128]{1,0:T(8,128)S(1)}, u32[]{:S(2)}, u32[]{:S(2)}) %collective-permute-start.7) | collective-permute-done | bytes 270368 | tf_op jit(solution)/shard_map/ppermute | solution.py:368
  27.9 2.4 %collective-permute-start.9 = (f32[528,128]{1,0:T(8,128)S(1)}, f32[528,128]{1,0:T(8,128)S(1)}, u32[]{:S(2)}, u32[]{:S(2)}) collective-permute-start(f32[528,128]{1,0:T(8,128)S(1)} %shard_map.123), channel_id=1, source_target_pairs={{8,16},{12,20},{16,8},{20,12},{9,17},{13,21},{17,9},{21,13},{10,18... | collective-permute-start | bytes 811016 | tf_op jit(solution)/shard_map/ppermute | solution.py:368
  30.3 0.2 shard_map.120
  30.4 0.1 collective-permute-start.8
  30.5 0.7 %shard_map.114 = (f32[256,512]{1,0:T(8,128)S(1)}, f32[8,256]{1,0:T(8,128)S(1)}) custom-call(f32[256,1024]{1,0:T(8,128)S(1)} %get-tuple-element.49.q_ref.refs_0_, f32[256,1024]{1,0:T(8,128)S(1)} %get-tuple-element.58.refs_1_, f32[3,256,128]{2,1,0:T(8,128)S(1)} %get-tuple-element.59.refs_2_, f32[16,128]{1,0:T(8,128)S(1)} %shard_map.107.factor_ref.refs_3_, ...), custom_call_target="tpu_custom_call" | custom-call | flops 1 | bytes 1 | tf_op jit(solution)/shard_map/pallas_call | solution.py:497
  31.2 0.8 %shard_map.115 = (f32[256,512]{1,0:T(8,128)S(1)}, f32[8,256]{1,0:T(8,128)S(1)}) custom-call(f32[256,1024]{1,0:T(8,128)S(1)} %get-tuple-element.49.q_ref.refs_0_, f32[256,1024]{1,0:T(8,128)S(1)} %get-tuple-element.58.refs_1_, f32[3,256,128]{2,1,0:T(8,128)S(1)} %get-tuple-element.59.refs_2_, f32[16,128]{1,0:T(8,128)S(1)} %shard_map.107.factor_ref.refs_3_, ...), custom_call_target="tpu_custom_call" | custom-call | flops 1 | bytes 1 | tf_op jit(solution)/shard_map/pallas_call | solution.py:497
  32.0 2.1 %collective-permute-done.3.refs_2_.refs_1_.refs_6_.refs_3_.refs_0_ = f32[528,128]{1,0:T(8,128)S(1)} collective-permute-done((f32[528,128]{1,0:T(8,128)S(1)}, f32[528,128]{1,0:T(8,128)S(1)}, u32[]{:S(2)}, u32[]{:S(2)}) %collective-permute-start.3) | collective-permute-done | bytes 270368 | tf_op jit(solution)/shard_map/ppermute | solution.py:368
  34.2 0.1 shard_map.116
  34.4 1.9 %collective-permute-start.6 = (f32[528,128]{1,0:T(8,128)S(1)}, f32[528,128]{1,0:T(8,128)S(1)}, u32[]{:S(2)}, u32[]{:S(2)}) collective-permute-start(f32[528,128]{1,0:T(8,128)S(1)} %shard_map.116), channel_id=1, source_target_pairs={{8,16},{12,20},{16,24},{20,28},{9,17},{13,21},{17,25},{21,29},{10,... | collective-permute-start | bytes 811016 | tf_op jit(solution)/shard_map/ppermute | solution.py:368
  36.3 2.1 %collective-permute-done.9.refs_2_ = f32[528,128]{1,0:T(8,128)S(1)} collective-permute-done((f32[528,128]{1,0:T(8,128)S(1)}, f32[528,128]{1,0:T(8,128)S(1)}, u32[]{:S(2)}, u32[]{:S(2)}) %collective-permute-start.9) | collective-permute-done | bytes 270368 | tf_op jit(solution)/shard_map/ppermute | solution.py:368
  38.5 0.1 shard_map.124
  38.6 3.0 %collective-permute-start.10 = (f32[528,128]{1,0:T(8,128)S(1)}, f32[528,128]{1,0:T(8,128)S(1)}, u32[]{:S(2)}, u32[]{:S(2)}) collective-permute-start(f32[528,128]{1,0:T(8,128)S(1)} %shard_map.124), channel_id=1, source_target_pairs={{8,16},{12,20},{16,24},{20,28},{9,17},{13,21},{17,25},{21,29},{10,... | collective-permute-start | bytes 811016 | tf_op jit(solution)/shard_map/ppermute | solution.py:368
  41.6 0.1 shard_map.126.factor_ref
  41.7 0.1 shard_map.129.refs_0_.kept_ref
  41.8 0.1 shard_map.130
  42.0 0.8 %collective-permute-start.12 = (f32[528,128]{1,0:T(8,128)S(1)}, f32[528,128]{1,0:T(8,128)S(1)}, u32[]{:S(2)}, u32[]{:S(2)}) collective-permute-start(f32[528,128]{1,0:T(8,128)S(1)} %shard_map.130), channel_id=1, source_target_pairs={{0,4},{4,0},{8,12},{12,8},{16,20},{20,16},{24,28},{28,24},{1,5},{5... | collective-permute-start | bytes 811016 | tf_op jit(solution)/shard_map/ppermute | solution.py:368
  42.8 0.2 shard_map.127.refs_0_.kept_ref
  43.0 0.1 shard_map.128
  43.1 1.3 %collective-permute-start.11 = (f32[528,128]{1,0:T(8,128)S(1)}, f32[528,128]{1,0:T(8,128)S(1)}, u32[]{:S(2)}, u32[]{:S(2)}) collective-permute-start(f32[528,128]{1,0:T(8,128)S(1)} %shard_map.128), channel_id=1, source_target_pairs={{0,4},{4,0},{8,12},{12,8},{16,20},{20,16},{24,28},{28,24},{1,5},{5... | collective-permute-start | bytes 811016 | tf_op jit(solution)/shard_map/ppermute | solution.py:368
  44.4 0.7 %shard_map.118 = (f32[256,512]{1,0:T(8,128)S(1)}, f32[8,256]{1,0:T(8,128)S(1)}) custom-call(f32[256,1024]{1,0:T(8,128)S(1)} %get-tuple-element.49.q_ref.refs_0_, f32[256,1024]{1,0:T(8,128)S(1)} %get-tuple-element.58.refs_1_, f32[3,256,128]{2,1,0:T(8,128)S(1)} %get-tuple-element.59.refs_2_, f32[16,128]{1,0:T(8,128)S(1)} %shard_map.112.factor_ref.refs_3_, ...), custom_call_target="tpu_custom_call" | custom-call | flops 1 | bytes 1 | tf_op jit(solution)/shard_map/pallas_call | solution.py:497
  45.2 0.8 %shard_map.121 = (f32[256,512]{1,0:T(8,128)S(1)}, f32[8,256]{1,0:T(8,128)S(1)}) custom-call(f32[256,1024]{1,0:T(8,128)S(1)} %get-tuple-element.49.q_ref.refs_0_, f32[256,1024]{1,0:T(8,128)S(1)} %get-tuple-element.58.refs_1_, f32[3,256,128]{2,1,0:T(8,128)S(1)} %get-tuple-element.59.refs_2_, f32[16,128]{1,0:T(8,128)S(1)} %shard_map.112.factor_ref.refs_3_, ...), custom_call_target="tpu_custom_call" | custom-call | flops 1 | bytes 1 | tf_op jit(solution)/shard_map/pallas_call | solution.py:497
  46.0 0.2 shard_map.117.refs_3_
  46.2 1.4 %shard_map.122 = (f32[256,1024]{1,0:T(8,128)}, f32[8,256]{1,0:T(8,128)S(1)}) custom-call(f32[256,1024]{1,0:T(8,128)S(1)} %get-tuple-element.49.q_ref.refs_0_, f32[256,1024]{1,0:T(8,128)S(1)} %get-tuple-element.58.refs_1_, f32[3,256,128]{2,1,0:T(8,128)S(1)} %get-tuple-element.59.refs_2_, f32[16,128]{1,0:T(8,128)S(1)} %shard_map.117.refs_3_, ...), custom_call_target="tpu_custom_call" | custom-call | flops 1 | bytes 1 | tf_op jit(solution)/shard_map/pallas_call | solution.py:497
  47.6 1.0 %collective-permute-done.10.refs_6_ = f32[528,128]{1,0:T(8,128)S(1)} collective-permute-done((f32[528,128]{1,0:T(8,128)S(1)}, f32[528,128]{1,0:T(8,128)S(1)}, u32[]{:S(2)}, u32[]{:S(2)}) %collective-permute-start.10) | collective-permute-done | bytes 270368 | tf_op jit(solution)/shard_map/ppermute | solution.py:368
  48.5 1.4 %shard_map.125 = (f32[256,1024]{1,0:T(8,128)}, f32[8,256]{1,0:T(8,128)S(1)}) custom-call(f32[256,1024]{1,0:T(8,128)S(1)} %get-tuple-element.49.q_ref.refs_0_, f32[256,1024]{1,0:T(8,128)S(1)} %get-tuple-element.58.refs_1_, f32[3,256,128]{2,1,0:T(8,128)S(1)} %get-tuple-element.59.refs_2_, ...), custom_call_target="tpu_custom_call", output_to_operand_aliasing={{0}: (7, {})} | custom-call | flops 1 | bytes 1 | tf_op jit(solution)/shard_map/pallas_call | solution.py:497
  50.0 0.1 collective-permute-start.15
  50.0 1.6 %collective-permute-start.14 = (f32[8,256]{1,0:T(8,128)S(1)}, f32[8,256]{1,0:T(8,128)S(1)}, u32[]{:S(2)}, u32[]{:S(2)}) collective-permute-start(f32[8,256]{1,0:T(8,128)S(1)} %get-tuple-element.93.refs_0_), channel_id=1, source_target_pairs={{0,2},{1,3},{2,0},{3,1},{4,6},{5,7},{6,4},{7,5},{8,10},{9,11},{10,... | collective-permute-start | bytes 24584 | tf_op jit(solution)/shard_map/ppermute | solution.py:614
  51.6 0.2 collective-permute-start.13
  51.8 1.4 %shard_map.131 = (f32[256,1024]{1,0:T(8,128)}, f32[256,1024]{1,0:T(8,128)}) custom-call(s32[1]{0:T(128)} %bitcast.device_ref, f32[256,1024]{1,0:T(8,128)S(1)} %get-tuple-element.81.wk_ref, f32[256,1024]{1,0:T(8,128)S(1)} %get-tuple-element.82.wv_ref, f32[16,128]{1,0:T(8,128)S(1)} %shard_map.107.factor_ref.refs_3_, ...), custom_call_target="tpu_custom_call" | custom-call | flops 1 | bytes 1 | tf_op jit(solution)/shard_map/pallas_call | solution.py:619
  53.2 1.5 %shard_map.132 = (f32[256,1024]{1,0:T(8,128)}, f32[256,1024]{1,0:T(8,128)}) custom-call(s32[1]{0:T(128)} %bitcast.device_ref, f32[256,1024]{1,0:T(8,128)S(1)} %get-tuple-element.81.wk_ref, f32[256,1024]{1,0:T(8,128)S(1)} %get-tuple-element.82.wv_ref, f32[16,128]{1,0:T(8,128)S(1)} %shard_map.107.factor_ref.refs_3_, ...), custom_call_target="tpu_custom_call", output_to_operand_aliasing={{0}: (8, {}), {1}: (9, {})} | custom-call | flops 1 | bytes 1 | tf_op jit(solution)/shard_map/pallas_call | solution.py:619
  54.7 0.6 %shard_map.133 = f32[7,256]{1,0:T(8,128)} custom-call(f32[8,256]{1,0:T(8,128)S(1)} %get-tuple-element.93.refs_0_, f32[8,256]{1,0:T(8,128)S(1)} %collective-permute-done.13.refs_1_, f32[8,256]{1,0:T(8,128)S(1)} %collective-permute-done.14.refs_2_, f32[8,256]{1,0:T(8,128)S(1)} %collective-permute-done.15.refs_3_), custom_call_target="tpu_custom_call" | custom-call | tf_op jit(solution)/shard_map/pallas_call | solution.py:634
  (18 shorter events, 0.2 us)
Async XLA Ops:
  2.9 1.6 %copy-start = (f32[256,7]{0,1:T(8,128)S(1)}, f32[256,7]{0,1:T(8,128)}, u32[]{:S(2)}) copy-start(f32[256,7]{0,1:T(8,128)} %param.12) | copy-start | bytes 21508
  2.9 4.1 %collective-permute-start = (f32[8,128]{1,0:T(8,128)S(1)}, f32[8,128]{1,0:T(8,128)S(1)}, u32[]{:S(2)}, u32[]{:S(2)}) collective-permute-start(f32[8,128]{1,0:T(8,128)S(1)} %get-tuple-element.52.own_ref), channel_id=1, source_target_pairs={{0,4},{4,0},{8,12},{12,8},{16,20},{20,16},{24,28},{28,24},{1,5},{5... | collective-permute-start | bytes 12296 | tf_op jit(solution)/shard_map/ppermute | solution.py:368
  8.0 10.7 %collective-permute-start.2 = (f32[528,128]{1,0:T(8,128)S(1)}, f32[528,128]{1,0:T(8,128)S(1)}, u32[]{:S(2)}, u32[]{:S(2)}) collective-permute-start(f32[528,128]{1,0:T(8,128)S(1)} %get-tuple-element.62.refs_0_), channel_id=1, source_target_pairs={{0,4},{4,0},{8,12},{12,8},{16,20},{20,16},{24,28},{28,24},{1,5},{5... | collective-permute-start | bytes 811016 | tf_op jit(solution)/shard_map/ppermute | solution.py:368
  10.8 11.3 %collective-permute-start.1 = (f32[528,128]{1,0:T(8,128)S(1)}, f32[528,128]{1,0:T(8,128)S(1)}, u32[]{:S(2)}, u32[]{:S(2)}) collective-permute-start(f32[528,128]{1,0:T(8,128)S(1)} %get-tuple-element.60), channel_id=1, source_target_pairs={{16,8},{20,12},{24,16},{28,20},{17,9},{21,13},{25,17},{29,21},{18,... | collective-permute-start | bytes 811016 | tf_op jit(solution)/shard_map/ppermute | solution.py:368
  13.1 11.6 %collective-permute-start.5 = (f32[528,128]{1,0:T(8,128)S(1)}, f32[528,128]{1,0:T(8,128)S(1)}, u32[]{:S(2)}, u32[]{:S(2)}) collective-permute-start(f32[528,128]{1,0:T(8,128)S(1)} %get-tuple-element.68.refs_0_), channel_id=1, source_target_pairs={{0,4},{4,0},{8,12},{12,8},{16,20},{20,16},{24,28},{28,24},{1,5},{5... | collective-permute-start | bytes 811016 | tf_op jit(solution)/shard_map/ppermute | solution.py:368
  14.2 13.7 %collective-permute-start.7 = (f32[528,128]{1,0:T(8,128)S(1)}, f32[528,128]{1,0:T(8,128)S(1)}, u32[]{:S(2)}, u32[]{:S(2)}) collective-permute-start(f32[528,128]{1,0:T(8,128)S(1)} %get-tuple-element.74), channel_id=1, source_target_pairs={{16,8},{20,12},{24,16},{28,20},{17,9},{21,13},{25,17},{29,21},{18,... | collective-permute-start | bytes 811016 | tf_op jit(solution)/shard_map/ppermute | solution.py:368
  22.2 12.1 %collective-permute-start.4 = (f32[528,128]{1,0:T(8,128)S(1)}, f32[528,128]{1,0:T(8,128)S(1)}, u32[]{:S(2)}, u32[]{:S(2)}) collective-permute-start(f32[528,128]{1,0:T(8,128)S(1)} %shard_map.113), channel_id=1, source_target_pairs={{8,16},{12,20},{16,8},{20,12},{9,17},{13,21},{17,9},{21,13},{10,18... | collective-permute-start | bytes 811016 | tf_op jit(solution)/shard_map/ppermute | solution.py:368
  24.7 9.5 %collective-permute-start.3 = (f32[528,128]{1,0:T(8,128)S(1)}, f32[528,128]{1,0:T(8,128)S(1)}, u32[]{:S(2)}, u32[]{:S(2)}) collective-permute-start(f32[528,128]{1,0:T(8,128)S(1)} %shard_map.111), channel_id=1, source_target_pairs={{0,8},{4,12},{8,0},{12,4},{16,24},{20,28},{24,16},{28,20},{1,9},{5... | collective-permute-start | bytes 811016 | tf_op jit(solution)/shard_map/ppermute | solution.py:368
  27.9 10.6 %collective-permute-start.9 = (f32[528,128]{1,0:T(8,128)S(1)}, f32[528,128]{1,0:T(8,128)S(1)}, u32[]{:S(2)}, u32[]{:S(2)}) collective-permute-start(f32[528,128]{1,0:T(8,128)S(1)} %shard_map.123), channel_id=1, source_target_pairs={{8,16},{12,20},{16,8},{20,12},{9,17},{13,21},{17,9},{21,13},{10,18... | collective-permute-start | bytes 811016 | tf_op jit(solution)/shard_map/ppermute | solution.py:368
  30.4 8.0 %collective-permute-start.8 = (f32[528,128]{1,0:T(8,128)S(1)}, f32[528,128]{1,0:T(8,128)S(1)}, u32[]{:S(2)}, u32[]{:S(2)}) collective-permute-start(f32[528,128]{1,0:T(8,128)S(1)} %shard_map.120), channel_id=1, source_target_pairs={{0,8},{4,12},{8,0},{12,4},{16,24},{20,28},{24,16},{28,20},{1,9},{5... | collective-permute-start | bytes 811016 | tf_op jit(solution)/shard_map/ppermute | solution.py:368
  34.4 11.6 %collective-permute-start.6 = (f32[528,128]{1,0:T(8,128)S(1)}, f32[528,128]{1,0:T(8,128)S(1)}, u32[]{:S(2)}, u32[]{:S(2)}) collective-permute-start(f32[528,128]{1,0:T(8,128)S(1)} %shard_map.116), channel_id=1, source_target_pairs={{8,16},{12,20},{16,24},{20,28},{9,17},{13,21},{17,25},{21,29},{10,... | collective-permute-start | bytes 811016 | tf_op jit(solution)/shard_map/ppermute | solution.py:368
  38.6 9.9 %collective-permute-start.10 = (f32[528,128]{1,0:T(8,128)S(1)}, f32[528,128]{1,0:T(8,128)S(1)}, u32[]{:S(2)}, u32[]{:S(2)}) collective-permute-start(f32[528,128]{1,0:T(8,128)S(1)} %shard_map.124), channel_id=1, source_target_pairs={{8,16},{12,20},{16,24},{20,28},{9,17},{13,21},{17,25},{21,29},{10,... | collective-permute-start | bytes 811016 | tf_op jit(solution)/shard_map/ppermute | solution.py:368
  42.0 9.8 %collective-permute-start.12 = (f32[528,128]{1,0:T(8,128)S(1)}, f32[528,128]{1,0:T(8,128)S(1)}, u32[]{:S(2)}, u32[]{:S(2)}) collective-permute-start(f32[528,128]{1,0:T(8,128)S(1)} %shard_map.130), channel_id=1, source_target_pairs={{0,4},{4,0},{8,12},{12,8},{16,20},{20,16},{24,28},{28,24},{1,5},{5... | collective-permute-start | bytes 811016 | tf_op jit(solution)/shard_map/ppermute | solution.py:368
  43.1 10.1 %collective-permute-start.11 = (f32[528,128]{1,0:T(8,128)S(1)}, f32[528,128]{1,0:T(8,128)S(1)}, u32[]{:S(2)}, u32[]{:S(2)}) collective-permute-start(f32[528,128]{1,0:T(8,128)S(1)} %shard_map.128), channel_id=1, source_target_pairs={{0,4},{4,0},{8,12},{12,8},{16,20},{20,16},{24,28},{28,24},{1,5},{5... | collective-permute-start | bytes 811016 | tf_op jit(solution)/shard_map/ppermute | solution.py:368
  50.0 4.7 %collective-permute-start.15 = (f32[8,256]{1,0:T(8,128)S(1)}, f32[8,256]{1,0:T(8,128)S(1)}, u32[]{:S(2)}, u32[]{:S(2)}) collective-permute-start(f32[8,256]{1,0:T(8,128)S(1)} %get-tuple-element.93.refs_0_), channel_id=1, source_target_pairs={{0,3},{1,0},{2,1},{3,2},{4,7},{5,4},{6,5},{7,6},{8,11},{9,8},{10,9... | collective-permute-start | bytes 24584 | tf_op jit(solution)/shard_map/ppermute | solution.py:614
  50.0 4.7 %collective-permute-start.14 = (f32[8,256]{1,0:T(8,128)S(1)}, f32[8,256]{1,0:T(8,128)S(1)}, u32[]{:S(2)}, u32[]{:S(2)}) collective-permute-start(f32[8,256]{1,0:T(8,128)S(1)} %get-tuple-element.93.refs_0_), channel_id=1, source_target_pairs={{0,2},{1,3},{2,0},{3,1},{4,6},{5,7},{6,4},{7,5},{8,10},{9,11},{10,... | collective-permute-start | bytes 24584 | tf_op jit(solution)/shard_map/ppermute | solution.py:614
  51.6 3.1 %collective-permute-start.13 = (f32[8,256]{1,0:T(8,128)S(1)}, f32[8,256]{1,0:T(8,128)S(1)}, u32[]{:S(2)}, u32[]{:S(2)}) collective-permute-start(f32[8,256]{1,0:T(8,128)S(1)} %get-tuple-element.93.refs_0_), channel_id=1, source_target_pairs={{0,1},{1,2},{2,3},{3,0},{4,5},{5,6},{6,7},{7,4},{8,9},{9,10},{10,1... | collective-permute-start | bytes 24584 | tf_op jit(solution)/shard_map/ppermute | solution.py:614

commit v6 on v5

--- a/solution.py
+++ b/solution.py
@@ -609,11 +609,6 @@
         grad_query, terms = add_levels(
             [depth], p, after_top, gq[p], terms, [topmost[p]], grad_query, True
         )
-    groups = lax.axis_size("head")
-    others = [
-        lax.ppermute(terms, "head", [(i, (i + k) % groups) for i in range(groups)])
-        for k in range(1, groups)
-    ]
     done = []
     for p in parts:
         done = pl.pallas_call(
@@ -631,13 +626,18 @@
             *map(near, (weighted_k, weighted_v, inside, kept[p], sources[p], gk[p], gv[p])),
             *done,
         )
-    grad_level = pl.pallas_call(
-        total_kernel,
-        out_shape=shape(levels, tokens),
-        in_specs=[WHOLE] * groups,
-        out_specs=WHOLE,
-        compiler_params=params(),
-    )(terms, *others)
+    groups = lax.axis_size("head")
+    bits = groups.bit_length() - 1
+    grad_level = terms
+    for bit in range(bits):
+        other = lax.ppermute(grad_level, "head", [(i, i ^ (1 << bit)) for i in range(groups)])
+        grad_level = pl.pallas_call(
+            total_kernel,
+            out_shape=shape(levels if bit == bits - 1 else turned_rows, tokens),
+            in_specs=[WHOLE] * 2,
+            out_specs=WHOLE,
+            compiler_params=params(),
+        )(grad_level, other)
     return grad_query, done[0], done[1], grad_level.T
 
 

time: 56.2 us -> 56.6 us (level)
  waiting for transfers between devices: 11.3 us -> 12.5 us
    ppermute x3 -> x2, waiting for transfers between devices: 0.01 us -> 1.16 us  [on_device(): lax.ppermute(grad_level, 'head', [(i, i ^ 1 << bit) for i in range(groups)])]
    ppermute x3 -> x2, starting transfers between devices: 1.8 us -> 1.58 us  [on_device(): lax.ppermute(grad_level, 'head', [(i, i ^ 1 << bit) for i in range(groups)])]
  transfers between devices with their start and end apart: 16 -> 15, of which waited for: 5 -> 6; matrix products, arithmetic and copies ran while one was open for 0% -> 0% of each run, Pallas kernels for 32% -> 31%
where the time goes in v6:
time: 56.6 us; the launch traced here: 56.2 us
  starting transfers between devices  21.5 us (38%)
  Pallas kernels  21.3 us (38%)
  waiting for transfers between devices  12.5 us (22%)
  between operations  0.95 us (2%)
    ppermute x13, starting transfers between devices, send(): return lax.ppermute(array, 'seq', route)  19.9 us
    ppermute x13, waiting for transfers between devices, send(): return lax.ppermute(array, 'seq', route)  11.3 us
    pallas_call x6, Pallas kernels, add_levels(): pl.pallas_call(functools.partial(levels_kernel, heads, p * part_heads, ch...  5.78 us
    pallas_call x2, Pallas kernels, on_device(): pl.pallas_call(functools.partial(local_kernel, heads, p * part_heads), ou...  5.14 us
    pallas_call x2, Pallas kernels, on_device(): pl.pallas_call(functools.partial(sources_kernel, heads, p * part_heads, b...  2.88 us
    pallas_call x1, Pallas kernels, on_device(): pl.pallas_call(functools.partial(first_kernel, heads), out_shape=[tall] *...  2.26 us
    pallas_call x1, Pallas kernels, on_device(): pl.pallas_call(functools.partial(second_kernel, heads, depth, part_heads)...  1.65 us
    ppermute x2, starting transfers between devices, on_device(): lax.ppermute(grad_level, 'head', [(i, i ^ 1 << bit) for i in range(groups)])  1.58 us
  transfers between devices with their start and end apart: 15, of which 6 were waited for; matrix products, arithmetic and copies ran while one was open for 0% of the time, Pallas kernels for 31%

profile of v6, /device:TPU:16, one launch (start us, length us, event | category | flops | bytes accessed | tf_op | source)
XLA Modules:
  0.0 56.2 jit_solution(15545620812107843483)
XLA Ops:
  0.6 2.3 %shard_map.102 = (f32[256,1024]{1,0:T(8,128)S(1)}, f32[256,1024]{1,0:T(8,128)S(1)}, f32[256,1024]{1,0:T(8,128)S(1)}, f32[256,1024]{1,0:T(8,128)S(1)}, f32[256,12...) custom-call(s32[1]{0:T(128)} %bitcast.device_ref, ...), custom_call_target="tpu_custom_call" | custom-call | tf_op jit(solution)/shard_map/pallas_call | solution.py:396
  2.9 1.6 %collective-permute-start = (f32[8,128]{1,0:T(8,128)S(1)}, f32[8,128]{1,0:T(8,128)S(1)}, u32[]{:S(2)}, u32[]{:S(2)}) collective-permute-start(f32[8,128]{1,0:T(8,128)S(1)} %get-tuple-element.52.own_ref), channel_id=1, source_target_pairs={{0,4},{4,0},{8,12},{12,8},{16,20},{20,16},{24,28},{28,24},{1,5},{5... | collective-permute-start | bytes 12296 | tf_op jit(solution)/shard_map/ppermute | solution.py:368
  4.5 2.6 %shard_map.103 = (f32[256,512]{1,0:T(8,128)S(1)}, f32[256,512]{1,0:T(8,128)S(1)}, f32[256,512]{1,0:T(8,128)S(1)}, f32[8,256]{1,0:T(8,128)S(1)}) custom-call(f32[256,1024]{1,0:T(8,128)S(1)} %get-tuple-element.49.q_ref.refs_0_, f32[256,1024]{1,0:T(8,128)S(1)} %get-tuple-element.53.k_ref, f32[256,1024]{1,0:T(8,128)S(1)} %get-tuple-element.54.v_ref, ...), custom_call_target="tpu_custom_call" | custom-call | flops 1 | bytes 1 | tf_op jit(solution)/shard_map/pallas_call | solution.py:420
  7.1 1.0 %shard_map.108 = (f32[256,1024]{1,0:T(8,128)S(1)}, f32[256,1024]{1,0:T(8,128)S(1)}, f32[528,128]{1,0:T(8,128)S(1)}, f32[528,128]{1,0:T(8,128)S(1)}) custom-call(f32[8,256]{1,0:T(8,128)S(1)} %get-tuple-element.61.source_ref, f32[256,1024]{1,0:T(8,128)S(1)} %get-tuple-element.53.k_ref, f32[256,1024]{1,0:T(8,128)S(1)} %get-tuple-element.54.v_ref, ...), custom_call_target="tpu_custom_call" | custom-call | flops 1 | bytes 1 | tf_op jit(solution)/shard_map/pallas_call | solution.py:455
  8.0 1.1 %collective-permute-start.2 = (f32[528,128]{1,0:T(8,128)S(1)}, f32[528,128]{1,0:T(8,128)S(1)}, u32[]{:S(2)}, u32[]{:S(2)}) collective-permute-start(f32[528,128]{1,0:T(8,128)S(1)} %get-tuple-element.62.refs_0_), channel_id=1, source_target_pairs={{0,4},{4,0},{8,12},{12,8},{16,20},{20,16},{24,28},{28,24},{1,5},{5... | collective-permute-start | bytes 811016 | tf_op jit(solution)/shard_map/ppermute | solution.py:368
  9.1 1.6 %shard_map.105 = (f32[256,1024]{1,0:T(8,128)S(1)}, f32[3,256,128]{2,1,0:T(8,128)S(1)}, f32[528,128]{1,0:T(8,128)S(1)}, f32[528,128]{1,0:T(8,128)S(1)}, f32[528,1...) custom-call(f32[7,256]{1,0:T(8,128)S(1)} %bitcast.6, ...), custom_call_target="tpu_custom_call" | custom-call | flops 1 | bytes 1 | tf_op jit(solution)/shard_map/pallas_call | solution.py:465
  10.8 2.4 %collective-permute-start.1 = (f32[528,128]{1,0:T(8,128)S(1)}, f32[528,128]{1,0:T(8,128)S(1)}, u32[]{:S(2)}, u32[]{:S(2)}) collective-permute-start(f32[528,128]{1,0:T(8,128)S(1)} %get-tuple-element.60), channel_id=1, source_target_pairs={{16,8},{20,12},{24,16},{28,20},{17,9},{21,13},{25,17},{29,21},{18,... | collective-permute-start | bytes 811016 | tf_op jit(solution)/shard_map/ppermute | solution.py:368
  13.1 1.1 %collective-permute-start.5 = (f32[528,128]{1,0:T(8,128)S(1)}, f32[528,128]{1,0:T(8,128)S(1)}, u32[]{:S(2)}, u32[]{:S(2)}) collective-permute-start(f32[528,128]{1,0:T(8,128)S(1)} %get-tuple-element.68.refs_0_), channel_id=1, source_target_pairs={{0,4},{4,0},{8,12},{12,8},{16,20},{20,16},{24,28},{28,24},{1,5},{5... | collective-permute-start | bytes 811016 | tf_op jit(solution)/shard_map/ppermute | solution.py:368
  14.2 1.9 %collective-permute-start.7 = (f32[528,128]{1,0:T(8,128)S(1)}, f32[528,128]{1,0:T(8,128)S(1)}, u32[]{:S(2)}, u32[]{:S(2)}) collective-permute-start(f32[528,128]{1,0:T(8,128)S(1)} %get-tuple-element.74), channel_id=1, source_target_pairs={{16,8},{20,12},{24,16},{28,20},{17,9},{21,13},{25,17},{29,21},{18,... | collective-permute-start | bytes 811016 | tf_op jit(solution)/shard_map/ppermute | solution.py:368
  16.1 2.6 %shard_map.109 = (f32[256,512]{1,0:T(8,128)S(1)}, f32[256,512]{1,0:T(8,128)S(1)}, f32[256,512]{1,0:T(8,128)S(1)}, f32[8,256]{1,0:T(8,128)S(1)}) custom-call(f32[256,1024]{1,0:T(8,128)S(1)} %get-tuple-element.49.q_ref.refs_0_, f32[256,1024]{1,0:T(8,128)S(1)} %get-tuple-element.53.k_ref, f32[256,1024]{1,0:T(8,128)S(1)} %get-tuple-element.54.v_ref, ...), custom_call_target="tpu_custom_call" | custom-call | flops 1 | bytes 1 | tf_op jit(solution)/shard_map/pallas_call | solution.py:420
  18.7 0.1 shard_map.107.factor_ref.refs_3_
  18.8 0.1 shard_map.110.refs_0_
  18.9 3.2 %collective-permute-done.1.refs_1_.refs_2_ = f32[528,128]{1,0:T(8,128)S(1)} collective-permute-done((f32[528,128]{1,0:T(8,128)S(1)}, f32[528,128]{1,0:T(8,128)S(1)}, u32[]{:S(2)}, u32[]{:S(2)}) %collective-permute-start.1) | collective-permute-done | bytes 270368 | tf_op jit(solution)/shard_map/ppermute | solution.py:368
  22.2 2.4 %collective-permute-start.4 = (f32[528,128]{1,0:T(8,128)S(1)}, f32[528,128]{1,0:T(8,128)S(1)}, u32[]{:S(2)}, u32[]{:S(2)}) collective-permute-start(f32[528,128]{1,0:T(8,128)S(1)} %shard_map.113), channel_id=1, source_target_pairs={{8,16},{12,20},{16,8},{20,12},{9,17},{13,21},{17,9},{21,13},{10,18... | collective-permute-start | bytes 811016 | tf_op jit(solution)/shard_map/ppermute | solution.py:368
  24.5 0.1 shard_map.111
  24.7 0.1 collective-permute-start.3
  24.8 0.1 shard_map.119.refs_0_
  24.9 2.9 %collective-permute-done.7.refs_2_.refs_1_ = f32[528,128]{1,0:T(8,128)S(1)} collective-permute-done((f32[528,128]{1,0:T(8,128)S(1)}, f32[528,128]{1,0:T(8,128)S(1)}, u32[]{:S(2)}, u32[]{:S(2)}) %collective-permute-start.7) | collective-permute-done | bytes 270368 | tf_op jit(solution)/shard_map/ppermute | solution.py:368
  27.9 2.4 %collective-permute-start.9 = (f32[528,128]{1,0:T(8,128)S(1)}, f32[528,128]{1,0:T(8,128)S(1)}, u32[]{:S(2)}, u32[]{:S(2)}) collective-permute-start(f32[528,128]{1,0:T(8,128)S(1)} %shard_map.123), channel_id=1, source_target_pairs={{8,16},{12,20},{16,8},{20,12},{9,17},{13,21},{17,9},{21,13},{10,18... | collective-permute-start | bytes 811016 | tf_op jit(solution)/shard_map/ppermute | solution.py:368
  30.3 0.2 shard_map.120
  30.4 0.1 collective-permute-start.8
  30.5 0.7 %shard_map.114 = (f32[256,512]{1,0:T(8,128)S(1)}, f32[8,256]{1,0:T(8,128)S(1)}) custom-call(f32[256,1024]{1,0:T(8,128)S(1)} %get-tuple-element.49.q_ref.refs_0_, f32[256,1024]{1,0:T(8,128)S(1)} %get-tuple-element.58.refs_1_, f32[3,256,128]{2,1,0:T(8,128)S(1)} %get-tuple-element.59.refs_2_, f32[16,128]{1,0:T(8,128)S(1)} %shard_map.107.factor_ref.refs_3_, ...), custom_call_target="tpu_custom_call" | custom-call | flops 1 | bytes 1 | tf_op jit(solution)/shard_map/pallas_call | solution.py:497
  31.2 0.8 %shard_map.115 = (f32[256,512]{1,0:T(8,128)S(1)}, f32[8,256]{1,0:T(8,128)S(1)}) custom-call(f32[256,1024]{1,0:T(8,128)S(1)} %get-tuple-element.49.q_ref.refs_0_, f32[256,1024]{1,0:T(8,128)S(1)} %get-tuple-element.58.refs_1_, f32[3,256,128]{2,1,0:T(8,128)S(1)} %get-tuple-element.59.refs_2_, f32[16,128]{1,0:T(8,128)S(1)} %shard_map.107.factor_ref.refs_3_, ...), custom_call_target="tpu_custom_call" | custom-call | flops 1 | bytes 1 | tf_op jit(solution)/shard_map/pallas_call | solution.py:497
  32.0 2.1 %collective-permute-done.3.refs_2_.refs_1_.refs_6_.refs_3_.refs_0_ = f32[528,128]{1,0:T(8,128)S(1)} collective-permute-done((f32[528,128]{1,0:T(8,128)S(1)}, f32[528,128]{1,0:T(8,128)S(1)}, u32[]{:S(2)}, u32[]{:S(2)}) %collective-permute-start.3) | collective-permute-done | bytes 270368 | tf_op jit(solution)/shard_map/ppermute | solution.py:368
  34.2 0.1 shard_map.116
  34.4 1.9 %collective-permute-start.6 = (f32[528,128]{1,0:T(8,128)S(1)}, f32[528,128]{1,0:T(8,128)S(1)}, u32[]{:S(2)}, u32[]{:S(2)}) collective-permute-start(f32[528,128]{1,0:T(8,128)S(1)} %shard_map.116), channel_id=1, source_target_pairs={{8,16},{12,20},{16,24},{20,28},{9,17},{13,21},{17,25},{21,29},{10,... | collective-permute-start | bytes 811016 | tf_op jit(solution)/shard_map/ppermute | solution.py:368
  36.3 2.1 %collective-permute-done.9.refs_2_ = f32[528,128]{1,0:T(8,128)S(1)} collective-permute-done((f32[528,128]{1,0:T(8,128)S(1)}, f32[528,128]{1,0:T(8,128)S(1)}, u32[]{:S(2)}, u32[]{:S(2)}) %collective-permute-start.9) | collective-permute-done | bytes 270368 | tf_op jit(solution)/shard_map/ppermute | solution.py:368
  38.5 0.1 shard_map.124
  38.6 3.0 %collective-permute-start.10 = (f32[528,128]{1,0:T(8,128)S(1)}, f32[528,128]{1,0:T(8,128)S(1)}, u32[]{:S(2)}, u32[]{:S(2)}) collective-permute-start(f32[528,128]{1,0:T(8,128)S(1)} %shard_map.124), channel_id=1, source_target_pairs={{8,16},{12,20},{16,24},{20,28},{9,17},{13,21},{17,25},{21,29},{10,... | collective-permute-start | bytes 811016 | tf_op jit(solution)/shard_map/ppermute | solution.py:368
  41.6 0.1 shard_map.126.factor_ref
  41.7 0.1 shard_map.129.refs_0_.kept_ref
  41.8 0.1 shard_map.130
  42.0 0.8 %collective-permute-start.12 = (f32[528,128]{1,0:T(8,128)S(1)}, f32[528,128]{1,0:T(8,128)S(1)}, u32[]{:S(2)}, u32[]{:S(2)}) collective-permute-start(f32[528,128]{1,0:T(8,128)S(1)} %shard_map.130), channel_id=1, source_target_pairs={{0,4},{4,0},{8,12},{12,8},{16,20},{20,16},{24,28},{28,24},{1,5},{5... | collective-permute-start | bytes 811016 | tf_op jit(solution)/shard_map/ppermute | solution.py:368
  42.8 0.2 shard_map.127.refs_0_.kept_ref
  43.0 0.1 shard_map.128
  43.1 1.3 %collective-permute-start.11 = (f32[528,128]{1,0:T(8,128)S(1)}, f32[528,128]{1,0:T(8,128)S(1)}, u32[]{:S(2)}, u32[]{:S(2)}) collective-permute-start(f32[528,128]{1,0:T(8,128)S(1)} %shard_map.128), channel_id=1, source_target_pairs={{0,4},{4,0},{8,12},{12,8},{16,20},{20,16},{24,28},{28,24},{1,5},{5... | collective-permute-start | bytes 811016 | tf_op jit(solution)/shard_map/ppermute | solution.py:368
  44.4 0.7 %shard_map.118 = (f32[256,512]{1,0:T(8,128)S(1)}, f32[8,256]{1,0:T(8,128)S(1)}) custom-call(f32[256,1024]{1,0:T(8,128)S(1)} %get-tuple-element.49.q_ref.refs_0_, f32[256,1024]{1,0:T(8,128)S(1)} %get-tuple-element.58.refs_1_, f32[3,256,128]{2,1,0:T(8,128)S(1)} %get-tuple-element.59.refs_2_, f32[16,128]{1,0:T(8,128)S(1)} %shard_map.112.factor_ref.refs_3_, ...), custom_call_target="tpu_custom_call" | custom-call | flops 1 | bytes 1 | tf_op jit(solution)/shard_map/pallas_call | solution.py:497
  45.2 0.8 %shard_map.121 = (f32[256,512]{1,0:T(8,128)S(1)}, f32[8,256]{1,0:T(8,128)S(1)}) custom-call(f32[256,1024]{1,0:T(8,128)S(1)} %get-tuple-element.49.q_ref.refs_0_, f32[256,1024]{1,0:T(8,128)S(1)} %get-tuple-element.58.refs_1_, f32[3,256,128]{2,1,0:T(8,128)S(1)} %get-tuple-element.59.refs_2_, f32[16,128]{1,0:T(8,128)S(1)} %shard_map.112.factor_ref.refs_3_, ...), custom_call_target="tpu_custom_call" | custom-call | flops 1 | bytes 1 | tf_op jit(solution)/shard_map/pallas_call | solution.py:497
  46.0 0.2 shard_map.117.refs_3_
  46.2 1.4 %shard_map.122 = (f32[256,1024]{1,0:T(8,128)}, f32[8,256]{1,0:T(8,128)S(1)}) custom-call(f32[256,1024]{1,0:T(8,128)S(1)} %get-tuple-element.49.q_ref.refs_0_, f32[256,1024]{1,0:T(8,128)S(1)} %get-tuple-element.58.refs_1_, f32[3,256,128]{2,1,0:T(8,128)S(1)} %get-tuple-element.59.refs_2_, f32[16,128]{1,0:T(8,128)S(1)} %shard_map.117.refs_3_, ...), custom_call_target="tpu_custom_call" | custom-call | flops 1 | bytes 1 | tf_op jit(solution)/shard_map/pallas_call | solution.py:497
  47.6 1.0 %collective-permute-done.10.refs_6_ = f32[528,128]{1,0:T(8,128)S(1)} collective-permute-done((f32[528,128]{1,0:T(8,128)S(1)}, f32[528,128]{1,0:T(8,128)S(1)}, u32[]{:S(2)}, u32[]{:S(2)}) %collective-permute-start.10) | collective-permute-done | bytes 270368 | tf_op jit(solution)/shard_map/ppermute | solution.py:368
  48.5 1.4 %shard_map.125 = (f32[256,1024]{1,0:T(8,128)}, f32[8,256]{1,0:T(8,128)S(1)}) custom-call(f32[256,1024]{1,0:T(8,128)S(1)} %get-tuple-element.49.q_ref.refs_0_, f32[256,1024]{1,0:T(8,128)S(1)} %get-tuple-element.58.refs_1_, f32[3,256,128]{2,1,0:T(8,128)S(1)} %get-tuple-element.59.refs_2_, ...), custom_call_target="tpu_custom_call", output_to_operand_aliasing={{0}: (7, {})} | custom-call | flops 1 | bytes 1 | tf_op jit(solution)/shard_map/pallas_call | solution.py:497
  50.0 0.1 collective-permute-start.13
  50.0 1.2 %collective-permute-done.13.refs_1_ = f32[8,256]{1,0:T(8,128)S(1)} collective-permute-done((f32[8,256]{1,0:T(8,128)S(1)}, f32[8,256]{1,0:T(8,128)S(1)}, u32[]{:S(2)}, u32[]{:S(2)}) %collective-permute-start.13) | collective-permute-done | bytes 8224 | tf_op jit(solution)/shard_map/ppermute | solution.py:633
  51.2 1.5 %collective-permute-start.14 = (f32[8,256]{1,0:T(8,128)S(1)}, f32[8,256]{1,0:T(8,128)S(1)}, u32[]{:S(2)}, u32[]{:S(2)}) collective-permute-start(f32[8,256]{1,0:T(8,128)S(1)} %shard_map.133.refs_0_), channel_id=1, source_target_pairs={{0,2},{1,3},{2,0},{3,1},{4,6},{5,7},{6,4},{7,5},{8,10},{9,11},{10,... | collective-permute-start | bytes 24584 | tf_op jit(solution)/shard_map/ppermute | solution.py:633
  52.7 1.4 %shard_map.131 = (f32[256,1024]{1,0:T(8,128)}, f32[256,1024]{1,0:T(8,128)}) custom-call(s32[1]{0:T(128)} %bitcast.device_ref, f32[256,1024]{1,0:T(8,128)S(1)} %get-tuple-element.81.wk_ref, f32[256,1024]{1,0:T(8,128)S(1)} %get-tuple-element.82.wv_ref, f32[16,128]{1,0:T(8,128)S(1)} %shard_map.107.factor_ref.refs_3_, ...), custom_call_target="tpu_custom_call" | custom-call | flops 1 | bytes 1 | tf_op jit(solution)/shard_map/pallas_call | solution.py:614
  54.1 1.5 %shard_map.132 = (f32[256,1024]{1,0:T(8,128)}, f32[256,1024]{1,0:T(8,128)}) custom-call(s32[1]{0:T(128)} %bitcast.device_ref, f32[256,1024]{1,0:T(8,128)S(1)} %get-tuple-element.81.wk_ref, f32[256,1024]{1,0:T(8,128)S(1)} %get-tuple-element.82.wv_ref, f32[16,128]{1,0:T(8,128)S(1)} %shard_map.107.factor_ref.refs_3_, ...), custom_call_target="tpu_custom_call", output_to_operand_aliasing={{0}: (8, {}), {1}: (9, {})} | custom-call | flops 1 | bytes 1 | tf_op jit(solution)/shard_map/pallas_call | solution.py:614
  55.6 0.6 %shard_map.134 = f32[7,256]{1,0:T(8,128)} custom-call(f32[8,256]{1,0:T(8,128)S(1)} %shard_map.133.refs_0_, f32[8,256]{1,0:T(8,128)S(1)} %collective-permute-done.14.refs_1_), custom_call_target="tpu_custom_call" | custom-call | tf_op jit(solution)/shard_map/pallas_call | solution.py:634
  (17 shorter events, 0.2 us)
Async XLA Ops:
  2.9 1.6 %copy-start = (f32[256,7]{0,1:T(8,128)S(1)}, f32[256,7]{0,1:T(8,128)}, u32[]{:S(2)}) copy-start(f32[256,7]{0,1:T(8,128)} %param.12) | copy-start | bytes 21508
  2.9 4.1 %collective-permute-start = (f32[8,128]{1,0:T(8,128)S(1)}, f32[8,128]{1,0:T(8,128)S(1)}, u32[]{:S(2)}, u32[]{:S(2)}) collective-permute-start(f32[8,128]{1,0:T(8,128)S(1)} %get-tuple-element.52.own_ref), channel_id=1, source_target_pairs={{0,4},{4,0},{8,12},{12,8},{16,20},{20,16},{24,28},{28,24},{1,5},{5... | collective-permute-start | bytes 12296 | tf_op jit(solution)/shard_map/ppermute | solution.py:368
  8.0 10.7 %collective-permute-start.2 = (f32[528,128]{1,0:T(8,128)S(1)}, f32[528,128]{1,0:T(8,128)S(1)}, u32[]{:S(2)}, u32[]{:S(2)}) collective-permute-start(f32[528,128]{1,0:T(8,128)S(1)} %get-tuple-element.62.refs_0_), channel_id=1, source_target_pairs={{0,4},{4,0},{8,12},{12,8},{16,20},{20,16},{24,28},{28,24},{1,5},{5... | collective-permute-start | bytes 811016 | tf_op jit(solution)/shard_map/ppermute | solution.py:368
  10.8 11.3 %collective-permute-start.1 = (f32[528,128]{1,0:T(8,128)S(1)}, f32[528,128]{1,0:T(8,128)S(1)}, u32[]{:S(2)}, u32[]{:S(2)}) collective-permute-start(f32[528,128]{1,0:T(8,128)S(1)} %get-tuple-element.60), channel_id=1, source_target_pairs={{16,8},{20,12},{24,16},{28,20},{17,9},{21,13},{25,17},{29,21},{18,... | collective-permute-start | bytes 811016 | tf_op jit(solution)/shard_map/ppermute | solution.py:368
  13.1 11.6 %collective-permute-start.5 = (f32[528,128]{1,0:T(8,128)S(1)}, f32[528,128]{1,0:T(8,128)S(1)}, u32[]{:S(2)}, u32[]{:S(2)}) collective-permute-start(f32[528,128]{1,0:T(8,128)S(1)} %get-tuple-element.68.refs_0_), channel_id=1, source_target_pairs={{0,4},{4,0},{8,12},{12,8},{16,20},{20,16},{24,28},{28,24},{1,5},{5... | collective-permute-start | bytes 811016 | tf_op jit(solution)/shard_map/ppermute | solution.py:368
  14.2 13.7 %collective-permute-start.7 = (f32[528,128]{1,0:T(8,128)S(1)}, f32[528,128]{1,0:T(8,128)S(1)}, u32[]{:S(2)}, u32[]{:S(2)}) collective-permute-start(f32[528,128]{1,0:T(8,128)S(1)} %get-tuple-element.74), channel_id=1, source_target_pairs={{16,8},{20,12},{24,16},{28,20},{17,9},{21,13},{25,17},{29,21},{18,... | collective-permute-start | bytes 811016 | tf_op jit(solution)/shard_map/ppermute | solution.py:368
  22.2 12.1 %collective-permute-start.4 = (f32[528,128]{1,0:T(8,128)S(1)}, f32[528,128]{1,0:T(8,128)S(1)}, u32[]{:S(2)}, u32[]{:S(2)}) collective-permute-start(f32[528,128]{1,0:T(8,128)S(1)} %shard_map.113), channel_id=1, source_target_pairs={{8,16},{12,20},{16,8},{20,12},{9,17},{13,21},{17,9},{21,13},{10,18... | collective-permute-start | bytes 811016 | tf_op jit(solution)/shard_map/ppermute | solution.py:368
  24.7 9.5 %collective-permute-start.3 = (f32[528,128]{1,0:T(8,128)S(1)}, f32[528,128]{1,0:T(8,128)S(1)}, u32[]{:S(2)}, u32[]{:S(2)}) collective-permute-start(f32[528,128]{1,0:T(8,128)S(1)} %shard_map.111), channel_id=1, source_target_pairs={{0,8},{4,12},{8,0},{12,4},{16,24},{20,28},{24,16},{28,20},{1,9},{5... | collective-permute-start | bytes 811016 | tf_op jit(solution)/shard_map/ppermute | solution.py:368
  27.9 10.6 %collective-permute-start.9 = (f32[528,128]{1,0:T(8,128)S(1)}, f32[528,128]{1,0:T(8,128)S(1)}, u32[]{:S(2)}, u32[]{:S(2)}) collective-permute-start(f32[528,128]{1,0:T(8,128)S(1)} %shard_map.123), channel_id=1, source_target_pairs={{8,16},{12,20},{16,8},{20,12},{9,17},{13,21},{17,9},{21,13},{10,18... | collective-permute-start | bytes 811016 | tf_op jit(solution)/shard_map/ppermute | solution.py:368
  30.4 8.0 %collective-permute-start.8 = (f32[528,128]{1,0:T(8,128)S(1)}, f32[528,128]{1,0:T(8,128)S(1)}, u32[]{:S(2)}, u32[]{:S(2)}) collective-permute-start(f32[528,128]{1,0:T(8,128)S(1)} %shard_map.120), channel_id=1, source_target_pairs={{0,8},{4,12},{8,0},{12,4},{16,24},{20,28},{24,16},{28,20},{1,9},{5... | collective-permute-start | bytes 811016 | tf_op jit(solution)/shard_map/ppermute | solution.py:368
  34.4 11.6 %collective-permute-start.6 = (f32[528,128]{1,0:T(8,128)S(1)}, f32[528,128]{1,0:T(8,128)S(1)}, u32[]{:S(2)}, u32[]{:S(2)}) collective-permute-start(f32[528,128]{1,0:T(8,128)S(1)} %shard_map.116), channel_id=1, source_target_pairs={{8,16},{12,20},{16,24},{20,28},{9,17},{13,21},{17,25},{21,29},{10,... | collective-permute-start | bytes 811016 | tf_op jit(solution)/shard_map/ppermute | solution.py:368
  38.6 9.9 %collective-permute-start.10 = (f32[528,128]{1,0:T(8,128)S(1)}, f32[528,128]{1,0:T(8,128)S(1)}, u32[]{:S(2)}, u32[]{:S(2)}) collective-permute-start(f32[528,128]{1,0:T(8,128)S(1)} %shard_map.124), channel_id=1, source_target_pairs={{8,16},{12,20},{16,24},{20,28},{9,17},{13,21},{17,25},{21,29},{10,... | collective-permute-start | bytes 811016 | tf_op jit(solution)/shard_map/ppermute | solution.py:368
  42.0 10.7 %collective-permute-start.12 = (f32[528,128]{1,0:T(8,128)S(1)}, f32[528,128]{1,0:T(8,128)S(1)}, u32[]{:S(2)}, u32[]{:S(2)}) collective-permute-start(f32[528,128]{1,0:T(8,128)S(1)} %shard_map.130), channel_id=1, source_target_pairs={{0,4},{4,0},{8,12},{12,8},{16,20},{20,16},{24,28},{28,24},{1,5},{5... | collective-permute-start | bytes 811016 | tf_op jit(solution)/shard_map/ppermute | solution.py:368
  43.1 11.0 %collective-permute-start.11 = (f32[528,128]{1,0:T(8,128)S(1)}, f32[528,128]{1,0:T(8,128)S(1)}, u32[]{:S(2)}, u32[]{:S(2)}) collective-permute-start(f32[528,128]{1,0:T(8,128)S(1)} %shard_map.128), channel_id=1, source_target_pairs={{0,4},{4,0},{8,12},{12,8},{16,20},{20,16},{24,28},{28,24},{1,5},{5... | collective-permute-start | bytes 811016 | tf_op jit(solution)/shard_map/ppermute | solution.py:368
  50.0 1.2 %collective-permute-start.13 = (f32[8,256]{1,0:T(8,128)S(1)}, f32[8,256]{1,0:T(8,128)S(1)}, u32[]{:S(2)}, u32[]{:S(2)}) collective-permute-start(f32[8,256]{1,0:T(8,128)S(1)} %get-tuple-element.93.refs_0_), channel_id=1, source_target_pairs={{0,1},{1,0},{2,3},{3,2},{4,5},{5,4},{6,7},{7,6},{8,9},{9,8},{10,11... | collective-permute-start | bytes 24584 | tf_op jit(solution)/shard_map/ppermute | solution.py:633
  51.2 4.4 %collective-permute-start.14 = (f32[8,256]{1,0:T(8,128)S(1)}, f32[8,256]{1,0:T(8,128)S(1)}, u32[]{:S(2)}, u32[]{:S(2)}) collective-permute-start(f32[8,256]{1,0:T(8,128)S(1)} %shard_map.133.refs_0_), channel_id=1, source_target_pairs={{0,2},{1,3},{2,0},{3,1},{4,6},{5,7},{6,4},{7,5},{8,10},{9,11},{10,... | collective-permute-start | bytes 24584 | tf_op jit(solution)/shard_map/ppermute | solution.py:633
